TPU v7x, 32 devices: a whole 2x2x4 slice. The times are simulated.
32 devices in a mesh: sect: 2 (over x), dp: 4 (over z), tp: 4 (over y, core).
Axes of the slice: x: 2, y: 2, z: 4, core: 2. Of those that a mesh axis runs over, the one named last changes fastest.
Arguments:
- w_key: bfloat16 [8192, 1024], P(('sect', 'dp', 'tp')), may hold values from -0.0625 to 0.0625
- w_value: bfloat16 [8192, 1024], P(('sect', 'dp', 'tp')), may hold values from -0.0625 to 0.0625
- hidden: bfloat16 [32, 16, 8192], P(('sect', 'dp'), None, 'tp'), may hold values from -6 to 6
- queries: bfloat16 [32, 16, 8192], P(('sect', 'dp'), None, 'tp'), may hold values from -36 to 36
- key_cache: bfloat16 [32, 512, 1024], P(('sect', 'dp'), None, 'tp'), may hold values from -6 to 6
- value_cache: bfloat16 [32, 512, 1024], P(('sect', 'dp'), None, 'tp'), may hold values from -6 to 6
- prompt_lengths: int32 [32], P(('sect', 'dp')), may hold values from 64 to 512
- rollout_lengths: int32 [32], P(('sect', 'dp')), may hold values from 1 to 16
- batch_slots: int32 [32], replicated, may hold values from 0 to 31, as said below
Outputs:
- batched: bfloat16 [32, 16, 8192], P(('sect', 'dp'), None, 'tp')
Inputs may be any that keep to these rules, and one draw needn't show every extreme that they name: `batch_slots`: every row number appears once; a holder owns 4 consecutive rows of the micro-batch order, and the 4 sequences of one index of sect and dp go to 4 different holders.
All inputs are finite; a program needn't handle non-finite values.
Results may differ from a plain program's by a relative error of at most 0.0059.
Values may be sent and summed in bfloat16 or wider, within the bound.
No kernel may reach another device: no remote copies, remote signals or barrier semaphores. Data moves between devices by JAX's collectives and lax.ppermute only.
A program may use at most 64 MiB of HBM per device.

v0:
```python
import jax
import jax.numpy as jnp
from jax import lax
from jax.sharding import PartitionSpec as P

D = 8192
HEAD = 128
STEPS = 16
CTX = 512
GROUP = 8


def attend(queries, new_keys, new_values, key_cache, value_cache, prompt_lengths, rollout_lengths):
    count = queries.shape[0]
    heads_kv = key_cache.shape[2] // HEAD
    scale = HEAD ** (-0.5)
    query = queries.reshape(count, STEPS, heads_kv, GROUP, HEAD)
    cache_k = key_cache.reshape(count, CTX, heads_kv, HEAD)
    cache_v = value_cache.reshape(count, CTX, heads_kv, HEAD)
    fresh_k = new_keys.reshape(count, STEPS, heads_kv, HEAD)
    fresh_v = new_values.reshape(count, STEPS, heads_kv, HEAD)
    live = (jnp.arange(CTX)[None, :] < prompt_lengths[:, None])[:, None, None, None, :]
    causal = (jnp.arange(STEPS)[None, :] <= jnp.arange(STEPS)[:, None])[None, :, None, None, :]
    score_c = (
        jnp.einsum("nikgd,njkd->nikgj", query, cache_k, preferred_element_type=jnp.float32) * scale
    )
    score_n = (
        jnp.einsum("nikgd,njkd->nikgj", query, fresh_k, preferred_element_type=jnp.float32) * scale
    )
    score_c = jnp.where(live, score_c, -1e30)
    score_n = jnp.where(causal, score_n, -1e30)
    top = jnp.maximum(jnp.max(score_c, axis=-1), jnp.max(score_n, axis=-1))
    exp_c = jnp.exp(score_c - top[..., None])
    exp_n = jnp.exp(score_n - top[..., None])
    total = jnp.sum(exp_c, axis=-1) + jnp.sum(exp_n, axis=-1)
    weight_c = (exp_c / total[..., None]).astype(jnp.bfloat16)
    weight_n = (exp_n / total[..., None]).astype(jnp.bfloat16)
    result = jnp.einsum("nikgj,njkd->nikgd", weight_c, cache_v, preferred_element_type=jnp.float32)
    result = result + jnp.einsum(
        "nikgj,njkd->nikgd", weight_n, fresh_v, preferred_element_type=jnp.float32
    )
    keep = (jnp.arange(STEPS)[None, :] < rollout_lengths[:, None])[:, :, None, None, None]
    result = jnp.where(keep, result, 0.0)
    return result.astype(jnp.bfloat16).reshape(count, STEPS, heads_kv * GROUP * HEAD)


def shards(
    w_key,
    w_value,
    hidden,
    queries,
    key_cache,
    value_cache,
    prompt_lengths,
    rollout_lengths,
    batch_slots,
):
    count = hidden.shape[0]
    whole = lax.all_gather(hidden, "tp", axis=2, tiled=True)
    flat = whole.reshape(count * STEPS, D)
    rows_key, rows_value = (
        lax.all_gather(w_key, ("sect", "dp"), axis=0, tiled=True),
        lax.all_gather(w_value, ("sect", "dp"), axis=0, tiled=True),
    )
    cols_key, cols_value = (
        lax.all_to_all(rows_key, "tp", split_axis=1, concat_axis=0, tiled=True),
        lax.all_to_all(rows_value, "tp", split_axis=1, concat_axis=0, tiled=True),
    )
    heads_tp = lax.axis_size("tp")
    groups = lax.axis_size(("sect", "dp"))
    block = w_key.shape[0]
    width = cols_key.shape[1]

    def reorder(a):
        return a.reshape(heads_tp, groups, block, width).transpose(1, 0, 2, 3).reshape(D, width)

    key_sum = jnp.dot(flat, reorder(cols_key), preferred_element_type=jnp.float32)
    value_sum = jnp.dot(flat, reorder(cols_value), preferred_element_type=jnp.float32)
    new_keys = key_sum.astype(jnp.bfloat16).reshape(count, STEPS, -1)
    new_values = value_sum.astype(jnp.bfloat16).reshape(count, STEPS, -1)
    attended = attend(
        queries, new_keys, new_values, key_cache, value_cache, prompt_lengths, rollout_lengths
    )
    owner = lax.axis_index(("sect", "dp"))
    targets = owner * count + jnp.arange(count, dtype=jnp.int32)
    select = (batch_slots[None, :] == targets[:, None]).astype(jnp.bfloat16)
    gathered = jnp.einsum(
        "rs,sid->rid",
        select,
        lax.all_gather(attended, ("sect", "dp"), axis=0, tiled=True),
        preferred_element_type=jnp.float32,
    )
    return gathered.astype(jnp.bfloat16)


def solution(mesh):
    in_specs = (
        P(("sect", "dp", "tp"), None),
        P(("sect", "dp", "tp"), None),
        P(("sect", "dp"), None, "tp"),
        P(("sect", "dp"), None, "tp"),
        P(("sect", "dp"), None, "tp"),
        P(("sect", "dp"), None, "tp"),
        P(("sect", "dp")),
        P(("sect", "dp")),
        P(),
    )
    out_specs = P(("sect", "dp"), None, "tp")
    return jax.shard_map(shards, mesh=mesh, in_specs=in_specs, out_specs=out_specs, check_vma=False)
```

profile of v0, /device:TPU:0, one launch (start us, length us, event | category | flops | bytes accessed | tf_op | source)
XLA Modules:
  0.0 291.0 jit_solution(15368048363304497216)
XLA Ops:
  6.5 2.1 copy.64
  8.7 2.1 copy.71
  10.8 76.3 %all-gather.7.cloned.1.call-done = bf16[2048,1024]{0,1:T(8,128)(2,1)} async-done(((bf16[256,1024]{0,1:T(8,128)(2,1)}), bf16[2048,1024]{0,1:T(8,128)(2,1)}) %all-gather.7.cloned.1.call-update) | async-done | bytes 4194320 | tf_op jit(solution)/shard_map/all_gather | solution.py:62
  87.1 4.9 %all-to-all-start = ((bf16[2048,4,256]{0,2,1:T(8,128)(2,1)}), bf16[2048,4,256]{0,2,1:T(8,128)(2,1)}, u32[]{:S(2)}, u32[]{:S(2)}) async-start(bf16[2048,4,256]{0,2,1:T(8,128)(2,1)} %bitcast.61), calls=%async_computation | async-start | bytes 8388608 | tf_op jit(solution)/shard_map/all_to_all | solution.py:66
  92.1 0.7 all-gather.5.cloned.1.call-update
  92.8 69.6 %all-gather.9.cloned.1.call-done = bf16[2048,1024]{0,1:T(8,128)(2,1)} async-done(((bf16[256,1024]{0,1:T(8,128)(2,1)}), bf16[2048,1024]{0,1:T(8,128)(2,1)}) %all-gather.9.cloned.1.call-update) | async-done | bytes 4194320 | tf_op jit(solution)/shard_map/all_gather | solution.py:63
  162.4 5.0 %all-to-all-start.1 = ((bf16[2048,4,256]{0,2,1:T(8,128)(2,1)}), bf16[2048,4,256]{0,2,1:T(8,128)(2,1)}, u32[]{:S(2)}, u32[]{:S(2)}) async-start(bf16[2048,4,256]{0,2,1:T(8,128)(2,1)} %bitcast.60), calls=%async_computation.1 | async-start | bytes 8388608 | tf_op jit(solution)/shard_map/all_to_all | solution.py:67
  167.5 1.2 reshape.100
  169.2 1.9 bitcast_reduce_fusion
  171.0 6.3 %copy.65 = bf16[4,2048,256]{2,1,0:T(8,128)(2,1)} copy(bf16[4,2048,256]{1,2,0:T(8,128)(2,1)} %bitcast.5) | data formatting | bytes 8388608 | tf_op jit(solution)/shard_map/all_to_all | solution.py:66
  177.3 4.6 %copy.66 = bf16[8,4,256,256]{3,2,1,0:T(8,128)(2,1)} copy(bf16[8,4,256,256]{3,2,0,1:T(8,128)(2,1)} %bitcast.56) | data formatting | bytes 8388608 | tf_op jit(solution)/shard_map/transpose | solution.py:75
  181.9 2.5 all-gather.5.cloned.1.call-done
  184.4 3.3 %convolution_convert_fusion.2 = bf16[64,256]{1,0:T(8,128)(2,1)S(1)} fusion(bf16[64,8192]{1,0:T(8,128)(2,1)} %bitcast.58, bf16[8192,256]{1,0:T(8,128)(2,1)} %bitcast.54), kind=kOutput, calls=%fused_computation.17 | convolution fusion | flops 268451840 | bytes 5275648 | tf_op jit(solution)/shard_map/dot_general | solution.py:77
  187.7 0.7 fusion.21
  189.5 1.6 divide_convert_fusion
  191.1 30.1 %all-to-all-done.1 = bf16[2048,4,256]{0,2,1:T(8,128)(2,1)} async-done(((bf16[2048,4,256]{0,2,1:T(8,128)(2,1)}), bf16[2048,4,256]{0,2,1:T(8,128)(2,1)}, u32[]{:S(2)}, u32[]{:S(2)}) %all-to-all-start.1) | async-done | bytes 4194336 | tf_op jit(solution)/shard_map/all_to_all | solution.py:67
  221.2 6.2 %copy.72 = bf16[4,2048,256]{2,1,0:T(8,128)(2,1)} copy(bf16[4,2048,256]{1,2,0:T(8,128)(2,1)} %bitcast.14) | data formatting | bytes 8388608 | tf_op jit(solution)/shard_map/all_to_all | solution.py:67
  227.4 2.5 copy.73
  230.0 0.8 convolution_convert_fusion.1
  231.3 0.8 fusion.7
  232.1 0.8 reshape.108
  233.0 46.7 %all-gather.11.cloned.1.call-done = bf16[32,16,2048]{2,1,0:T(8,128)(2,1)} async-done(((bf16[4,16,2048]{2,1,0:T(8,128)(2,1)}), bf16[32,16,2048]{2,1,0:T(8,128)(2,1)}) %all-gather.11.cloned.1.call-update) | async-done | bytes 2097168 | tf_op jit(solution)/shard_map/all_gather | solution.py:90
  279.7 3.9 %convolution_convert_fusion = bf16[4,16,2048]{2,0,1:T(4,128)(2,1)S(1)} fusion(bf16[32,16,2048]{2,1,0:T(8,128)(2,1)} %all-gather.11.cloned.1.call-done, s32[32]{0:T(128)S(1)} %copy-done.6, s32[4]{0:T(128)S(1)} %iota_add_fusion), kind=kOutput, calls=%fused_computation | convolution fusion | flops 8519808 | bytes 2359440 | tf_op jit(solution)/shard_map/rs,sid->rid/dot_general | solution.py:87
  283.6 0.9 copy.78
  (40 shorter events, 2.1 us)
Async XLA Ops:
  6.5 80.6 %all-gather.7.cloned.1.call-start = ((), (), s32[]{:S(2)}) async-start(), calls=%async_computation.3 | async-start | bytes 4718592 | tf_op jit(solution)/shard_map/all_gather | solution.py:62
  8.6 153.7 %all-gather.9.cloned.1.call-start = ((), (), s32[]{:S(2)}) async-start(), calls=%async_computation.4 | async-start | bytes 4718592 | tf_op jit(solution)/shard_map/all_gather | solution.py:63
  87.1 75.2 %all-to-all-start = ((bf16[2048,4,256]{0,2,1:T(8,128)(2,1)}), bf16[2048,4,256]{0,2,1:T(8,128)(2,1)}, u32[]{:S(2)}, u32[]{:S(2)}) async-start(bf16[2048,4,256]{0,2,1:T(8,128)(2,1)} %bitcast.61), calls=%async_computation | async-start | bytes 8388608 | tf_op jit(solution)/shard_map/all_to_all | solution.py:66
  92.1 92.3 %all-gather.5.cloned.1.call-start = ((), (), s32[]{:S(2)}) async-start(), calls=%async_computation.2 | async-start | bytes 1310720 | tf_op jit(solution)/shard_map/all_gather | solution.py:59
  162.4 5.0 %copy-start.4 = (bf16[4,16,2048]{2,1,0:T(8,128)(2,1)S(1)}, bf16[4,16,2048]{2,1,0:T(8,128)(2,1)}, u32[]{:S(2)}) copy-start(bf16[4,16,2048]{2,1,0:T(8,128)(2,1)} %param.12) | copy-start | bytes 786436
  162.4 5.1 %copy-start.1 = (bf16[4,512,256]{2,1,0:T(8,128)(2,1)S(1)}, bf16[4,512,256]{2,1,0:T(8,128)(2,1)}, u32[]{:S(2)}) copy-start(bf16[4,512,256]{2,1,0:T(8,128)(2,1)} %param.13) | copy-start | bytes 3145732
  162.4 58.8 %all-to-all-start.1 = ((bf16[2048,4,256]{0,2,1:T(8,128)(2,1)}), bf16[2048,4,256]{0,2,1:T(8,128)(2,1)}, u32[]{:S(2)}, u32[]{:S(2)}) async-start(bf16[2048,4,256]{0,2,1:T(8,128)(2,1)} %bitcast.60), calls=%async_computation.1 | async-start | bytes 8388608 | tf_op jit(solution)/shard_map/all_to_all | solution.py:67
  167.4 1.3 copy-start.2
  167.4 112.3 %all-gather.11.cloned.1.call-start = ((), (), s32[]{:S(2)}) async-start(), calls=%async_computation.5 | async-start | bytes 2359296 | tf_op jit(solution)/shard_map/all_gather | solution.py:90
  167.5 1.5 copy-start.7
  167.5 1.6 copy-start.5
  227.4 2.6 copy-start
  230.0 1.3 copy-start.3
  231.3 48.4 %copy-start.6 = (s32[32]{0:T(128)S(1)}, s32[32]{0:T(128)}, u32[]{:S(2)}) copy-start(s32[32]{0:T(128)} %param.17) | copy-start | bytes 388
Sparse Core Ops, SparseCore 0:
  9.3 77.7 all-gather.6
  89.1 73.2 all-gather.8
  163.9 20.4 all-gather.4
  233.1 46.5 all-gather.10
where the time goes:
time: 292 us; the launch traced here: 291 us
  waiting for transfers between devices  226 us (77%)
  local copies, waits for them, and re-layouts  27.3 us (9%)
  between operations  13.4 us (5%)
  matrix products  11.6 us (4%)
  starting transfers between devices  10 us (3%)
    all_gather x1, waiting for transfers between devices, shards(): lax.all_gather(w_key, ('sect', 'dp'), axis=0, tiled=True)  76.3 us
    all_gather x1, waiting for transfers between devices, shards(): lax.all_gather(w_value, ('sect', 'dp'), axis=0, tiled=True)  69.6 us
    all_gather x1, waiting for transfers between devices, shards(): lax.all_gather(attended, ('sect', 'dp'), axis=0, tiled=True)  46.7 us
    all_to_all x1, waiting for transfers between devices, shards(): lax.all_to_all(rows_value, 'tp', split_axis=1, concat_axis=0, tiled=True)  30.1 us
    transpose x2, local copies, waits for them, and re-layouts, reorder(): a.reshape(heads_tp, groups, block, width).transpose(1, 0, 2, 3)  7.15 us
    all_to_all x1, local copies, waits for them, and re-layouts, shards(): lax.all_to_all(rows_key, 'tp', split_axis=1, concat_axis=0, tiled=True)  6.27 us
    all_to_all x1, local copies, waits for them, and re-layouts, shards(): lax.all_to_all(rows_value, 'tp', split_axis=1, concat_axis=0, tiled=True)  6.22 us
  transfers between devices with their start and end apart: 6, of which 5 were waited for; matrix products, arithmetic and copies ran while one was open for 8% of the time, Pallas kernels for 0%

commit v1 on v0

v1 whole, which is shorter than its diff:
```python
import functools
import jax
import jax.numpy as jnp
from jax import lax
from jax.experimental import pallas as pl
from jax.experimental.pallas import tpu as pltpu
from jax.sharding import PartitionSpec as P

HEAD = 128
GROUP = 8
SCALE = HEAD ** (-0.5)
MIB = 1 << 20
CORE, HALF, SECT, DEPTH, PROMPT = range(5)


def vmem():
    return pl.BlockSpec(memory_space=pltpu.VMEM)


def smem():
    return pl.BlockSpec(memory_space=pltpu.SMEM)


def limit(*arrays):
    total = sum(a.size * a.dtype.itemsize for a in arrays)
    return pltpu.CompilerParams(vmem_limit_bytes=max(6 * MIB, total + 2 * MIB))


def stacked_heads(q, kv):
    first = kv * GROUP
    return jnp.concatenate(
        [q[:, (first + g) * HEAD : (first + g + 1) * HEAD] for g in range(GROUP)], axis=0
    )


def dot32(a, b):
    return jnp.dot(a, b, preferred_element_type=jnp.float32)


def dot_t(a, b):
    return lax.dot_general(a, b, (((1,), (1,)), ((), ())), preferred_element_type=jnp.float32)


def bf16(a):
    return a.astype(jnp.bfloat16)


def cache_kernel(meta_ref, q_ref, k_ref, v_ref, o_ref, stat_ref):
    slots, width = k_ref.shape[1:]
    steps = q_ref.shape[1]
    rows = steps * GROUP
    live = lax.broadcasted_iota(jnp.int32, (rows, slots), 1) < meta_ref[PROMPT + pl.program_id(0)]
    lane = lax.broadcasted_iota(jnp.int32, (rows, HEAD), 1)
    for kv in range(width // HEAD):
        cols = slice(kv * HEAD, (kv + 1) * HEAD)
        q = stacked_heads(q_ref[0], kv)
        s = jnp.where(live, dot_t(q, k_ref[0, :, cols]) * SCALE, -1e30)
        top = jnp.max(s, axis=1, keepdims=True)
        e = jnp.exp(s - top)
        total = jnp.sum(e, axis=1, keepdims=True)
        o_ref[0, kv] = dot32(bf16(e), v_ref[0, :, cols])
        stat_ref[0, kv] = jnp.where(lane == 0, top, total)


def cache_attention(meta, queries, key_cache, value_cache):
    count, steps, qw = queries.shape
    slots, width = key_cache.shape[1:]
    shape = (count, width // HEAD, steps * GROUP, HEAD)

    def one(n, meta):
        return (n, 0, 0)

    def one4(n, meta):
        return (n, 0, 0, 0)

    return pl.pallas_call(
        cache_kernel,
        grid_spec=pltpu.PrefetchScalarGridSpec(
            num_scalar_prefetch=1,
            grid=(count,),
            in_specs=[
                pl.BlockSpec((1, steps, qw), one),
                pl.BlockSpec((1, slots, width), one),
                pl.BlockSpec((1, slots, width), one),
            ],
            out_specs=[pl.BlockSpec((1,) + shape[1:], one4)] * 2,
        ),
        out_shape=[jax.ShapeDtypeStruct(shape, jnp.float32)] * 2,
        compiler_params=pltpu.CompilerParams(vmem_limit_bytes=8 * MIB),
        name="cache_attention",
    )(meta, queries, key_cache, value_cache)


def project_kernel(dp, meta_ref, x_ref, key_ref, value_ref, key_mate_ref, value_mate_ref, *refs):
    out_refs, w_ref, held = refs[:8], refs[8], refs[9]
    seqs, steps, width = held.shape
    count = seqs // dp
    rows, kind_width = key_ref.shape
    core, half = meta_ref[CORE], meta_ref[HALF]
    for side, pair in ((0, (key_ref, value_ref)), (1, (key_mate_ref, value_mate_ref))):
        for kind, ref in enumerate(pair):
            first = pl.multiple_of((core ^ side) * rows, rows)
            w_ref[pl.ds(first, rows), kind * kind_width : (kind + 1) * kind_width] = ref[...]
    place = (meta_ref[DEPTH] & (dp // 2 - 1)) * 2 + half
    chunk = 4 * count * steps
    for m in range(dp):
        if m % 4 == 0:
            first = m * count * steps
            sums = bf16(dot32(x_ref[first : first + chunk], w_ref[...]))
        for n in range(count):
            i = (m % 4) * count + n
            held[(place ^ m) * count + n] = sums[i * steps : (i + 1) * steps]
    cw = width // 8
    own_half = (meta_ref[DEPTH] >= dp // 2).astype(jnp.int32)
    for i, ref in enumerate(out_refs):
        t = (half ^ ((i >> 1) & 1)) * 2 + (meta_ref[SECT] ^ (i & 1))
        group = pl.ds((own_half ^ (1 - (i >> 2))) * (seqs // 2), seqs // 2)
        for kind in range(2):
            cols = pl.ds(pl.multiple_of(kind * kind_width + t * cw, cw), cw)
            ref[:, :, kind * cw : (kind + 1) * cw] = held[group, :, cols]


def project(meta, x, weights, mates, dp, steps):
    seqs = x.shape[0] // steps
    rows, width = weights[0].shape
    out = jax.ShapeDtypeStruct((seqs // 2, steps, width // 2), jnp.bfloat16)
    return pl.pallas_call(
        functools.partial(project_kernel, dp),
        in_specs=[smem()] + [vmem()] * 5,
        out_specs=[vmem()] * 8,
        out_shape=[out] * 8,
        scratch_shapes=[
            pltpu.VMEM((2 * rows, 2 * width), x.dtype),
            pltpu.VMEM((seqs, steps, 2 * width), jnp.bfloat16),
        ],
        compiler_params=limit(x, *weights, *weights, *weights, *weights, *[out] * 32),
        name="project",
    )(meta, x, *weights, *mates)


def cut_kernel(spans, meta_ref, *refs):
    in_refs, out_refs = refs[:-spans], refs[-spans:]
    count = out_refs[0].shape[0]
    place = meta_ref[DEPTH] & (spans - 1)
    for m, ref in enumerate(out_refs):
        rows = pl.ds((place ^ m) * count, count)
        total = in_refs[0][rows].astype(jnp.float32)
        for part in in_refs[1:]:
            total += part[rows].astype(jnp.float32)
        ref[...] = total.astype(ref.dtype)


def cut(meta, parts, spans, first_type):
    shape = (parts[0].shape[0] // spans,) + parts[0].shape[1:]
    return pl.pallas_call(
        functools.partial(cut_kernel, spans),
        in_specs=[smem()] + [vmem()] * len(parts),
        out_specs=[vmem()] * spans,
        out_shape=[jax.ShapeDtypeStruct(shape, first_type)]
        + [jax.ShapeDtypeStruct(shape, jnp.bfloat16)] * (spans - 1),
        compiler_params=limit(*parts, *parts, *parts),
        name="cut",
    )(meta, *parts)


def own_group(meta_ref, groups):
    return meta_ref[SECT] * (groups // 2) + meta_ref[DEPTH]


def merge_kernel(groups, meta_ref, q_ref, o_ref, stat_ref, *refs):
    part_refs, out_refs, held = refs[: -groups - 1], refs[-groups - 1 : -1], refs[-1]
    count, steps, _ = q_ref.shape
    width = part_refs[0].shape[2] // 2
    rows = steps * GROUP
    fresh = part_refs[0][...]
    for ref in part_refs[1:]:
        fresh += ref[...].astype(jnp.float32)
    fresh = bf16(fresh).reshape(count * steps, 2 * width)
    shape = (count * rows, count * steps)
    row = lax.broadcasted_iota(jnp.int32, shape, 0)
    col = lax.broadcasted_iota(jnp.int32, shape, 1)
    causal = (row // rows == col // steps) & (col % steps <= row % steps)
    step = lax.broadcasted_iota(jnp.int32, (rows, HEAD), 0) % steps
    keep = jnp.concatenate([step < meta_ref[PROMPT + count + n] for n in range(count)], axis=0)
    for kv in range(width // HEAD):
        q = jnp.concatenate([stacked_heads(q_ref[n], kv) for n in range(count)], axis=0)
        stat = jnp.concatenate([stat_ref[n, kv, :, :2] for n in range(count)], axis=0)
        o = jnp.concatenate([o_ref[n, kv] for n in range(count)], axis=0)
        k = fresh[:, kv * HEAD : (kv + 1) * HEAD]
        v = fresh[:, width + kv * HEAD : width + (kv + 1) * HEAD]
        s = jnp.where(causal, dot_t(q, k) * SCALE, -1e30)
        top = jnp.maximum(stat[:, :1], jnp.max(s, axis=1, keepdims=True))
        e = jnp.exp(s - top)
        back = jnp.exp(stat[:, :1] - top)
        share = 1.0 / (back * stat[:, 1:] + jnp.sum(e, axis=1, keepdims=True))
        r = o * (back * share) + dot32(bf16(e * share), v)
        r = bf16(jnp.where(keep, r, 0.0))
        for n in range(count):
            for g in range(GROUP):
                h = kv * GROUP + g
                first = n * rows + g * steps
                held[n, :, h * HEAD : (h + 1) * HEAD] = r[first : first + steps]
    own = own_group(meta_ref, groups)
    slots = PROMPT + 2 * count
    for n in range(count):
        holder = lax.div(meta_ref[slots + own * count + n], count)
        for i in range(groups):

            @pl.when((holder ^ own) == i)
            def _():
                out_refs[i][...] = held[n]


def merge(meta, queries, o_cache, stats, parts, groups):
    shape = queries.shape[1:]
    return pl.pallas_call(
        functools.partial(merge_kernel, groups),
        in_specs=[smem()] + [vmem()] * (3 + len(parts)),
        out_specs=[vmem()] * groups,
        out_shape=[jax.ShapeDtypeStruct(shape, jnp.bfloat16)] * groups,
        scratch_shapes=[pltpu.VMEM(queries.shape, jnp.bfloat16)],
        compiler_params=limit(queries, o_cache, stats, *parts, *[queries] * (groups // queries.shape[0] + 1)),
        name="merge_fresh",
    )(meta, queries, o_cache, stats, *parts)


def pick_kernel(order, meta_ref, *refs):
    in_refs, out_ref, places = refs[:-2], refs[-2], refs[-1]
    groups = len(in_refs)
    count = out_ref.shape[0]
    slots = PROMPT + 2 * count

    def note(s, carry):
        places[meta_ref[slots + s]] = s
        return carry

    lax.fori_loop(0, groups * count, note, 0, unroll=8)
    own = own_group(meta_ref, groups)
    for r in range(count):
        source = lax.div(places[own * count + r], count)
        for m, ref in zip(order, in_refs):

            @pl.when((source ^ own) == m)
            def _():
                out_ref[r] = ref[...]


def pick(meta, blocks, order, count):
    out = jax.ShapeDtypeStruct((count,) + blocks[0].shape, jnp.bfloat16)
    return pl.pallas_call(
        functools.partial(pick_kernel, order),
        in_specs=[smem()] + [vmem()] * len(blocks),
        out_specs=vmem(),
        out_shape=out,
        scratch_shapes=[pltpu.SMEM((len(blocks) * count,), jnp.int32)],
        compiler_params=limit(out, *blocks),
        name="pick_rows",
    )(meta, *blocks)


def shards(
    dp,
    w_key,
    w_value,
    hidden,
    queries,
    key_cache,
    value_cache,
    prompt_lengths,
    rollout_lengths,
    batch_slots,
):
    count, steps, feats = hidden.shape
    tokens = count * steps
    groups = 2 * dp
    spans = dp // 2
    wide = feats // dp
    x, z, t = lax.axis_index("sect"), lax.axis_index("dp"), lax.axis_index("tp")
    p, c = t >> 1, t & 1
    everyone = ("sect", "dp", "tp")
    devices = [(i, j, k) for i in range(2) for j in range(dp) for k in range(4)]

    def flat(i, j, k):
        return (i * dp + j) * 4 + k

    def send(a, target):
        return lax.ppermute(a, everyone, [(flat(*d), target(*d)) for d in devices])

    def to_features(m):
        def target(i, j, k):
            e, half = divmod(j ^ m, 2)
            return (k * spans + e) * 4 + half * 2 + i

        return target

    def to_mate(i, j, k):
        return flat(i, j, k ^ 1)

    def in_plane(m):
        return lambda i, j, k: flat(k & 1, j, ((k >> 1) ^ (m >> 1)) * 2 + (i ^ (m & 1)))

    def to_depth(m):
        return lambda i, j, k: flat(i, j ^ m, k)

    def to_group(m):
        return lambda i, j, k: ((i * dp + j) ^ m) * 4 + k

    scalars = jnp.stack([c, p, x, z]).astype(jnp.int32)
    meta = jnp.concatenate([scalars, prompt_lengths, rollout_lengths, batch_slots])

    flat_hidden = hidden.reshape(tokens, feats)
    near = [
        send(lax.dynamic_slice_in_dim(flat_hidden, (z ^ m) * wide, wide, 1), to_features(m))
        for m in range(dp)
    ]
    weights = (w_key, w_value)
    mates = [send(w, to_mate) for w in weights]
    o_cache, stats = cache_attention(meta, queries, key_cache, value_cache)

    parts = project(meta, jnp.concatenate(near, axis=0), weights, mates, dp, steps)
    far, near = ([send(parts[first + m], in_plane(m)) for m in (3, 2, 1, 0)] for first in (0, 4))
    far = cut(meta, far, spans, jnp.bfloat16)
    far = [send(a, to_depth(spans + m)) for m, a in enumerate(far)]
    near = cut(meta, near, spans, jnp.float32)
    near = [a if m == 0 else send(a, to_depth(m)) for m, a in enumerate(near)]
    parts = near + far
    sends = merge(meta, queries, o_cache, stats, parts, groups)
    order = sorted(range(1, groups), key=lambda m: -(m & (dp - 1)))
    blocks = [send(sends[m], to_group(m)) for m in order]
    return pick(meta, blocks + [sends[0]], order + [0], count)


def solution(mesh):
    in_specs = (
        P(("sect", "dp", "tp"), None),
        P(("sect", "dp", "tp"), None),
        P(("sect", "dp"), None, "tp"),
        P(("sect", "dp"), None, "tp"),
        P(("sect", "dp"), None, "tp"),
        P(("sect", "dp"), None, "tp"),
        P(("sect", "dp")),
        P(("sect", "dp")),
        P(),
    )
    out_specs = P(("sect", "dp"), None, "tp")
    body = functools.partial(shards, mesh.shape["dp"])
    return jax.shard_map(body, mesh=mesh, in_specs=in_specs, out_specs=out_specs, check_vma=False)
```

time: 292 us -> 65.4 us (0.22)
  waiting for transfers between devices: 226 us -> 13.6 us
  starting transfers between devices: 10 us -> 40.7 us
  local copies, waits for them, and re-layouts: 27.3 us -> 1.17 us
  between operations: 13.4 us -> 0.2 us
  matrix products: 11.6 us -> 0 us
  Pallas kernels: 0 us -> 9.55 us
    all_gather x4 -> x0, waiting for transfers between devices: 195 us -> none  [the longest x1 76.3 us: shards(): lax.all_gather(w_key, ('sect', 'dp'), axis=0, tiled=True)]
    ppermute x0 -> x24, starting transfers between devices: none -> 40.7 us  [send(): return lax.ppermute(a, everyone, [(flat(*d), target(*d)) for d in devices])]
    all_to_all x2 -> x0, waiting for transfers between devices: 30.1 us -> none  [the longest x1 30.1 us: shards(): lax.all_to_all(rows_value, 'tp', split_axis=1, concat_axis=0, tiled=True)]
    ppermute x0 -> x24, waiting for transfers between devices: none -> 13.6 us  [send(): return lax.ppermute(a, everyone, [(flat(*d), target(*d)) for d in devices])]
    all_to_all x2 -> x0, local copies, waits for them, and re-layouts: 12.5 us -> none  [the longest x1 6.27 us: shards(): lax.all_to_all(rows_key, 'tp', split_axis=1, concat_axis=0, tiled=True)]
    dot_general x7 -> x0, matrix products: 11.6 us -> none  [the longest x1 3.93 us: shards(): jnp.einsum('rs,sid->rid', select, lax.all_gather(attended, ('sect', 'dp')...]
    all_to_all x2 -> x0, starting transfers between devices: 9.91 us -> none  [the longest x1 4.97 us: shards(): lax.all_to_all(rows_value, 'tp', split_axis=1, concat_axis=0, tiled=True)]
    pallas_call x0 -> x6, Pallas kernels: none -> 9.55 us  [the longest x1 3.26 us: cache_attention(): pl.pallas_call(cache_kernel, grid_spec=pltpu.PrefetchScalarGridSpec(num_s...]
  transfers between devices with their start and end apart: 6 -> 24, of which waited for: 5 -> 10; matrix products, arithmetic and copies ran while one was open for 8% -> 2% of each run, Pallas kernels for 0% -> 7%
where the time goes in v1:
time: 65.4 us; the launch traced here: 65.2 us
  starting transfers between devices  40.7 us (62%)
  waiting for transfers between devices  13.6 us (21%)
  Pallas kernels  9.55 us (15%)
  local copies, waits for them, and re-layouts  1.17 us (2%)
    ppermute x24, starting transfers between devices, send(): return lax.ppermute(a, everyone, [(flat(*d), target(*d)) for d in devices])  40.7 us
    ppermute x24, waiting for transfers between devices, send(): return lax.ppermute(a, everyone, [(flat(*d), target(*d)) for d in devices])  13.6 us
    pallas_call x1, Pallas kernels, cache_attention(): pl.pallas_call(cache_kernel, grid_spec=pltpu.PrefetchScalarGridSpec(num_s...  3.26 us
    pallas_call x1, Pallas kernels, merge(): pl.pallas_call(functools.partial(merge_kernel, groups), in_specs=[smem()]...  2 us
    pallas_call x1, Pallas kernels, project(): pl.pallas_call(functools.partial(project_kernel, dp), in_specs=[smem()] +...  1.57 us
    pallas_call x1, Pallas kernels, pick(): pl.pallas_call(functools.partial(pick_kernel, order), in_specs=[smem()] +...  1.49 us
  transfers between devices with their start and end apart: 24, of which 10 were waited for; matrix products, arithmetic and copies ran while one was open for 2% of the time, Pallas kernels for 7%

profile of v1, /device:TPU:0, one launch (start us, length us, event | category | flops | bytes accessed | tf_op | source)
XLA Modules:
  0.0 65.2 jit_solution(14783733410688991890)
XLA Ops:
  0.5 1.1 %constant_dynamic-slice_fusion.3 = (bf16[64,512]{1,0:T(8,128)(2,1)S(1)}, bf16[64,512]{1,0:T(8,128)(2,1)S(1)}, bf16[64,512]{1,0:T(8,128)(2,1)S(1)}, bf16[64,512]{1,0:T(8,128)(2,1)S(1)}) fusion(bf16[64,2048]{1,0:T(8,128)(2,1)} %bitcast.5, s32[]{:T(128)S(6)} %select_n.12, s32[]{:T(128)S(6)} %select_n.15, s32[]{:T(128)S(6)} %select_n.14, s32[]{:T(128)S(6)} %select_n.13), kind=kLoop, calls=%fused_computation.4 | loop fusion | bytes 524304 | tf_op jit(solution)/shard_map/dynamic_slice | solution.py:313
  2.3 8.5 %collective-permute-start.3 = (bf16[64,512]{1,0:T(8,128)(2,1)S(1)}, bf16[64,512]{1,0:T(8,128)(2,1)S(1)}, u32[]{:S(2)}, u32[]{:S(2)}) collective-permute-start(bf16[64,512]{1,0:T(8,128)(2,1)S(1)} %get-tuple-element.50), channel_id=1, source_target_pairs={{0,6},{1,14},{2,22},{3,30},{4,4},{5,12},{6,20},{7,28},{8,2},{9,10}... | collective-permute-start | bytes 196616 | tf_op jit(solution)/shard_map/ppermute | solution.py:287
  10.9 2.8 %collective-permute-start.1 = (bf16[64,512]{1,0:T(8,128)(2,1)S(1)}, bf16[64,512]{1,0:T(8,128)(2,1)S(1)}, u32[]{:S(2)}, u32[]{:S(2)}) collective-permute-start(bf16[64,512]{1,0:T(8,128)(2,1)S(1)} %get-tuple-element.52), channel_id=1, source_target_pairs={{0,2},{1,10},{2,18},{3,26},{4,0},{5,8},{6,16},{7,24},{8,6},{9,14},... | collective-permute-start | bytes 196616 | tf_op jit(solution)/shard_map/ppermute | solution.py:287
  14.4 3.0 %collective-permute-done.2 = bf16[64,512]{1,0:T(8,128)(2,1)S(1)} collective-permute-done((bf16[64,512]{1,0:T(8,128)(2,1)S(1)}, bf16[64,512]{1,0:T(8,128)(2,1)S(1)}, u32[]{:S(2)}, u32[]{:S(2)}) %collective-permute-start.2) | collective-permute-done | bytes 65568 | tf_op jit(solution)/shard_map/ppermute | solution.py:287
  17.5 1.6 %project.1 = (bf16[8,16,512]{2,1,0:T(8,128)(2,1)S(1)}, bf16[8,16,512]{2,1,0:T(8,128)(2,1)S(1)}, bf16[8,16,512]{2,1,0:T(8,128)(2,1)S(1)}, bf16[8,16,512]{2,1,0:T(...) custom-call(s32[44]{0:T(128)S(1)} %concatenate.6.meta_ref, ...), custom_call_target="tpu_custom_call" | custom-call | tf_op jit(solution)/shard_map/project/pallas_call | solution.py:127
  19.1 3.4 %collective-permute-start.6 = (bf16[8,16,512]{2,1,0:T(8,128)(2,1)S(1)}, bf16[8,16,512]{2,1,0:T(8,128)(2,1)S(1)}, u32[]{:S(2)}, u32[]{:S(2)}) collective-permute-start(bf16[8,16,512]{2,1,0:T(8,128)(2,1)S(1)} %get-tuple-element.29), channel_id=1, source_target_pairs={{0,3},{1,19},{2,1},{3,17},{4,7},{5,23},{6,5},{7,21},{8,11},{9,27},... | collective-permute-start | bytes 393224 | tf_op jit(solution)/shard_map/ppermute | solution.py:287
  23.8 4.5 %collective-permute-start.11 = (bf16[8,16,512]{2,1,0:T(8,128)(2,1)S(1)}, bf16[8,16,512]{2,1,0:T(8,128)(2,1)S(1)}, u32[]{:S(2)}, u32[]{:S(2)}) collective-permute-start(bf16[8,16,512]{2,1,0:T(8,128)(2,1)S(1)} %get-tuple-element.35), channel_id=1, source_target_pairs={{0,3},{1,19},{2,1},{3,17},{4,7},{5,23},{6,5},{7,21},{8,11},{9,27},... | collective-permute-start | bytes 393224 | tf_op jit(solution)/shard_map/ppermute | solution.py:287
  28.9 0.8 %collective-permute-done.7.refs_1_ = bf16[8,16,512]{2,1,0:T(8,128)(2,1)S(1)} collective-permute-done((bf16[8,16,512]{2,1,0:T(8,128)(2,1)S(1)}, bf16[8,16,512]{2,1,0:T(8,128)(2,1)S(1)}, u32[]{:S(2)}, u32[]{:S(2)}) %collective-permute-start.7) | collective-permute-done | bytes 131104 | tf_op jit(solution)/shard_map/ppermute | solution.py:287
  31.0 0.8 %collective-permute-start.10 = (bf16[4,16,512]{2,1,0:T(8,128)(2,1)S(1)}, bf16[4,16,512]{2,1,0:T(8,128)(2,1)S(1)}, u32[]{:S(2)}, u32[]{:S(2)}) collective-permute-start(bf16[4,16,512]{2,1,0:T(8,128)(2,1)S(1)} %get-tuple-element.34), channel_id=1, source_target_pairs={{0,4},{1,5},{2,6},{3,7},{4,0},{5,1},{6,2},{7,3},{8,12},{9,13},{10,... | collective-permute-start | bytes 196616 | tf_op jit(solution)/shard_map/ppermute | solution.py:287
  31.8 1.8 %collective-permute-done.11.refs_0_ = bf16[8,16,512]{2,1,0:T(8,128)(2,1)S(1)} collective-permute-done((bf16[8,16,512]{2,1,0:T(8,128)(2,1)S(1)}, bf16[8,16,512]{2,1,0:T(8,128)(2,1)S(1)}, u32[]{:S(2)}, u32[]{:S(2)}) %collective-permute-start.11) | collective-permute-done | bytes 131104 | tf_op jit(solution)/shard_map/ppermute | solution.py:287
  33.6 2.5 %collective-permute-done.12.refs_1_ = bf16[8,16,512]{2,1,0:T(8,128)(2,1)S(1)} collective-permute-done((bf16[8,16,512]{2,1,0:T(8,128)(2,1)S(1)}, bf16[8,16,512]{2,1,0:T(8,128)(2,1)S(1)}, u32[]{:S(2)}, u32[]{:S(2)}) %collective-permute-start.12) | collective-permute-done | bytes 131104 | tf_op jit(solution)/shard_map/ppermute | solution.py:287
  36.6 1.5 %collective-permute-start.15 = (bf16[4,16,512]{2,1,0:T(8,128)(2,1)S(1)}, bf16[4,16,512]{2,1,0:T(8,128)(2,1)S(1)}, u32[]{:S(2)}, u32[]{:S(2)}) collective-permute-start(bf16[4,16,512]{2,1,0:T(8,128)(2,1)S(1)} %get-tuple-element.39), channel_id=1, source_target_pairs={{0,8},{1,9},{2,10},{3,11},{4,12},{5,13},{6,14},{7,15},{8,0},{9,1},... | collective-permute-start | bytes 196616 | tf_op jit(solution)/shard_map/ppermute | solution.py:287
  38.2 1.6 %collective-permute-start.16 = (bf16[4,16,512]{2,1,0:T(8,128)(2,1)S(1)}, bf16[4,16,512]{2,1,0:T(8,128)(2,1)S(1)}, u32[]{:S(2)}, u32[]{:S(2)}) collective-permute-start(bf16[4,16,512]{2,1,0:T(8,128)(2,1)S(1)} %get-tuple-element.40), channel_id=1, source_target_pairs={{0,12},{1,13},{2,14},{3,15},{4,8},{5,9},{6,10},{7,11},{8,4},{9,5},... | collective-permute-start | bytes 196616 | tf_op jit(solution)/shard_map/ppermute | solution.py:287
  39.8 3.3 %cache_attention.1 = (f32[4,2,128,128]{3,2,1,0:T(8,128)S(1)}, f32[4,2,128,128]{3,2,1,0:T(8,128)S(1)}) custom-call(s32[44]{0:T(128)S(1)} %concatenate.6.meta_ref, bf16[4,16,2048]{2,1,0:T(8,128)(2,1)S(1)} %copy-done.2, bf16[4,512,256]{2,1,0:T(8,128)(2,1)S(1)} %copy-done, bf16[4,512,256]{2,1,0:T(8,128)(2,1)S(1)} %copy-done.1), custom_call_target="tpu_custom_call" | custom-call | tf_op jit(solution)/shard_map/cache_attention/pallas_call | solution.py:76
  43.1 2.1 %collective-permute-done.15.refs_2_ = bf16[4,16,512]{2,1,0:T(8,128)(2,1)S(1)} collective-permute-done((bf16[4,16,512]{2,1,0:T(8,128)(2,1)S(1)}, bf16[4,16,512]{2,1,0:T(8,128)(2,1)S(1)}, u32[]{:S(2)}, u32[]{:S(2)}) %collective-permute-start.15) | collective-permute-done | bytes 65568 | tf_op jit(solution)/shard_map/ppermute | solution.py:287
  45.2 2.0 %merge_fresh.1 = (bf16[16,2048]{1,0:T(8,128)(2,1)S(1)}, bf16[16,2048]{1,0:T(8,128)(2,1)S(1)}, bf16[16,2048]{1,0:T(8,128)(2,1)S(1)}, bf16[16,2048]{1,0:T(8,128)(2...) custom-call(s32[44]{0:T(128)S(1)} %concatenate.6.meta_ref, ...), custom_call_target="tpu_custom_call" | custom-call | tf_op jit(solution)/shard_map/merge_fresh/pallas_call | solution.py:216
  47.2 1.2 %collective-permute-start.17 = (bf16[16,2048]{1,0:T(8,128)(2,1)S(1)}, bf16[16,2048]{1,0:T(8,128)(2,1)S(1)}, u32[]{:S(2)}, u32[]{:S(2)}) collective-permute-start(bf16[16,2048]{1,0:T(8,128)(2,1)S(1)} %get-tuple-element.41), channel_id=1, source_target_pairs={{0,12},{1,13},{2,14},{3,15},{4,8},{5,9},{6,10},{7,11},{8,4},{9,5},... | collective-permute-start | bytes 196616 | tf_op jit(solution)/shard_map/ppermute | solution.py:287
  48.4 3.6 %collective-permute-start.18 = (bf16[16,2048]{1,0:T(8,128)(2,1)S(1)}, bf16[16,2048]{1,0:T(8,128)(2,1)S(1)}, u32[]{:S(2)}, u32[]{:S(2)}) collective-permute-start(bf16[16,2048]{1,0:T(8,128)(2,1)S(1)} %get-tuple-element.42), channel_id=1, source_target_pairs={{0,28},{1,29},{2,30},{3,31},{4,24},{5,25},{6,26},{7,27},{8,20},{9,... | collective-permute-start | bytes 196616 | tf_op jit(solution)/shard_map/ppermute | solution.py:287
  52.0 2.9 %collective-permute-start.20 = (bf16[16,2048]{1,0:T(8,128)(2,1)S(1)}, bf16[16,2048]{1,0:T(8,128)(2,1)S(1)}, u32[]{:S(2)}, u32[]{:S(2)}) collective-permute-start(bf16[16,2048]{1,0:T(8,128)(2,1)S(1)} %get-tuple-element.44), channel_id=1, source_target_pairs={{0,24},{1,25},{2,26},{3,27},{4,28},{5,29},{6,30},{7,31},{8,16},{9,... | collective-permute-start | bytes 196616 | tf_op jit(solution)/shard_map/ppermute | solution.py:287
  55.0 2.8 %collective-permute-start.22 = (bf16[16,2048]{1,0:T(8,128)(2,1)S(1)}, bf16[16,2048]{1,0:T(8,128)(2,1)S(1)}, u32[]{:S(2)}, u32[]{:S(2)}) collective-permute-start(bf16[16,2048]{1,0:T(8,128)(2,1)S(1)} %get-tuple-element.46), channel_id=1, source_target_pairs={{0,20},{1,21},{2,22},{3,23},{4,16},{5,17},{6,18},{7,19},{8,28},{9,... | collective-permute-start | bytes 196616 | tf_op jit(solution)/shard_map/ppermute | solution.py:287
  57.9 3.1 %collective-permute-start.23 = (bf16[16,2048]{1,0:T(8,128)(2,1)S(1)}, bf16[16,2048]{1,0:T(8,128)(2,1)S(1)}, u32[]{:S(2)}, u32[]{:S(2)}) collective-permute-start(bf16[16,2048]{1,0:T(8,128)(2,1)S(1)} %get-tuple-element.47), channel_id=1, source_target_pairs={{0,16},{1,17},{2,18},{3,19},{4,20},{5,21},{6,22},{7,23},{8,24},{9,... | collective-permute-start | bytes 196616 | tf_op jit(solution)/shard_map/ppermute | solution.py:287
  61.0 1.0 %collective-permute-done.19.refs_2_ = bf16[16,2048]{1,0:T(8,128)(2,1)S(1)} collective-permute-done((bf16[16,2048]{1,0:T(8,128)(2,1)S(1)}, bf16[16,2048]{1,0:T(8,128)(2,1)S(1)}, u32[]{:S(2)}, u32[]{:S(2)}) %collective-permute-start.19) | collective-permute-done | bytes 65568 | tf_op jit(solution)/shard_map/ppermute | solution.py:287
  62.0 1.1 %collective-permute-done.22.refs_5_ = bf16[16,2048]{1,0:T(8,128)(2,1)S(1)} collective-permute-done((bf16[16,2048]{1,0:T(8,128)(2,1)S(1)}, bf16[16,2048]{1,0:T(8,128)(2,1)S(1)}, u32[]{:S(2)}, u32[]{:S(2)}) %collective-permute-start.22) | collective-permute-done | bytes 65568 | tf_op jit(solution)/shard_map/ppermute | solution.py:287
  63.7 1.5 %pick_rows.1 = bf16[4,16,2048]{2,1,0:T(8,128)(2,1)} custom-call(s32[44]{0:T(128)S(1)} %concatenate.6.meta_ref, bf16[16,2048]{1,0:T(8,128)(2,1)S(1)} %collective-permute-done.17.refs_0_, bf16[16,2048]{1,0:T(8,128)(2,1)S(1)} %collective-permute-done.18.refs_1_, bf16[16,2048]{1,0:T(8,128)(2,1)S(1)} %collective-permute-done.19.refs_2_, ...), custom_call_target="tpu_custom_call" | custom-call | tf_op jit(solution)/shard_map/pick_rows/pallas_call | solution.py:250
  (49 shorter events, 6.7 us)
Async XLA Ops:
  0.0 17.4 %collective-permute-start.4 = (bf16[256,1024]{1,0:T(8,128)(2,1)}, bf16[256,1024]{1,0:T(8,128)(2,1)S(1)}, u32[]{:S(2)}, u32[]{:S(2)}) collective-permute-start(bf16[256,1024]{1,0:T(8,128)(2,1)} %key_ref.1), channel_id=1, source_target_pairs={{0,1},{1,0},{2,3},{3,2},{4,5},{5,4},{6,7},{7,6},{8,9},{9,8},{10,11... | collective-permute-start | bytes 1572872 | tf_op jit(solution)/shard_map/ppermute | solution.py:287
  0.5 17.0 %collective-permute-start.5 = (bf16[256,1024]{1,0:T(8,128)(2,1)}, bf16[256,1024]{1,0:T(8,128)(2,1)S(1)}, u32[]{:S(2)}, u32[]{:S(2)}) collective-permute-start(bf16[256,1024]{1,0:T(8,128)(2,1)} %value_ref.1), channel_id=1, source_target_pairs={{0,1},{1,0},{2,3},{3,2},{4,5},{5,4},{6,7},{7,6},{8,9},{9,8},{10,11... | collective-permute-start | bytes 1572872 | tf_op jit(solution)/shard_map/ppermute | solution.py:287
  1.6 9.3 %collective-permute-start = (bf16[64,512]{1,0:T(8,128)(2,1)S(1)}, bf16[64,512]{1,0:T(8,128)(2,1)S(1)}, u32[]{:S(2)}, u32[]{:S(2)}) collective-permute-start(bf16[64,512]{1,0:T(8,128)(2,1)S(1)} %get-tuple-element.49), channel_id=1, source_target_pairs={{0,0},{1,8},{2,16},{3,24},{4,2},{5,10},{6,18},{7,26},{8,4},{9,12},... | collective-permute-start | bytes 196616 | tf_op jit(solution)/shard_map/ppermute | solution.py:287
  2.3 12.2 %collective-permute-start.3 = (bf16[64,512]{1,0:T(8,128)(2,1)S(1)}, bf16[64,512]{1,0:T(8,128)(2,1)S(1)}, u32[]{:S(2)}, u32[]{:S(2)}) collective-permute-start(bf16[64,512]{1,0:T(8,128)(2,1)S(1)} %get-tuple-element.50), channel_id=1, source_target_pairs={{0,6},{1,14},{2,22},{3,30},{4,4},{5,12},{6,20},{7,28},{8,2},{9,10}... | collective-permute-start | bytes 196616 | tf_op jit(solution)/shard_map/ppermute | solution.py:287
  10.8 6.6 %collective-permute-start.2 = (bf16[64,512]{1,0:T(8,128)(2,1)S(1)}, bf16[64,512]{1,0:T(8,128)(2,1)S(1)}, u32[]{:S(2)}, u32[]{:S(2)}) collective-permute-start(bf16[64,512]{1,0:T(8,128)(2,1)S(1)} %get-tuple-element.51), channel_id=1, source_target_pairs={{0,4},{1,12},{2,20},{3,28},{4,6},{5,14},{6,22},{7,30},{8,0},{9,8},... | collective-permute-start | bytes 196616 | tf_op jit(solution)/shard_map/ppermute | solution.py:287
  10.9 6.5 %collective-permute-start.1 = (bf16[64,512]{1,0:T(8,128)(2,1)S(1)}, bf16[64,512]{1,0:T(8,128)(2,1)S(1)}, u32[]{:S(2)}, u32[]{:S(2)}) collective-permute-start(bf16[64,512]{1,0:T(8,128)(2,1)S(1)} %get-tuple-element.52), channel_id=1, source_target_pairs={{0,2},{1,10},{2,18},{3,26},{4,0},{5,8},{6,16},{7,24},{8,6},{9,14},... | collective-permute-start | bytes 196616 | tf_op jit(solution)/shard_map/ppermute | solution.py:287
  19.1 9.2 %collective-permute-start.6 = (bf16[8,16,512]{2,1,0:T(8,128)(2,1)S(1)}, bf16[8,16,512]{2,1,0:T(8,128)(2,1)S(1)}, u32[]{:S(2)}, u32[]{:S(2)}) collective-permute-start(bf16[8,16,512]{2,1,0:T(8,128)(2,1)S(1)} %get-tuple-element.29), channel_id=1, source_target_pairs={{0,3},{1,19},{2,1},{3,17},{4,7},{5,23},{6,5},{7,21},{8,11},{9,27},... | collective-permute-start | bytes 393224 | tf_op jit(solution)/shard_map/ppermute | solution.py:287
  22.5 7.2 %collective-permute-start.7 = (bf16[8,16,512]{2,1,0:T(8,128)(2,1)S(1)}, bf16[8,16,512]{2,1,0:T(8,128)(2,1)S(1)}, u32[]{:S(2)}, u32[]{:S(2)}) collective-permute-start(bf16[8,16,512]{2,1,0:T(8,128)(2,1)S(1)} %get-tuple-element.30), channel_id=1, source_target_pairs={{0,2},{1,18},{2,0},{3,16},{4,6},{5,22},{6,4},{7,20},{8,10},{9,26},... | collective-permute-start | bytes 393224 | tf_op jit(solution)/shard_map/ppermute | solution.py:287
  23.1 6.6 %collective-permute-start.8 = (bf16[8,16,512]{2,1,0:T(8,128)(2,1)S(1)}, bf16[8,16,512]{2,1,0:T(8,128)(2,1)S(1)}, u32[]{:S(2)}, u32[]{:S(2)}) collective-permute-start(bf16[8,16,512]{2,1,0:T(8,128)(2,1)S(1)} %get-tuple-element.31), channel_id=1, source_target_pairs={{0,1},{1,17},{2,3},{3,19},{4,5},{5,21},{6,7},{7,23},{8,9},{9,25},{... | collective-permute-start | bytes 393224 | tf_op jit(solution)/shard_map/ppermute | solution.py:287
  23.1 7.2 %collective-permute-start.9 = (bf16[8,16,512]{2,1,0:T(8,128)(2,1)S(1)}, bf16[8,16,512]{2,1,0:T(8,128)(2,1)S(1)}, u32[]{:S(2)}, u32[]{:S(2)}) collective-permute-start(bf16[8,16,512]{2,1,0:T(8,128)(2,1)S(1)} %get-tuple-element.32), channel_id=1, source_target_pairs={{0,0},{1,16},{2,2},{3,18},{4,4},{5,20},{6,6},{7,22},{8,8},{9,24},{... | collective-permute-start | bytes 393224 | tf_op jit(solution)/shard_map/ppermute | solution.py:287
  23.8 9.8 %collective-permute-start.11 = (bf16[8,16,512]{2,1,0:T(8,128)(2,1)S(1)}, bf16[8,16,512]{2,1,0:T(8,128)(2,1)S(1)}, u32[]{:S(2)}, u32[]{:S(2)}) collective-permute-start(bf16[8,16,512]{2,1,0:T(8,128)(2,1)S(1)} %get-tuple-element.35), channel_id=1, source_target_pairs={{0,3},{1,19},{2,1},{3,17},{4,7},{5,23},{6,5},{7,21},{8,11},{9,27},... | collective-permute-start | bytes 393224 | tf_op jit(solution)/shard_map/ppermute | solution.py:287
  28.3 7.7 %collective-permute-start.12 = (bf16[8,16,512]{2,1,0:T(8,128)(2,1)S(1)}, bf16[8,16,512]{2,1,0:T(8,128)(2,1)S(1)}, u32[]{:S(2)}, u32[]{:S(2)}) collective-permute-start(bf16[8,16,512]{2,1,0:T(8,128)(2,1)S(1)} %get-tuple-element.36), channel_id=1, source_target_pairs={{0,2},{1,18},{2,0},{3,16},{4,6},{5,22},{6,4},{7,20},{8,10},{9,26},... | collective-permute-start | bytes 393224 | tf_op jit(solution)/shard_map/ppermute | solution.py:287
  29.7 6.3 %collective-permute-start.13 = (bf16[8,16,512]{2,1,0:T(8,128)(2,1)S(1)}, bf16[8,16,512]{2,1,0:T(8,128)(2,1)S(1)}, u32[]{:S(2)}, u32[]{:S(2)}) collective-permute-start(bf16[8,16,512]{2,1,0:T(8,128)(2,1)S(1)} %get-tuple-element.37), channel_id=1, source_target_pairs={{0,1},{1,17},{2,3},{3,19},{4,5},{5,21},{6,7},{7,23},{8,9},{9,25},{... | collective-permute-start | bytes 393224 | tf_op jit(solution)/shard_map/ppermute | solution.py:287
  29.7 6.3 %collective-permute-start.14 = (bf16[8,16,512]{2,1,0:T(8,128)(2,1)S(1)}, bf16[8,16,512]{2,1,0:T(8,128)(2,1)S(1)}, u32[]{:S(2)}, u32[]{:S(2)}) collective-permute-start(bf16[8,16,512]{2,1,0:T(8,128)(2,1)S(1)} %get-tuple-element.38), channel_id=1, source_target_pairs={{0,0},{1,16},{2,2},{3,18},{4,4},{5,20},{6,6},{7,22},{8,8},{9,24},{... | collective-permute-start | bytes 393224 | tf_op jit(solution)/shard_map/ppermute | solution.py:287
  31.0 12.1 %collective-permute-start.10 = (bf16[4,16,512]{2,1,0:T(8,128)(2,1)S(1)}, bf16[4,16,512]{2,1,0:T(8,128)(2,1)S(1)}, u32[]{:S(2)}, u32[]{:S(2)}) collective-permute-start(bf16[4,16,512]{2,1,0:T(8,128)(2,1)S(1)} %get-tuple-element.34), channel_id=1, source_target_pairs={{0,4},{1,5},{2,6},{3,7},{4,0},{5,1},{6,2},{7,3},{8,12},{9,13},{10,... | collective-permute-start | bytes 196616 | tf_op jit(solution)/shard_map/ppermute | solution.py:287
  36.6 8.5 %collective-permute-start.15 = (bf16[4,16,512]{2,1,0:T(8,128)(2,1)S(1)}, bf16[4,16,512]{2,1,0:T(8,128)(2,1)S(1)}, u32[]{:S(2)}, u32[]{:S(2)}) collective-permute-start(bf16[4,16,512]{2,1,0:T(8,128)(2,1)S(1)} %get-tuple-element.39), channel_id=1, source_target_pairs={{0,8},{1,9},{2,10},{3,11},{4,12},{5,13},{6,14},{7,15},{8,0},{9,1},... | collective-permute-start | bytes 196616 | tf_op jit(solution)/shard_map/ppermute | solution.py:287
  38.2 7.0 %collective-permute-start.16 = (bf16[4,16,512]{2,1,0:T(8,128)(2,1)S(1)}, bf16[4,16,512]{2,1,0:T(8,128)(2,1)S(1)}, u32[]{:S(2)}, u32[]{:S(2)}) collective-permute-start(bf16[4,16,512]{2,1,0:T(8,128)(2,1)S(1)} %get-tuple-element.40), channel_id=1, source_target_pairs={{0,12},{1,13},{2,14},{3,15},{4,8},{5,9},{6,10},{7,11},{8,4},{9,5},... | collective-permute-start | bytes 196616 | tf_op jit(solution)/shard_map/ppermute | solution.py:287
  47.2 7.9 %collective-permute-start.17 = (bf16[16,2048]{1,0:T(8,128)(2,1)S(1)}, bf16[16,2048]{1,0:T(8,128)(2,1)S(1)}, u32[]{:S(2)}, u32[]{:S(2)}) collective-permute-start(bf16[16,2048]{1,0:T(8,128)(2,1)S(1)} %get-tuple-element.41), channel_id=1, source_target_pairs={{0,12},{1,13},{2,14},{3,15},{4,8},{5,9},{6,10},{7,11},{8,4},{9,5},... | collective-permute-start | bytes 196616 | tf_op jit(solution)/shard_map/ppermute | solution.py:287
  48.4 9.5 %collective-permute-start.18 = (bf16[16,2048]{1,0:T(8,128)(2,1)S(1)}, bf16[16,2048]{1,0:T(8,128)(2,1)S(1)}, u32[]{:S(2)}, u32[]{:S(2)}) collective-permute-start(bf16[16,2048]{1,0:T(8,128)(2,1)S(1)} %get-tuple-element.42), channel_id=1, source_target_pairs={{0,28},{1,29},{2,30},{3,31},{4,24},{5,25},{6,26},{7,27},{8,20},{9,... | collective-permute-start | bytes 196616 | tf_op jit(solution)/shard_map/ppermute | solution.py:287
  52.0 9.9 %collective-permute-start.19 = (bf16[16,2048]{1,0:T(8,128)(2,1)S(1)}, bf16[16,2048]{1,0:T(8,128)(2,1)S(1)}, u32[]{:S(2)}, u32[]{:S(2)}) collective-permute-start(bf16[16,2048]{1,0:T(8,128)(2,1)S(1)} %get-tuple-element.43), channel_id=1, source_target_pairs={{0,8},{1,9},{2,10},{3,11},{4,12},{5,13},{6,14},{7,15},{8,0},{9,1},... | collective-permute-start | bytes 196616 | tf_op jit(solution)/shard_map/ppermute | solution.py:287
  52.0 10.0 %collective-permute-start.20 = (bf16[16,2048]{1,0:T(8,128)(2,1)S(1)}, bf16[16,2048]{1,0:T(8,128)(2,1)S(1)}, u32[]{:S(2)}, u32[]{:S(2)}) collective-permute-start(bf16[16,2048]{1,0:T(8,128)(2,1)S(1)} %get-tuple-element.44), channel_id=1, source_target_pairs={{0,24},{1,25},{2,26},{3,27},{4,28},{5,29},{6,30},{7,31},{8,16},{9,... | collective-permute-start | bytes 196616 | tf_op jit(solution)/shard_map/ppermute | solution.py:287
  54.9 7.1 %collective-permute-start.21 = (bf16[16,2048]{1,0:T(8,128)(2,1)S(1)}, bf16[16,2048]{1,0:T(8,128)(2,1)S(1)}, u32[]{:S(2)}, u32[]{:S(2)}) collective-permute-start(bf16[16,2048]{1,0:T(8,128)(2,1)S(1)} %get-tuple-element.45), channel_id=1, source_target_pairs={{0,4},{1,5},{2,6},{3,7},{4,0},{5,1},{6,2},{7,3},{8,12},{9,13},{10,... | collective-permute-start | bytes 196616 | tf_op jit(solution)/shard_map/ppermute | solution.py:287
  55.0 8.0 %collective-permute-start.22 = (bf16[16,2048]{1,0:T(8,128)(2,1)S(1)}, bf16[16,2048]{1,0:T(8,128)(2,1)S(1)}, u32[]{:S(2)}, u32[]{:S(2)}) collective-permute-start(bf16[16,2048]{1,0:T(8,128)(2,1)S(1)} %get-tuple-element.46), channel_id=1, source_target_pairs={{0,20},{1,21},{2,22},{3,23},{4,16},{5,17},{6,18},{7,19},{8,28},{9,... | collective-permute-start | bytes 196616 | tf_op jit(solution)/shard_map/ppermute | solution.py:287
  57.9 5.9 %collective-permute-start.23 = (bf16[16,2048]{1,0:T(8,128)(2,1)S(1)}, bf16[16,2048]{1,0:T(8,128)(2,1)S(1)}, u32[]{:S(2)}, u32[]{:S(2)}) collective-permute-start(bf16[16,2048]{1,0:T(8,128)(2,1)S(1)} %get-tuple-element.47), channel_id=1, source_target_pairs={{0,16},{1,17},{2,18},{3,19},{4,20},{5,21},{6,22},{7,23},{8,24},{9,... | collective-permute-start | bytes 196616 | tf_op jit(solution)/shard_map/ppermute | solution.py:287
  (8 other events, 138.7 us)

commit v2 on v1

--- a/solution.py
+++ b/solution.py
@@ -92,24 +92,24 @@
 
 
 def project_kernel(dp, meta_ref, x_ref, key_ref, value_ref, key_mate_ref, value_mate_ref, *refs):
-    out_refs, w_ref, held = refs[:8], refs[8], refs[9]
+    out_refs, held = refs[:8], refs[8]
     seqs, steps, width = held.shape
     count = seqs // dp
     rows, kind_width = key_ref.shape
     core, half = meta_ref[CORE], meta_ref[HALF]
-    for side, pair in ((0, (key_ref, value_ref)), (1, (key_mate_ref, value_mate_ref))):
-        for kind, ref in enumerate(pair):
-            first = pl.multiple_of((core ^ side) * rows, rows)
-            w_ref[pl.ds(first, rows), kind * kind_width : (kind + 1) * kind_width] = ref[...]
+    first, second = x_ref[:, :rows], x_ref[:, rows:]
+    own, mate = jnp.where(core == 0, first, second), jnp.where(core == 0, second, first)
     place = (meta_ref[DEPTH] & (dp // 2 - 1)) * 2 + half
     chunk = 4 * count * steps
-    for m in range(dp):
-        if m % 4 == 0:
-            first = m * count * steps
-            sums = bf16(dot32(x_ref[first : first + chunk], w_ref[...]))
-        for n in range(count):
-            i = (m % 4) * count + n
-            held[(place ^ m) * count + n] = sums[i * steps : (i + 1) * steps]
+    for kind, refs in enumerate(((key_ref, key_mate_ref), (value_ref, value_mate_ref))):
+        cols = slice(kind * kind_width, (kind + 1) * kind_width)
+        for m in range(dp):
+            if m % 4 == 0:
+                part = slice(m * count * steps, m * count * steps + chunk)
+                sums = bf16(dot32(own[part], refs[0][...]) + dot32(mate[part], refs[1][...]))
+            for n in range(count):
+                i = (m % 4) * count + n
+                held[(place ^ m) * count + n, :, cols] = sums[i * steps : (i + 1) * steps]
     cw = width // 8
     own_half = (meta_ref[DEPTH] >= dp // 2).astype(jnp.int32)
     for i, ref in enumerate(out_refs):
@@ -129,16 +129,32 @@
         in_specs=[smem()] + [vmem()] * 5,
         out_specs=[vmem()] * 8,
         out_shape=[out] * 8,
-        scratch_shapes=[
-            pltpu.VMEM((2 * rows, 2 * width), x.dtype),
-            pltpu.VMEM((seqs, steps, 2 * width), jnp.bfloat16),
-        ],
+        scratch_shapes=[pltpu.VMEM((seqs, steps, 2 * width), jnp.bfloat16)],
         compiler_params=limit(x, *weights, *weights, *weights, *weights, *[out] * 32),
         name="project",
     )(meta, x, *weights, *mates)
 
 
-def cut_kernel(spans, meta_ref, *refs):
+def add_kernel(*refs):
+    total = refs[0][...].astype(jnp.float32)
+    for ref in refs[1:-1]:
+        total += ref[...].astype(jnp.float32)
+    refs[-1][...] = bf16(total)
+
+
+def add(parts):
+    out = jax.ShapeDtypeStruct(parts[0].shape, jnp.bfloat16)
+    return pl.pallas_call(
+        add_kernel,
+        in_specs=[vmem()] * len(parts),
+        out_specs=vmem(),
+        out_shape=out,
+        compiler_params=limit(out, out, out, *parts),
+        name="add",
+    )(*parts)
+
+
+def cut_kernel(spans, meta_ref, _, *refs):
     in_refs, out_refs = refs[:-spans], refs[-spans:]
     count = out_refs[0].shape[0]
     place = meta_ref[DEPTH] & (spans - 1)
@@ -150,17 +166,17 @@
         ref[...] = total.astype(ref.dtype)
 
 
-def cut(meta, parts, spans, first_type):
+def cut(meta, before, parts, spans):
     shape = (parts[0].shape[0] // spans,) + parts[0].shape[1:]
     return pl.pallas_call(
         functools.partial(cut_kernel, spans),
-        in_specs=[smem()] + [vmem()] * len(parts),
+        in_specs=[smem()] + [vmem()] * (1 + len(parts)),
         out_specs=[vmem()] * spans,
-        out_shape=[jax.ShapeDtypeStruct(shape, first_type)]
+        out_shape=[jax.ShapeDtypeStruct(shape, jnp.float32)]
         + [jax.ShapeDtypeStruct(shape, jnp.bfloat16)] * (spans - 1),
-        compiler_params=limit(*parts, *parts, *parts),
+        compiler_params=limit(before, *parts, *parts, *parts),
         name="cut",
-    )(meta, *parts)
+    )(meta, before, *parts)
 
 
 def own_group(meta_ref, groups):
@@ -225,7 +241,7 @@
 
 
 def pick_kernel(order, meta_ref, *refs):
-    in_refs, out_ref, places = refs[:-2], refs[-2], refs[-1]
+    in_refs, out_ref, places, sems = refs[:-3], refs[-3], refs[-2], refs[-1]
     groups = len(in_refs)
     count = out_ref.shape[0]
     slots = PROMPT + 2 * count
@@ -242,7 +258,10 @@
 
             @pl.when((source ^ own) == m)
             def _():
-                out_ref[r] = ref[...]
+                pltpu.make_async_copy(ref, out_ref.at[r], sems.at[r]).start()
+
+    for r in range(count):
+        pltpu.make_async_copy(in_refs[0], out_ref.at[r], sems.at[r]).wait()
 
 
 def pick(meta, blocks, order, count):
@@ -250,10 +269,13 @@
     return pl.pallas_call(
         functools.partial(pick_kernel, order),
         in_specs=[smem()] + [vmem()] * len(blocks),
-        out_specs=vmem(),
+        out_specs=pl.BlockSpec(memory_space=pl.ANY),
         out_shape=out,
-        scratch_shapes=[pltpu.SMEM((len(blocks) * count,), jnp.int32)],
-        compiler_params=limit(out, *blocks),
+        scratch_shapes=[
+            pltpu.SMEM((len(blocks) * count,), jnp.int32),
+            pltpu.SemaphoreType.DMA((count,)),
+        ],
+        compiler_params=limit(*blocks),
         name="pick_rows",
     )(meta, *blocks)
 
@@ -319,11 +341,8 @@
 
     parts = project(meta, jnp.concatenate(near, axis=0), weights, mates, dp, steps)
     far, near = ([send(parts[first + m], in_plane(m)) for m in (3, 2, 1, 0)] for first in (0, 4))
-    far = cut(meta, far, spans, jnp.bfloat16)
-    far = [send(a, to_depth(spans + m)) for m, a in enumerate(far)]
-    near = cut(meta, near, spans, jnp.float32)
-    near = [a if m == 0 else send(a, to_depth(m)) for m, a in enumerate(near)]
-    parts = near + far
+    near = cut(meta, stats, near + [send(add(far), to_depth(spans))], spans)
+    parts = [a if m == 0 else send(a, to_depth(m)) for m, a in enumerate(near)]
     sends = merge(meta, queries, o_cache, stats, parts, groups)
     order = sorted(range(1, groups), key=lambda m: -(m & (dp - 1)))
     blocks = [send(sends[m], to_group(m)) for m in order]

time: 65.4 us -> 64.4 us (0.985)
  starting transfers between devices: 40.7 us -> 36.4 us
  waiting for transfers between devices: 13.6 us -> 17.7 us
  Pallas kernels: 9.55 us -> 8.7 us
    ppermute x24 -> x23, starting transfers between devices: 40.7 us -> 36.4 us  [send(): return lax.ppermute(a, everyone, [(flat(*d), target(*d)) for d in devices])]
    ppermute x24 -> x23, waiting for transfers between devices: 13.6 us -> 17.7 us  [send(): return lax.ppermute(a, everyone, [(flat(*d), target(*d)) for d in devices])]
  transfers between devices with their start and end apart: 24 -> 23, of which waited for: 10 -> 11; matrix products, arithmetic and copies ran while one was open for 2% -> 2% of each run, Pallas kernels for 7% -> 5%
where the time goes in v2:
time: 64.4 us; the launch traced here: 64.2 us
  starting transfers between devices  36.4 us (57%)
  waiting for transfers between devices  17.7 us (27%)
  Pallas kernels  8.7 us (14%)
  local copies, waits for them, and re-layouts  1.16 us (2%)
    ppermute x23, starting transfers between devices, send(): return lax.ppermute(a, everyone, [(flat(*d), target(*d)) for d in devices])  36.4 us
    ppermute x23, waiting for transfers between devices, send(): return lax.ppermute(a, everyone, [(flat(*d), target(*d)) for d in devices])  17.7 us
    pallas_call x1, Pallas kernels, cache_attention(): pl.pallas_call(cache_kernel, grid_spec=pltpu.PrefetchScalarGridSpec(num_s...  3.27 us
    pallas_call x1, Pallas kernels, merge(): pl.pallas_call(functools.partial(merge_kernel, groups), in_specs=[smem()]...  2 us
    pallas_call x1, Pallas kernels, project(): pl.pallas_call(functools.partial(project_kernel, dp), in_specs=[smem()] +...  1.4 us
    pallas_call x1, Pallas kernels, pick(): pl.pallas_call(functools.partial(pick_kernel, order), in_specs=[smem()] +...  1.34 us
  transfers between devices with their start and end apart: 23, of which 11 were waited for; matrix products, arithmetic and copies ran while one was open for 2% of the time, Pallas kernels for 5%

profile of v2, /device:TPU:0, one launch (start us, length us, event | category | flops | bytes accessed | tf_op | source)
XLA Modules:
  0.0 64.2 jit_solution(976196014489065771)
XLA Ops:
  0.5 1.1 %constant_dynamic-slice_fusion.3 = (bf16[64,512]{1,0:T(8,128)(2,1)S(1)}, bf16[64,512]{1,0:T(8,128)(2,1)S(1)}, bf16[64,512]{1,0:T(8,128)(2,1)S(1)}, bf16[64,512]{1,0:T(8,128)(2,1)S(1)}) fusion(bf16[64,2048]{1,0:T(8,128)(2,1)} %bitcast.5, s32[]{:T(128)S(6)} %select_n.12, s32[]{:T(128)S(6)} %select_n.15, s32[]{:T(128)S(6)} %select_n.14, s32[]{:T(128)S(6)} %select_n.13), kind=kLoop, calls=%fused_computation.4 | loop fusion | bytes 524304 | tf_op jit(solution)/shard_map/dynamic_slice | solution.py:335
  1.6 0.7 %collective-permute-start = (bf16[64,512]{1,0:T(8,128)(2,1)S(1)}, bf16[64,512]{1,0:T(8,128)(2,1)S(1)}, u32[]{:S(2)}, u32[]{:S(2)}) collective-permute-start(bf16[64,512]{1,0:T(8,128)(2,1)S(1)} %get-tuple-element.45), channel_id=1, source_target_pairs={{0,0},{1,8},{2,16},{3,24},{4,2},{5,10},{6,18},{7,26},{8,4},{9,12},... | collective-permute-start | bytes 196616 | tf_op jit(solution)/shard_map/ppermute | solution.py:309
  2.3 8.5 %collective-permute-start.3 = (bf16[64,512]{1,0:T(8,128)(2,1)S(1)}, bf16[64,512]{1,0:T(8,128)(2,1)S(1)}, u32[]{:S(2)}, u32[]{:S(2)}) collective-permute-start(bf16[64,512]{1,0:T(8,128)(2,1)S(1)} %get-tuple-element.46), channel_id=1, source_target_pairs={{0,6},{1,14},{2,22},{3,30},{4,4},{5,12},{6,20},{7,28},{8,2},{9,10}... | collective-permute-start | bytes 196616 | tf_op jit(solution)/shard_map/ppermute | solution.py:309
  10.9 2.8 %collective-permute-start.1 = (bf16[64,512]{1,0:T(8,128)(2,1)S(1)}, bf16[64,512]{1,0:T(8,128)(2,1)S(1)}, u32[]{:S(2)}, u32[]{:S(2)}) collective-permute-start(bf16[64,512]{1,0:T(8,128)(2,1)S(1)} %get-tuple-element.48), channel_id=1, source_target_pairs={{0,2},{1,10},{2,18},{3,26},{4,0},{5,8},{6,16},{7,24},{8,6},{9,14},... | collective-permute-start | bytes 196616 | tf_op jit(solution)/shard_map/ppermute | solution.py:309
  13.8 0.7 %collective-permute-done.3 = bf16[64,512]{1,0:T(8,128)(2,1)S(1)} collective-permute-done((bf16[64,512]{1,0:T(8,128)(2,1)S(1)}, bf16[64,512]{1,0:T(8,128)(2,1)S(1)}, u32[]{:S(2)}, u32[]{:S(2)}) %collective-permute-start.3) | collective-permute-done | bytes 65568 | tf_op jit(solution)/shard_map/ppermute | solution.py:309
  14.4 3.0 %collective-permute-done.2 = bf16[64,512]{1,0:T(8,128)(2,1)S(1)} collective-permute-done((bf16[64,512]{1,0:T(8,128)(2,1)S(1)}, bf16[64,512]{1,0:T(8,128)(2,1)S(1)}, u32[]{:S(2)}, u32[]{:S(2)}) %collective-permute-start.2) | collective-permute-done | bytes 65568 | tf_op jit(solution)/shard_map/ppermute | solution.py:309
  17.5 1.4 %project.1 = (bf16[8,16,512]{2,1,0:T(8,128)(2,1)S(1)}, bf16[8,16,512]{2,1,0:T(8,128)(2,1)S(1)}, bf16[8,16,512]{2,1,0:T(8,128)(2,1)S(1)}, bf16[8,16,512]{2,1,0:T(...) custom-call(s32[44]{0:T(128)S(1)} %concatenate.6.meta_ref, ...), custom_call_target="tpu_custom_call" | custom-call | tf_op jit(solution)/shard_map/project/pallas_call | solution.py:127
  18.9 3.4 %collective-permute-start.10 = (bf16[8,16,512]{2,1,0:T(8,128)(2,1)S(1)}, bf16[8,16,512]{2,1,0:T(8,128)(2,1)S(1)}, u32[]{:S(2)}, u32[]{:S(2)}) collective-permute-start(bf16[8,16,512]{2,1,0:T(8,128)(2,1)S(1)} %get-tuple-element.31), channel_id=1, source_target_pairs={{0,3},{1,19},{2,1},{3,17},{4,7},{5,23},{6,5},{7,21},{8,11},{9,27},... | collective-permute-start | bytes 393224 | tf_op jit(solution)/shard_map/ppermute | solution.py:309
  23.6 4.5 %collective-permute-start.6 = (bf16[8,16,512]{2,1,0:T(8,128)(2,1)S(1)}, bf16[8,16,512]{2,1,0:T(8,128)(2,1)S(1)}, u32[]{:S(2)}, u32[]{:S(2)}) collective-permute-start(bf16[8,16,512]{2,1,0:T(8,128)(2,1)S(1)} %get-tuple-element.27), channel_id=1, source_target_pairs={{0,3},{1,19},{2,1},{3,17},{4,7},{5,23},{6,5},{7,21},{8,11},{9,27},... | collective-permute-start | bytes 393224 | tf_op jit(solution)/shard_map/ppermute | solution.py:309
  28.7 0.8 %collective-permute-done.11.refs_1_ = bf16[8,16,512]{2,1,0:T(8,128)(2,1)S(1)} collective-permute-done((bf16[8,16,512]{2,1,0:T(8,128)(2,1)S(1)}, bf16[8,16,512]{2,1,0:T(8,128)(2,1)S(1)}, u32[]{:S(2)}, u32[]{:S(2)}) %collective-permute-start.11) | collective-permute-done | bytes 131104 | tf_op jit(solution)/shard_map/ppermute | solution.py:309
  29.5 0.8 %collective-permute-start.9 = (bf16[8,16,512]{2,1,0:T(8,128)(2,1)S(1)}, bf16[8,16,512]{2,1,0:T(8,128)(2,1)S(1)}, u32[]{:S(2)}, u32[]{:S(2)}) collective-permute-start(bf16[8,16,512]{2,1,0:T(8,128)(2,1)S(1)} %get-tuple-element.30), channel_id=1, source_target_pairs={{0,0},{1,16},{2,2},{3,18},{4,4},{5,20},{6,6},{7,22},{8,8},{9,24},{... | collective-permute-start | bytes 393224 | tf_op jit(solution)/shard_map/ppermute | solution.py:309
  30.4 2.0 %collective-permute-start.14 = (bf16[8,16,512]{2,1,0:T(8,128)(2,1)S(1)}, bf16[8,16,512]{2,1,0:T(8,128)(2,1)S(1)}, u32[]{:S(2)}, u32[]{:S(2)}) collective-permute-start(bf16[8,16,512]{2,1,0:T(8,128)(2,1)S(1)} %add.17), channel_id=1, source_target_pairs={{0,8},{1,9},{2,10},{3,11},{4,12},{5,13},{6,14},{7,15},{8,0},{9,1},... | collective-permute-start | bytes 393224 | tf_op jit(solution)/shard_map/ppermute | solution.py:309
  32.4 3.3 %cache_attention.1 = (f32[4,2,128,128]{3,2,1,0:T(8,128)S(1)}, f32[4,2,128,128]{3,2,1,0:T(8,128)S(1)}) custom-call(s32[44]{0:T(128)S(1)} %concatenate.6.meta_ref, bf16[4,16,2048]{2,1,0:T(8,128)(2,1)S(1)} %copy-done.2, bf16[4,512,256]{2,1,0:T(8,128)(2,1)S(1)} %copy-done, bf16[4,512,256]{2,1,0:T(8,128)(2,1)S(1)} %copy-done.1), custom_call_target="tpu_custom_call" | custom-call | tf_op jit(solution)/shard_map/cache_attention/pallas_call | solution.py:76
  35.8 3.7 %collective-permute-done.14.refs_4_ = bf16[8,16,512]{2,1,0:T(8,128)(2,1)S(1)} collective-permute-done((bf16[8,16,512]{2,1,0:T(8,128)(2,1)S(1)}, bf16[8,16,512]{2,1,0:T(8,128)(2,1)S(1)}, u32[]{:S(2)}, u32[]{:S(2)}) %collective-permute-start.14) | collective-permute-done | bytes 131104 | tf_op jit(solution)/shard_map/ppermute | solution.py:309
  40.2 4.9 %collective-permute-done.15.refs_1_ = bf16[4,16,512]{2,1,0:T(8,128)(2,1)S(1)} collective-permute-done((bf16[4,16,512]{2,1,0:T(8,128)(2,1)S(1)}, bf16[4,16,512]{2,1,0:T(8,128)(2,1)S(1)}, u32[]{:S(2)}, u32[]{:S(2)}) %collective-permute-start.15) | collective-permute-done | bytes 65568 | tf_op jit(solution)/shard_map/ppermute | solution.py:309
  45.1 2.0 %merge_fresh.1 = (bf16[16,2048]{1,0:T(8,128)(2,1)S(1)}, bf16[16,2048]{1,0:T(8,128)(2,1)S(1)}, bf16[16,2048]{1,0:T(8,128)(2,1)S(1)}, bf16[16,2048]{1,0:T(8,128)(2...) custom-call(s32[44]{0:T(128)S(1)} %concatenate.6.meta_ref, ...), custom_call_target="tpu_custom_call" | custom-call | tf_op jit(solution)/shard_map/merge_fresh/pallas_call | solution.py:232
  47.2 5.3 %collective-permute-start.17 = (bf16[16,2048]{1,0:T(8,128)(2,1)S(1)}, bf16[16,2048]{1,0:T(8,128)(2,1)S(1)}, u32[]{:S(2)}, u32[]{:S(2)}) collective-permute-start(bf16[16,2048]{1,0:T(8,128)(2,1)S(1)} %get-tuple-element.38), channel_id=1, source_target_pairs={{0,28},{1,29},{2,30},{3,31},{4,24},{5,25},{6,26},{7,27},{8,20},{9,... | collective-permute-start | bytes 196616 | tf_op jit(solution)/shard_map/ppermute | solution.py:309
  52.5 2.3 %collective-permute-start.19 = (bf16[16,2048]{1,0:T(8,128)(2,1)S(1)}, bf16[16,2048]{1,0:T(8,128)(2,1)S(1)}, u32[]{:S(2)}, u32[]{:S(2)}) collective-permute-start(bf16[16,2048]{1,0:T(8,128)(2,1)S(1)} %get-tuple-element.40), channel_id=1, source_target_pairs={{0,24},{1,25},{2,26},{3,27},{4,28},{5,29},{6,30},{7,31},{8,16},{9,... | collective-permute-start | bytes 196616 | tf_op jit(solution)/shard_map/ppermute | solution.py:309
  54.8 3.5 %collective-permute-start.21 = (bf16[16,2048]{1,0:T(8,128)(2,1)S(1)}, bf16[16,2048]{1,0:T(8,128)(2,1)S(1)}, u32[]{:S(2)}, u32[]{:S(2)}) collective-permute-start(bf16[16,2048]{1,0:T(8,128)(2,1)S(1)} %get-tuple-element.42), channel_id=1, source_target_pairs={{0,20},{1,21},{2,22},{3,23},{4,16},{5,17},{6,18},{7,19},{8,28},{9,... | collective-permute-start | bytes 196616 | tf_op jit(solution)/shard_map/ppermute | solution.py:309
  58.4 1.4 %collective-permute-done.18.refs_2_ = bf16[16,2048]{1,0:T(8,128)(2,1)S(1)} collective-permute-done((bf16[16,2048]{1,0:T(8,128)(2,1)S(1)}, bf16[16,2048]{1,0:T(8,128)(2,1)S(1)}, u32[]{:S(2)}, u32[]{:S(2)}) %collective-permute-start.18) | collective-permute-done | bytes 65568 | tf_op jit(solution)/shard_map/ppermute | solution.py:309
  59.8 1.1 %collective-permute-done.19.refs_3_ = bf16[16,2048]{1,0:T(8,128)(2,1)S(1)} collective-permute-done((bf16[16,2048]{1,0:T(8,128)(2,1)S(1)}, bf16[16,2048]{1,0:T(8,128)(2,1)S(1)}, u32[]{:S(2)}, u32[]{:S(2)}) %collective-permute-start.19) | collective-permute-done | bytes 65568 | tf_op jit(solution)/shard_map/ppermute | solution.py:309
  60.9 1.3 %collective-permute-done.21.refs_5_ = bf16[16,2048]{1,0:T(8,128)(2,1)S(1)} collective-permute-done((bf16[16,2048]{1,0:T(8,128)(2,1)S(1)}, bf16[16,2048]{1,0:T(8,128)(2,1)S(1)}, u32[]{:S(2)}, u32[]{:S(2)}) %collective-permute-start.21) | collective-permute-done | bytes 65568 | tf_op jit(solution)/shard_map/ppermute | solution.py:309
  62.2 0.7 %collective-permute-done.22.refs_6_ = bf16[16,2048]{1,0:T(8,128)(2,1)S(1)} collective-permute-done((bf16[16,2048]{1,0:T(8,128)(2,1)S(1)}, bf16[16,2048]{1,0:T(8,128)(2,1)S(1)}, u32[]{:S(2)}, u32[]{:S(2)}) %collective-permute-start.22) | collective-permute-done | bytes 65568 | tf_op jit(solution)/shard_map/ppermute | solution.py:309
  62.9 1.3 %pick_rows.1 = bf16[4,16,2048]{2,1,0:T(8,128)(2,1)} custom-call(s32[44]{0:T(128)S(1)} %concatenate.6.meta_ref, bf16[16,2048]{1,0:T(8,128)(2,1)S(1)} %collective-permute-done.16.refs_0_, bf16[16,2048]{1,0:T(8,128)(2,1)S(1)} %collective-permute-done.17.refs_1_, bf16[16,2048]{1,0:T(8,128)(2,1)S(1)} %collective-permute-done.18.refs_2_, ...), custom_call_target="tpu_custom_call" | custom-call | tf_op jit(solution)/shard_map/pick_rows/pallas_call | solution.py:269
  (47 shorter events, 3.7 us)
Async XLA Ops:
  0.0 17.5 %collective-permute-start.4 = (bf16[256,1024]{1,0:T(8,128)(2,1)}, bf16[256,1024]{1,0:T(8,128)(2,1)S(1)}, u32[]{:S(2)}, u32[]{:S(2)}) collective-permute-start(bf16[256,1024]{1,0:T(8,128)(2,1)} %key_ref.1), channel_id=1, source_target_pairs={{0,1},{1,0},{2,3},{3,2},{4,5},{5,4},{6,7},{7,6},{8,9},{9,8},{10,11... | collective-permute-start | bytes 1572872 | tf_op jit(solution)/shard_map/ppermute | solution.py:309
  0.5 17.0 %collective-permute-start.5 = (bf16[256,1024]{1,0:T(8,128)(2,1)}, bf16[256,1024]{1,0:T(8,128)(2,1)S(1)}, u32[]{:S(2)}, u32[]{:S(2)}) collective-permute-start(bf16[256,1024]{1,0:T(8,128)(2,1)} %value_ref.1), channel_id=1, source_target_pairs={{0,1},{1,0},{2,3},{3,2},{4,5},{5,4},{6,7},{7,6},{8,9},{9,8},{10,11... | collective-permute-start | bytes 1572872 | tf_op jit(solution)/shard_map/ppermute | solution.py:309
  0.5 17.0 %copy-start.4 = (bf16[256,1024]{1,0:T(8,128)(2,1)S(1)}, bf16[256,1024]{1,0:T(8,128)(2,1)}, u32[]{:S(2)}) copy-start(bf16[256,1024]{1,0:T(8,128)(2,1)} %value_ref.1) | copy-start | bytes 1572868
  1.6 9.3 %collective-permute-start = (bf16[64,512]{1,0:T(8,128)(2,1)S(1)}, bf16[64,512]{1,0:T(8,128)(2,1)S(1)}, u32[]{:S(2)}, u32[]{:S(2)}) collective-permute-start(bf16[64,512]{1,0:T(8,128)(2,1)S(1)} %get-tuple-element.45), channel_id=1, source_target_pairs={{0,0},{1,8},{2,16},{3,24},{4,2},{5,10},{6,18},{7,26},{8,4},{9,12},... | collective-permute-start | bytes 196616 | tf_op jit(solution)/shard_map/ppermute | solution.py:309
  2.3 12.2 %collective-permute-start.3 = (bf16[64,512]{1,0:T(8,128)(2,1)S(1)}, bf16[64,512]{1,0:T(8,128)(2,1)S(1)}, u32[]{:S(2)}, u32[]{:S(2)}) collective-permute-start(bf16[64,512]{1,0:T(8,128)(2,1)S(1)} %get-tuple-element.46), channel_id=1, source_target_pairs={{0,6},{1,14},{2,22},{3,30},{4,4},{5,12},{6,20},{7,28},{8,2},{9,10}... | collective-permute-start | bytes 196616 | tf_op jit(solution)/shard_map/ppermute | solution.py:309
  10.8 6.6 %collective-permute-start.2 = (bf16[64,512]{1,0:T(8,128)(2,1)S(1)}, bf16[64,512]{1,0:T(8,128)(2,1)S(1)}, u32[]{:S(2)}, u32[]{:S(2)}) collective-permute-start(bf16[64,512]{1,0:T(8,128)(2,1)S(1)} %get-tuple-element.47), channel_id=1, source_target_pairs={{0,4},{1,12},{2,20},{3,28},{4,6},{5,14},{6,22},{7,30},{8,0},{9,8},... | collective-permute-start | bytes 196616 | tf_op jit(solution)/shard_map/ppermute | solution.py:309
  10.9 6.5 %collective-permute-start.1 = (bf16[64,512]{1,0:T(8,128)(2,1)S(1)}, bf16[64,512]{1,0:T(8,128)(2,1)S(1)}, u32[]{:S(2)}, u32[]{:S(2)}) collective-permute-start(bf16[64,512]{1,0:T(8,128)(2,1)S(1)} %get-tuple-element.48), channel_id=1, source_target_pairs={{0,2},{1,10},{2,18},{3,26},{4,0},{5,8},{6,16},{7,24},{8,6},{9,14},... | collective-permute-start | bytes 196616 | tf_op jit(solution)/shard_map/ppermute | solution.py:309
  18.9 9.2 %collective-permute-start.10 = (bf16[8,16,512]{2,1,0:T(8,128)(2,1)S(1)}, bf16[8,16,512]{2,1,0:T(8,128)(2,1)S(1)}, u32[]{:S(2)}, u32[]{:S(2)}) collective-permute-start(bf16[8,16,512]{2,1,0:T(8,128)(2,1)S(1)} %get-tuple-element.31), channel_id=1, source_target_pairs={{0,3},{1,19},{2,1},{3,17},{4,7},{5,23},{6,5},{7,21},{8,11},{9,27},... | collective-permute-start | bytes 393224 | tf_op jit(solution)/shard_map/ppermute | solution.py:309
  22.4 7.2 %collective-permute-start.11 = (bf16[8,16,512]{2,1,0:T(8,128)(2,1)S(1)}, bf16[8,16,512]{2,1,0:T(8,128)(2,1)S(1)}, u32[]{:S(2)}, u32[]{:S(2)}) collective-permute-start(bf16[8,16,512]{2,1,0:T(8,128)(2,1)S(1)} %get-tuple-element.32), channel_id=1, source_target_pairs={{0,2},{1,18},{2,0},{3,16},{4,6},{5,22},{6,4},{7,20},{8,10},{9,26},... | collective-permute-start | bytes 393224 | tf_op jit(solution)/shard_map/ppermute | solution.py:309
  22.9 6.6 %collective-permute-start.12 = (bf16[8,16,512]{2,1,0:T(8,128)(2,1)S(1)}, bf16[8,16,512]{2,1,0:T(8,128)(2,1)S(1)}, u32[]{:S(2)}, u32[]{:S(2)}) collective-permute-start(bf16[8,16,512]{2,1,0:T(8,128)(2,1)S(1)} %get-tuple-element.33), channel_id=1, source_target_pairs={{0,1},{1,17},{2,3},{3,19},{4,5},{5,21},{6,7},{7,23},{8,9},{9,25},{... | collective-permute-start | bytes 393224 | tf_op jit(solution)/shard_map/ppermute | solution.py:309
  23.0 7.4 %collective-permute-start.13 = (bf16[8,16,512]{2,1,0:T(8,128)(2,1)S(1)}, bf16[8,16,512]{2,1,0:T(8,128)(2,1)S(1)}, u32[]{:S(2)}, u32[]{:S(2)}) collective-permute-start(bf16[8,16,512]{2,1,0:T(8,128)(2,1)S(1)} %get-tuple-element.34), channel_id=1, source_target_pairs={{0,0},{1,16},{2,2},{3,18},{4,4},{5,20},{6,6},{7,22},{8,8},{9,24},{... | collective-permute-start | bytes 393224 | tf_op jit(solution)/shard_map/ppermute | solution.py:309
  23.6 12.0 %collective-permute-start.6 = (bf16[8,16,512]{2,1,0:T(8,128)(2,1)S(1)}, bf16[8,16,512]{2,1,0:T(8,128)(2,1)S(1)}, u32[]{:S(2)}, u32[]{:S(2)}) collective-permute-start(bf16[8,16,512]{2,1,0:T(8,128)(2,1)S(1)} %get-tuple-element.27), channel_id=1, source_target_pairs={{0,3},{1,19},{2,1},{3,17},{4,7},{5,23},{6,5},{7,21},{8,11},{9,27},... | collective-permute-start | bytes 393224 | tf_op jit(solution)/shard_map/ppermute | solution.py:309
  28.1 7.7 %collective-permute-start.7 = (bf16[8,16,512]{2,1,0:T(8,128)(2,1)S(1)}, bf16[8,16,512]{2,1,0:T(8,128)(2,1)S(1)}, u32[]{:S(2)}, u32[]{:S(2)}) collective-permute-start(bf16[8,16,512]{2,1,0:T(8,128)(2,1)S(1)} %get-tuple-element.28), channel_id=1, source_target_pairs={{0,2},{1,18},{2,0},{3,16},{4,6},{5,22},{6,4},{7,20},{8,10},{9,26},... | collective-permute-start | bytes 393224 | tf_op jit(solution)/shard_map/ppermute | solution.py:309
  29.5 6.3 %collective-permute-start.8 = (bf16[8,16,512]{2,1,0:T(8,128)(2,1)S(1)}, bf16[8,16,512]{2,1,0:T(8,128)(2,1)S(1)}, u32[]{:S(2)}, u32[]{:S(2)}) collective-permute-start(bf16[8,16,512]{2,1,0:T(8,128)(2,1)S(1)} %get-tuple-element.29), channel_id=1, source_target_pairs={{0,1},{1,17},{2,3},{3,19},{4,5},{5,21},{6,7},{7,23},{8,9},{9,25},{... | collective-permute-start | bytes 393224 | tf_op jit(solution)/shard_map/ppermute | solution.py:309
  29.5 6.3 %collective-permute-start.9 = (bf16[8,16,512]{2,1,0:T(8,128)(2,1)S(1)}, bf16[8,16,512]{2,1,0:T(8,128)(2,1)S(1)}, u32[]{:S(2)}, u32[]{:S(2)}) collective-permute-start(bf16[8,16,512]{2,1,0:T(8,128)(2,1)S(1)} %get-tuple-element.30), channel_id=1, source_target_pairs={{0,0},{1,16},{2,2},{3,18},{4,4},{5,20},{6,6},{7,22},{8,8},{9,24},{... | collective-permute-start | bytes 393224 | tf_op jit(solution)/shard_map/ppermute | solution.py:309
  30.4 9.1 %collective-permute-start.14 = (bf16[8,16,512]{2,1,0:T(8,128)(2,1)S(1)}, bf16[8,16,512]{2,1,0:T(8,128)(2,1)S(1)}, u32[]{:S(2)}, u32[]{:S(2)}) collective-permute-start(bf16[8,16,512]{2,1,0:T(8,128)(2,1)S(1)} %add.17), channel_id=1, source_target_pairs={{0,8},{1,9},{2,10},{3,11},{4,12},{5,13},{6,14},{7,15},{8,0},{9,1},... | collective-permute-start | bytes 393224 | tf_op jit(solution)/shard_map/ppermute | solution.py:309
  40.1 4.9 %collective-permute-start.15 = (bf16[4,16,512]{2,1,0:T(8,128)(2,1)S(1)}, bf16[4,16,512]{2,1,0:T(8,128)(2,1)S(1)}, u32[]{:S(2)}, u32[]{:S(2)}) collective-permute-start(bf16[4,16,512]{2,1,0:T(8,128)(2,1)S(1)} %get-tuple-element.36), channel_id=1, source_target_pairs={{0,4},{1,5},{2,6},{3,7},{4,0},{5,1},{6,2},{7,3},{8,12},{9,13},{10,... | collective-permute-start | bytes 196616 | tf_op jit(solution)/shard_map/ppermute | solution.py:309
  47.1 7.7 %collective-permute-start.16 = (bf16[16,2048]{1,0:T(8,128)(2,1)S(1)}, bf16[16,2048]{1,0:T(8,128)(2,1)S(1)}, u32[]{:S(2)}, u32[]{:S(2)}) collective-permute-start(bf16[16,2048]{1,0:T(8,128)(2,1)S(1)} %get-tuple-element.37), channel_id=1, source_target_pairs={{0,12},{1,13},{2,14},{3,15},{4,8},{5,9},{6,10},{7,11},{8,4},{9,5},... | collective-permute-start | bytes 196616 | tf_op jit(solution)/shard_map/ppermute | solution.py:309
  47.2 11.2 %collective-permute-start.17 = (bf16[16,2048]{1,0:T(8,128)(2,1)S(1)}, bf16[16,2048]{1,0:T(8,128)(2,1)S(1)}, u32[]{:S(2)}, u32[]{:S(2)}) collective-permute-start(bf16[16,2048]{1,0:T(8,128)(2,1)S(1)} %get-tuple-element.38), channel_id=1, source_target_pairs={{0,28},{1,29},{2,30},{3,31},{4,24},{5,25},{6,26},{7,27},{8,20},{9,... | collective-permute-start | bytes 196616 | tf_op jit(solution)/shard_map/ppermute | solution.py:309
  52.5 7.3 %collective-permute-start.18 = (bf16[16,2048]{1,0:T(8,128)(2,1)S(1)}, bf16[16,2048]{1,0:T(8,128)(2,1)S(1)}, u32[]{:S(2)}, u32[]{:S(2)}) collective-permute-start(bf16[16,2048]{1,0:T(8,128)(2,1)S(1)} %get-tuple-element.39), channel_id=1, source_target_pairs={{0,8},{1,9},{2,10},{3,11},{4,12},{5,13},{6,14},{7,15},{8,0},{9,1},... | collective-permute-start | bytes 196616 | tf_op jit(solution)/shard_map/ppermute | solution.py:309
  52.5 8.4 %collective-permute-start.19 = (bf16[16,2048]{1,0:T(8,128)(2,1)S(1)}, bf16[16,2048]{1,0:T(8,128)(2,1)S(1)}, u32[]{:S(2)}, u32[]{:S(2)}) collective-permute-start(bf16[16,2048]{1,0:T(8,128)(2,1)S(1)} %get-tuple-element.40), channel_id=1, source_target_pairs={{0,24},{1,25},{2,26},{3,27},{4,28},{5,29},{6,30},{7,31},{8,16},{9,... | collective-permute-start | bytes 196616 | tf_op jit(solution)/shard_map/ppermute | solution.py:309
  54.8 6.1 %collective-permute-start.20 = (bf16[16,2048]{1,0:T(8,128)(2,1)S(1)}, bf16[16,2048]{1,0:T(8,128)(2,1)S(1)}, u32[]{:S(2)}, u32[]{:S(2)}) collective-permute-start(bf16[16,2048]{1,0:T(8,128)(2,1)S(1)} %get-tuple-element.41), channel_id=1, source_target_pairs={{0,4},{1,5},{2,6},{3,7},{4,0},{5,1},{6,2},{7,3},{8,12},{9,13},{10,... | collective-permute-start | bytes 196616 | tf_op jit(solution)/shard_map/ppermute | solution.py:309
  54.8 7.4 %collective-permute-start.21 = (bf16[16,2048]{1,0:T(8,128)(2,1)S(1)}, bf16[16,2048]{1,0:T(8,128)(2,1)S(1)}, u32[]{:S(2)}, u32[]{:S(2)}) collective-permute-start(bf16[16,2048]{1,0:T(8,128)(2,1)S(1)} %get-tuple-element.42), channel_id=1, source_target_pairs={{0,20},{1,21},{2,22},{3,23},{4,16},{5,17},{6,18},{7,19},{8,28},{9,... | collective-permute-start | bytes 196616 | tf_op jit(solution)/shard_map/ppermute | solution.py:309
  58.3 4.6 %collective-permute-start.22 = (bf16[16,2048]{1,0:T(8,128)(2,1)S(1)}, bf16[16,2048]{1,0:T(8,128)(2,1)S(1)}, u32[]{:S(2)}, u32[]{:S(2)}) collective-permute-start(bf16[16,2048]{1,0:T(8,128)(2,1)S(1)} %get-tuple-element.43), channel_id=1, source_target_pairs={{0,16},{1,17},{2,18},{3,19},{4,20},{5,21},{6,22},{7,23},{8,24},{9,... | collective-permute-start | bytes 196616 | tf_op jit(solution)/shard_map/ppermute | solution.py:309
  (7 other events, 89.2 us)

commit v3 on v2

--- a/solution.py
+++ b/solution.py
@@ -10,7 +10,7 @@
 GROUP = 8
 SCALE = HEAD ** (-0.5)
 MIB = 1 << 20
-CORE, HALF, SECT, DEPTH, PROMPT = range(5)
+SECT, DEPTH, PROMPT = range(3)
 
 
 def vmem():
@@ -45,7 +45,21 @@
     return a.astype(jnp.bfloat16)
 
 
-def cache_kernel(meta_ref, q_ref, k_ref, v_ref, o_ref, stat_ref):
+def cache_kernel(groups, meta_ref, q_ref, k_ref, v_ref, o_ref, stat_ref, source_ref, places):
+    count = source_ref.shape[0]
+
+    @pl.when(pl.program_id(0) == 0)
+    def _():
+        def note(s, carry):
+            places[meta_ref[PROMPT + 2 * count + s]] = s
+            return carry
+
+        lax.fori_loop(0, groups * count, note, 0, unroll=8)
+        own = own_group(meta_ref, groups)
+        for r in range(count):
+            source = lax.div(places[own * count + r], count) ^ own
+            source_ref[r] = bf16(jnp.full(source_ref.shape[1:], source.astype(jnp.float32)))
+
     slots, width = k_ref.shape[1:]
     steps = q_ref.shape[1]
     rows = steps * GROUP
@@ -62,7 +76,7 @@
         stat_ref[0, kv] = jnp.where(lane == 0, top, total)
 
 
-def cache_attention(meta, queries, key_cache, value_cache):
+def cache_attention(meta, queries, key_cache, value_cache, groups):
     count, steps, qw = queries.shape
     slots, width = key_cache.shape[1:]
     shape = (count, width // HEAD, steps * GROUP, HEAD)
@@ -74,7 +88,7 @@
         return (n, 0, 0, 0)
 
     return pl.pallas_call(
-        cache_kernel,
+        functools.partial(cache_kernel, groups),
         grid_spec=pltpu.PrefetchScalarGridSpec(
             num_scalar_prefetch=1,
             grid=(count,),
@@ -83,23 +97,27 @@
                 pl.BlockSpec((1, slots, width), one),
                 pl.BlockSpec((1, slots, width), one),
             ],
-            out_specs=[pl.BlockSpec((1,) + shape[1:], one4)] * 2,
+            out_specs=[pl.BlockSpec((1,) + shape[1:], one4)] * 2
+            + [pl.BlockSpec((count, steps, HEAD), lambda n, meta: (0, 0, 0))],
+            scratch_shapes=[pltpu.SMEM((groups * count,), jnp.int32)],
         ),
-        out_shape=[jax.ShapeDtypeStruct(shape, jnp.float32)] * 2,
+        out_shape=[jax.ShapeDtypeStruct(shape, jnp.float32)] * 2
+        + [jax.ShapeDtypeStruct((count, steps, HEAD), jnp.bfloat16)],
         compiler_params=pltpu.CompilerParams(vmem_limit_bytes=8 * MIB),
         name="cache_attention",
     )(meta, queries, key_cache, value_cache)
 
 
-def project_kernel(dp, meta_ref, x_ref, key_ref, value_ref, key_mate_ref, value_mate_ref, *refs):
+def project_kernel(dp, x_ref, key_ref, value_ref, key_mate_ref, value_mate_ref, *refs):
     out_refs, held = refs[:8], refs[8]
     seqs, steps, width = held.shape
     count = seqs // dp
     rows, kind_width = key_ref.shape
-    core, half = meta_ref[CORE], meta_ref[HALF]
+    core, half = lax.axis_index("tp") & 1, lax.axis_index("tp") >> 1
+    sect, depth = lax.axis_index("sect"), lax.axis_index("dp")
     first, second = x_ref[:, :rows], x_ref[:, rows:]
     own, mate = jnp.where(core == 0, first, second), jnp.where(core == 0, second, first)
-    place = (meta_ref[DEPTH] & (dp // 2 - 1)) * 2 + half
+    place = (depth & (dp // 2 - 1)) * 2 + half
     chunk = 4 * count * steps
     for kind, refs in enumerate(((key_ref, key_mate_ref), (value_ref, value_mate_ref))):
         cols = slice(kind * kind_width, (kind + 1) * kind_width)
@@ -111,28 +129,28 @@
                 i = (m % 4) * count + n
                 held[(place ^ m) * count + n, :, cols] = sums[i * steps : (i + 1) * steps]
     cw = width // 8
-    own_half = (meta_ref[DEPTH] >= dp // 2).astype(jnp.int32)
+    own_half = (depth >= dp // 2).astype(jnp.int32)
     for i, ref in enumerate(out_refs):
-        t = (half ^ ((i >> 1) & 1)) * 2 + (meta_ref[SECT] ^ (i & 1))
+        t = (half ^ ((i >> 1) & 1)) * 2 + (sect ^ (i & 1))
         group = pl.ds((own_half ^ (1 - (i >> 2))) * (seqs // 2), seqs // 2)
         for kind in range(2):
             cols = pl.ds(pl.multiple_of(kind * kind_width + t * cw, cw), cw)
             ref[:, :, kind * cw : (kind + 1) * cw] = held[group, :, cols]
 
 
-def project(meta, x, weights, mates, dp, steps):
+def project(x, weights, mates, dp, steps):
     seqs = x.shape[0] // steps
     rows, width = weights[0].shape
     out = jax.ShapeDtypeStruct((seqs // 2, steps, width // 2), jnp.bfloat16)
     return pl.pallas_call(
         functools.partial(project_kernel, dp),
-        in_specs=[smem()] + [vmem()] * 5,
+        in_specs=[vmem()] * 5,
         out_specs=[vmem()] * 8,
         out_shape=[out] * 8,
         scratch_shapes=[pltpu.VMEM((seqs, steps, 2 * width), jnp.bfloat16)],
         compiler_params=limit(x, *weights, *weights, *weights, *weights, *[out] * 32),
         name="project",
-    )(meta, x, *weights, *mates)
+    )(x, *weights, *mates)
 
 
 def add_kernel(*refs):
@@ -154,10 +172,10 @@
     )(*parts)
 
 
-def cut_kernel(spans, meta_ref, _, *refs):
+def cut_kernel(spans, _, *refs):
     in_refs, out_refs = refs[:-spans], refs[-spans:]
     count = out_refs[0].shape[0]
-    place = meta_ref[DEPTH] & (spans - 1)
+    place = lax.axis_index("dp") & (spans - 1)
     for m, ref in enumerate(out_refs):
         rows = pl.ds((place ^ m) * count, count)
         total = in_refs[0][rows].astype(jnp.float32)
@@ -166,25 +184,28 @@
         ref[...] = total.astype(ref.dtype)
 
 
-def cut(meta, before, parts, spans):
+def cut(before, parts, spans):
     shape = (parts[0].shape[0] // spans,) + parts[0].shape[1:]
     return pl.pallas_call(
         functools.partial(cut_kernel, spans),
-        in_specs=[smem()] + [vmem()] * (1 + len(parts)),
+        in_specs=[vmem()] * (1 + len(parts)),
         out_specs=[vmem()] * spans,
         out_shape=[jax.ShapeDtypeStruct(shape, jnp.float32)]
         + [jax.ShapeDtypeStruct(shape, jnp.bfloat16)] * (spans - 1),
         compiler_params=limit(before, *parts, *parts, *parts),
         name="cut",
-    )(meta, before, *parts)
+    )(before, *parts)
 
 
 def own_group(meta_ref, groups):
     return meta_ref[SECT] * (groups // 2) + meta_ref[DEPTH]
 
 
-def merge_kernel(groups, meta_ref, q_ref, o_ref, stat_ref, *refs):
-    part_refs, out_refs, held = refs[: -groups - 1], refs[-groups - 1 : -1], refs[-1]
+def merge_kernel(groups, meta_hbm, q_ref, o_ref, stat_ref, *refs):
+    part_refs, out_refs = refs[: -groups - 3], refs[-groups - 3 : -3]
+    held, meta_ref, sem = refs[-3:]
+    fetch = pltpu.make_async_copy(meta_hbm, meta_ref, sem)
+    fetch.start()
     count, steps, _ = q_ref.shape
     width = part_refs[0].shape[2] // 2
     rows = steps * GROUP
@@ -196,8 +217,6 @@
     row = lax.broadcasted_iota(jnp.int32, shape, 0)
     col = lax.broadcasted_iota(jnp.int32, shape, 1)
     causal = (row // rows == col // steps) & (col % steps <= row % steps)
-    step = lax.broadcasted_iota(jnp.int32, (rows, HEAD), 0) % steps
-    keep = jnp.concatenate([step < meta_ref[PROMPT + count + n] for n in range(count)], axis=0)
     for kv in range(width // HEAD):
         q = jnp.concatenate([stacked_heads(q_ref[n], kv) for n in range(count)], axis=0)
         stat = jnp.concatenate([stat_ref[n, kv, :, :2] for n in range(count)], axis=0)
@@ -209,75 +228,73 @@
         e = jnp.exp(s - top)
         back = jnp.exp(stat[:, :1] - top)
         share = 1.0 / (back * stat[:, 1:] + jnp.sum(e, axis=1, keepdims=True))
-        r = o * (back * share) + dot32(bf16(e * share), v)
-        r = bf16(jnp.where(keep, r, 0.0))
+        r = bf16(o * (back * share) + dot32(bf16(e * share), v))
         for n in range(count):
             for g in range(GROUP):
                 h = kv * GROUP + g
                 first = n * rows + g * steps
                 held[n, :, h * HEAD : (h + 1) * HEAD] = r[first : first + steps]
+    fetch.wait()
     own = own_group(meta_ref, groups)
     slots = PROMPT + 2 * count
+    step = lax.broadcasted_iota(jnp.int32, held.shape[1:], 0)
     for n in range(count):
+        live = step < meta_ref[PROMPT + count + n]
+        kept = jnp.where(live, held[n], jnp.zeros_like(held[n]))
         holder = lax.div(meta_ref[slots + own * count + n], count)
         for i in range(groups):
 
             @pl.when((holder ^ own) == i)
             def _():
-                out_refs[i][...] = held[n]
+                out_refs[i][...] = kept
 
 
 def merge(meta, queries, o_cache, stats, parts, groups):
     shape = queries.shape[1:]
     return pl.pallas_call(
         functools.partial(merge_kernel, groups),
-        in_specs=[smem()] + [vmem()] * (3 + len(parts)),
+        in_specs=[pl.BlockSpec(memory_space=pl.ANY)] + [vmem()] * (3 + len(parts)),
         out_specs=[vmem()] * groups,
         out_shape=[jax.ShapeDtypeStruct(shape, jnp.bfloat16)] * groups,
-        scratch_shapes=[pltpu.VMEM(queries.shape, jnp.bfloat16)],
+        scratch_shapes=[
+            pltpu.VMEM(queries.shape, jnp.bfloat16),
+            pltpu.SMEM(meta.shape, jnp.int32),
+            pltpu.SemaphoreType.DMA,
+        ],
         compiler_params=limit(queries, o_cache, stats, *parts, *[queries] * (groups // queries.shape[0] + 1)),
         name="merge_fresh",
     )(meta, queries, o_cache, stats, *parts)
 
 
-def pick_kernel(order, meta_ref, *refs):
-    in_refs, out_ref, places, sems = refs[:-3], refs[-3], refs[-2], refs[-1]
-    groups = len(in_refs)
-    count = out_ref.shape[0]
-    slots = PROMPT + 2 * count
-
-    def note(s, carry):
-        places[meta_ref[slots + s]] = s
-        return carry
-
-    lax.fori_loop(0, groups * count, note, 0, unroll=8)
-    own = own_group(meta_ref, groups)
+def pick_kernel(order, source_ref, *refs):
+    in_refs, out_ref, held, sems = refs[:-3], refs[-3], refs[-2], refs[-1]
+    count, _, width = held.shape
+    stores = [pltpu.make_async_copy(held.at[r], out_ref.at[r], sems.at[r]) for r in range(count)]
     for r in range(count):
-        source = lax.div(places[own * count + r], count)
-        for m, ref in zip(order, in_refs):
-
-            @pl.when((source ^ own) == m)
-            def _():
-                pltpu.make_async_copy(ref, out_ref.at[r], sems.at[r]).start()
-
-    for r in range(count):
-        pltpu.make_async_copy(in_refs[0], out_ref.at[r], sems.at[r]).wait()
-
-
-def pick(meta, blocks, order, count):
-    out = jax.ShapeDtypeStruct((count,) + blocks[0].shape, jnp.bfloat16)
+        source = source_ref[r]
+        masks = [source == m for m in order[1:]]
+        for first in range(0, width, HEAD):
+            cols = slice(first, first + HEAD)
+            row = in_refs[0][:, cols]
+            for mask, ref in zip(masks, in_refs[1:]):
+                row = jnp.where(mask, ref[:, cols], row)
+            held[r, :, cols] = row
+        stores[r].start()
+    for store in stores:
+        store.wait()
+
+
+def pick(sources, blocks, order):
+    out = jax.ShapeDtypeStruct(sources.shape[:1] + blocks[0].shape, jnp.bfloat16)
     return pl.pallas_call(
         functools.partial(pick_kernel, order),
-        in_specs=[smem()] + [vmem()] * len(blocks),
+        in_specs=[vmem()] * (1 + len(blocks)),
         out_specs=pl.BlockSpec(memory_space=pl.ANY),
         out_shape=out,
-        scratch_shapes=[
-            pltpu.SMEM((len(blocks) * count,), jnp.int32),
-            pltpu.SemaphoreType.DMA((count,)),
-        ],
-        compiler_params=limit(*blocks),
+        scratch_shapes=[pltpu.VMEM(out.shape, out.dtype), pltpu.SemaphoreType.DMA(sources.shape[:1])],
+        compiler_params=limit(sources, out, *blocks),
         name="pick_rows",
-    )(meta, *blocks)
+    )(sources, *blocks)
 
 
 def shards(
@@ -327,7 +344,7 @@
     def to_group(m):
         return lambda i, j, k: ((i * dp + j) ^ m) * 4 + k
 
-    scalars = jnp.stack([c, p, x, z]).astype(jnp.int32)
+    scalars = jnp.stack([x, z]).astype(jnp.int32)
     meta = jnp.concatenate([scalars, prompt_lengths, rollout_lengths, batch_slots])
 
     flat_hidden = hidden.reshape(tokens, feats)
@@ -337,16 +354,16 @@
     ]
     weights = (w_key, w_value)
     mates = [send(w, to_mate) for w in weights]
-    o_cache, stats = cache_attention(meta, queries, key_cache, value_cache)
-
-    parts = project(meta, jnp.concatenate(near, axis=0), weights, mates, dp, steps)
+    o_cache, stats, sources = cache_attention(meta, queries, key_cache, value_cache, groups)
+
+    parts = project(jnp.concatenate(near, axis=0), weights, mates, dp, steps)
     far, near = ([send(parts[first + m], in_plane(m)) for m in (3, 2, 1, 0)] for first in (0, 4))
-    near = cut(meta, stats, near + [send(add(far), to_depth(spans))], spans)
+    near = cut(stats, near + [send(add(far), to_depth(spans))], spans)
     parts = [a if m == 0 else send(a, to_depth(m)) for m, a in enumerate(near)]
     sends = merge(meta, queries, o_cache, stats, parts, groups)
-    order = sorted(range(1, groups), key=lambda m: -(m & (dp - 1)))
+    order = [dp] + sorted((m for m in range(1, groups) if m != dp), key=lambda m: -(m & (dp - 1)))
     blocks = [send(sends[m], to_group(m)) for m in order]
-    return pick(meta, blocks + [sends[0]], order + [0], count)
+    return pick(sources, blocks + [sends[0]], order + [0])
 
 
 def solution(mesh):

time: 64.4 us -> 63.6 us (0.988)
  Pallas kernels: 8.7 us -> 7.71 us
  local copies, waits for them, and re-layouts: 1.16 us -> 1.82 us
    pallas_call x5, Pallas kernels: 8.63 us -> 7.64 us  [the longest x1 3.38 us: cache_attention(): pl.pallas_call(functools.partial(cache_kernel, groups), grid_spec=pltpu.P...]
    unnamed x16, local copies, waits for them, and re-layouts: 0.04 us -> 0.71 us
  transfers between devices with their start and end apart: 23 -> 23, of which waited for: 11 -> 9; matrix products, arithmetic and copies ran while one was open for 2% -> 2% of each run, Pallas kernels for 5% -> 5%
where the time goes in v3:
time: 63.6 us; the launch traced here: 63.4 us
  starting transfers between devices  36.5 us (57%)
  waiting for transfers between devices  17.1 us (27%)
  Pallas kernels  7.71 us (12%)
  local copies, waits for them, and re-layouts  1.82 us (3%)
    ppermute x23, starting transfers between devices, send(): return lax.ppermute(a, everyone, [(flat(*d), target(*d)) for d in devices])  36.5 us
    ppermute x23, waiting for transfers between devices, send(): return lax.ppermute(a, everyone, [(flat(*d), target(*d)) for d in devices])  17.1 us
    pallas_call x1, Pallas kernels, cache_attention(): pl.pallas_call(functools.partial(cache_kernel, groups), grid_spec=pltpu.P...  3.38 us
    pallas_call x1, Pallas kernels, merge(): pl.pallas_call(functools.partial(merge_kernel, groups), in_specs=[pl.Bloc...  1.74 us
    pallas_call x1, Pallas kernels, project(): pl.pallas_call(functools.partial(project_kernel, dp), in_specs=[vmem()] *...  1.51 us
  transfers between devices with their start and end apart: 23, of which 9 were waited for; matrix products, arithmetic and copies ran while one was open for 2% of the time, Pallas kernels for 5%

profile of v3, /device:TPU:0, one launch (start us, length us, event | category | flops | bytes accessed | tf_op | source)
XLA Modules:
  0.0 63.4 jit_solution(7925610313448273591)
XLA Ops:
  0.5 1.0 %constant_dynamic-slice_fusion.3 = (bf16[64,512]{1,0:T(8,128)(2,1)S(1)}, bf16[64,512]{1,0:T(8,128)(2,1)S(1)}, bf16[64,512]{1,0:T(8,128)(2,1)S(1)}, bf16[64,512]{1,0:T(8,128)(2,1)S(1)}) fusion(bf16[64,2048]{1,0:T(8,128)(2,1)} %bitcast.3, s32[]{:T(128)S(6)} %select_n.12, s32[]{:T(128)S(6)} %select_n.15, s32[]{:T(128)S(6)} %select_n.14, s32[]{:T(128)S(6)} %select_n.13), kind=kLoop, calls=%fused_computation.4 | loop fusion | bytes 524304 | tf_op jit(solution)/shard_map/dynamic_slice | solution.py:352
  1.6 0.7 %collective-permute-start = (bf16[64,512]{1,0:T(8,128)(2,1)S(1)}, bf16[64,512]{1,0:T(8,128)(2,1)S(1)}, u32[]{:S(2)}, u32[]{:S(2)}) collective-permute-start(bf16[64,512]{1,0:T(8,128)(2,1)S(1)} %get-tuple-element.47), channel_id=1, source_target_pairs={{0,0},{1,8},{2,16},{3,24},{4,2},{5,10},{6,18},{7,26},{8,4},{9,12},... | collective-permute-start | bytes 196616 | tf_op jit(solution)/shard_map/ppermute | solution.py:326
  2.2 8.5 %collective-permute-start.3 = (bf16[64,512]{1,0:T(8,128)(2,1)S(1)}, bf16[64,512]{1,0:T(8,128)(2,1)S(1)}, u32[]{:S(2)}, u32[]{:S(2)}) collective-permute-start(bf16[64,512]{1,0:T(8,128)(2,1)S(1)} %get-tuple-element.48), channel_id=1, source_target_pairs={{0,6},{1,14},{2,22},{3,30},{4,4},{5,12},{6,20},{7,28},{8,2},{9,10}... | collective-permute-start | bytes 196616 | tf_op jit(solution)/shard_map/ppermute | solution.py:326
  10.8 2.8 %collective-permute-start.1 = (bf16[64,512]{1,0:T(8,128)(2,1)S(1)}, bf16[64,512]{1,0:T(8,128)(2,1)S(1)}, u32[]{:S(2)}, u32[]{:S(2)}) collective-permute-start(bf16[64,512]{1,0:T(8,128)(2,1)S(1)} %get-tuple-element.50), channel_id=1, source_target_pairs={{0,2},{1,10},{2,18},{3,26},{4,0},{5,8},{6,16},{7,24},{8,6},{9,14},... | collective-permute-start | bytes 196616 | tf_op jit(solution)/shard_map/ppermute | solution.py:326
  13.7 0.8 %collective-permute-done.3 = bf16[64,512]{1,0:T(8,128)(2,1)S(1)} collective-permute-done((bf16[64,512]{1,0:T(8,128)(2,1)S(1)}, bf16[64,512]{1,0:T(8,128)(2,1)S(1)}, u32[]{:S(2)}, u32[]{:S(2)}) %collective-permute-start.3) | collective-permute-done | bytes 65568 | tf_op jit(solution)/shard_map/ppermute | solution.py:326
  14.4 3.0 %collective-permute-done.2 = bf16[64,512]{1,0:T(8,128)(2,1)S(1)} collective-permute-done((bf16[64,512]{1,0:T(8,128)(2,1)S(1)}, bf16[64,512]{1,0:T(8,128)(2,1)S(1)}, u32[]{:S(2)}, u32[]{:S(2)}) %collective-permute-start.2) | collective-permute-done | bytes 65568 | tf_op jit(solution)/shard_map/ppermute | solution.py:326
  17.5 1.5 %project.1 = (bf16[8,16,512]{2,1,0:T(8,128)(2,1)S(1)}, bf16[8,16,512]{2,1,0:T(8,128)(2,1)S(1)}, bf16[8,16,512]{2,1,0:T(8,128)(2,1)S(1)}, bf16[8,16,512]{2,1,0:T(...) custom-call(bf16[256,512]{1,0:T(8,128)(2,1)S(1)} %pad_maximum_fusion, ...), custom_call_target="tpu_custom_call" | custom-call | tf_op jit(solution)/shard_map/project/pallas_call | solution.py:145
  19.0 3.4 %collective-permute-start.10 = (bf16[8,16,512]{2,1,0:T(8,128)(2,1)S(1)}, bf16[8,16,512]{2,1,0:T(8,128)(2,1)S(1)}, u32[]{:S(2)}, u32[]{:S(2)}) collective-permute-start(bf16[8,16,512]{2,1,0:T(8,128)(2,1)S(1)} %get-tuple-element.33), channel_id=1, source_target_pairs={{0,3},{1,19},{2,1},{3,17},{4,7},{5,23},{6,5},{7,21},{8,11},{9,27},... | collective-permute-start | bytes 393224 | tf_op jit(solution)/shard_map/ppermute | solution.py:326
  23.6 4.5 %collective-permute-start.6 = (bf16[8,16,512]{2,1,0:T(8,128)(2,1)}, bf16[8,16,512]{2,1,0:T(8,128)(2,1)S(1)}, u32[]{:S(2)}, u32[]{:S(2)}) collective-permute-start(bf16[8,16,512]{2,1,0:T(8,128)(2,1)} %get-tuple-element.29), channel_id=1, source_target_pairs={{0,3},{1,19},{2,1},{3,17},{4,7},{5,23},{6,5},{7,21},{8,11},{9,27},... | collective-permute-start | bytes 393224 | tf_op jit(solution)/shard_map/ppermute | solution.py:326
  28.7 0.8 %collective-permute-done.11.refs_1_ = bf16[8,16,512]{2,1,0:T(8,128)(2,1)S(1)} collective-permute-done((bf16[8,16,512]{2,1,0:T(8,128)(2,1)S(1)}, bf16[8,16,512]{2,1,0:T(8,128)(2,1)S(1)}, u32[]{:S(2)}, u32[]{:S(2)}) %collective-permute-start.11) | collective-permute-done | bytes 131104 | tf_op jit(solution)/shard_map/ppermute | solution.py:326
  29.5 0.8 %collective-permute-start.9 = (bf16[8,16,512]{2,1,0:T(8,128)(2,1)S(1)}, bf16[8,16,512]{2,1,0:T(8,128)(2,1)S(1)}, u32[]{:S(2)}, u32[]{:S(2)}) collective-permute-start(bf16[8,16,512]{2,1,0:T(8,128)(2,1)S(1)} %get-tuple-element.32), channel_id=1, source_target_pairs={{0,0},{1,16},{2,2},{3,18},{4,4},{5,20},{6,6},{7,22},{8,8},{9,24},{... | collective-permute-start | bytes 393224 | tf_op jit(solution)/shard_map/ppermute | solution.py:326
  30.4 2.0 %collective-permute-start.14 = (bf16[8,16,512]{2,1,0:T(8,128)(2,1)S(1)}, bf16[8,16,512]{2,1,0:T(8,128)(2,1)S(1)}, u32[]{:S(2)}, u32[]{:S(2)}) collective-permute-start(bf16[8,16,512]{2,1,0:T(8,128)(2,1)S(1)} %add.17), channel_id=1, source_target_pairs={{0,8},{1,9},{2,10},{3,11},{4,12},{5,13},{6,14},{7,15},{8,0},{9,1},... | collective-permute-start | bytes 393224 | tf_op jit(solution)/shard_map/ppermute | solution.py:326
  33.2 3.4 %cache_attention.1 = (f32[4,2,128,128]{3,2,1,0:T(8,128)S(1)}, f32[4,2,128,128]{3,2,1,0:T(8,128)S(1)}, bf16[4,16,128]{2,1,0:T(8,128)(2,1)S(1)}) custom-call(s32[42]{0:T(128)S(1)} %concatenate.6.meta_ref.meta_hbm, bf16[4,16,2048]{2,1,0:T(8,128)(2,1)S(1)} %copy-done.2, bf16[4,512,256]{2,1,0:T(8,128)(2,1)S(1)} %copy-done, bf16[4,512,256]{2,1,0:T(8,128)(2,1)S(1)} %copy-done.1), custom_call_target="tpu_custom_call" | custom-call | tf_op jit(solution)/shard_map/cache_attention/pallas_call | solution.py:90
  36.6 2.9 %collective-permute-done.14.refs_4_ = bf16[8,16,512]{2,1,0:T(8,128)(2,1)S(1)} collective-permute-done((bf16[8,16,512]{2,1,0:T(8,128)(2,1)S(1)}, bf16[8,16,512]{2,1,0:T(8,128)(2,1)S(1)}, u32[]{:S(2)}, u32[]{:S(2)}) %collective-permute-start.14) | collective-permute-done | bytes 131104 | tf_op jit(solution)/shard_map/ppermute | solution.py:326
  39.7 4.9 %collective-permute-done.15.refs_1_ = bf16[4,16,512]{2,1,0:T(8,128)(2,1)S(1)} collective-permute-done((bf16[4,16,512]{2,1,0:T(8,128)(2,1)S(1)}, bf16[4,16,512]{2,1,0:T(8,128)(2,1)S(1)}, u32[]{:S(2)}, u32[]{:S(2)}) %collective-permute-start.15) | collective-permute-done | bytes 65568 | tf_op jit(solution)/shard_map/ppermute | solution.py:326
  44.5 1.7 %merge_fresh.1 = (bf16[16,2048]{1,0:T(8,128)(2,1)S(1)}, bf16[16,2048]{1,0:T(8,128)(2,1)S(1)}, bf16[16,2048]{1,0:T(8,128)(2,1)S(1)}, bf16[16,2048]{1,0:T(8,128)(2...) custom-call(s32[42]{0:T(128)S(1)} %concatenate.6.meta_ref.meta_hbm, ...), custom_call_target="tpu_custom_call" | custom-call | tf_op jit(solution)/shard_map/merge_fresh/pallas_call | solution.py:254
  46.3 2.2 %collective-permute-start.16 = (bf16[16,2048]{1,0:T(8,128)(2,1)S(1)}, bf16[16,2048]{1,0:T(8,128)(2,1)S(1)}, u32[]{:S(2)}, u32[]{:S(2)}) collective-permute-start(bf16[16,2048]{1,0:T(8,128)(2,1)S(1)} %get-tuple-element.39), channel_id=1, source_target_pairs={{0,16},{1,17},{2,18},{3,19},{4,20},{5,21},{6,22},{7,23},{8,24},{9,... | collective-permute-start | bytes 196616 | tf_op jit(solution)/shard_map/ppermute | solution.py:326
  48.5 3.3 %collective-permute-start.18 = (bf16[16,2048]{1,0:T(8,128)(2,1)S(1)}, bf16[16,2048]{1,0:T(8,128)(2,1)S(1)}, u32[]{:S(2)}, u32[]{:S(2)}) collective-permute-start(bf16[16,2048]{1,0:T(8,128)(2,1)S(1)} %get-tuple-element.41), channel_id=1, source_target_pairs={{0,28},{1,29},{2,30},{3,31},{4,24},{5,25},{6,26},{7,27},{8,20},{9,... | collective-permute-start | bytes 196616 | tf_op jit(solution)/shard_map/ppermute | solution.py:326
  51.8 4.3 %collective-permute-start.20 = (bf16[16,2048]{1,0:T(8,128)(2,1)S(1)}, bf16[16,2048]{1,0:T(8,128)(2,1)S(1)}, u32[]{:S(2)}, u32[]{:S(2)}) collective-permute-start(bf16[16,2048]{1,0:T(8,128)(2,1)S(1)} %get-tuple-element.43), channel_id=1, source_target_pairs={{0,24},{1,25},{2,26},{3,27},{4,28},{5,29},{6,30},{7,31},{8,16},{9,... | collective-permute-start | bytes 196616 | tf_op jit(solution)/shard_map/ppermute | solution.py:326
  56.2 1.5 %collective-permute-start.22 = (bf16[16,2048]{1,0:T(8,128)(2,1)S(1)}, bf16[16,2048]{1,0:T(8,128)(2,1)S(1)}, u32[]{:S(2)}, u32[]{:S(2)}) collective-permute-start(bf16[16,2048]{1,0:T(8,128)(2,1)S(1)} %get-tuple-element.45), channel_id=1, source_target_pairs={{0,20},{1,21},{2,22},{3,23},{4,16},{5,17},{6,18},{7,19},{8,28},{9,... | collective-permute-start | bytes 196616 | tf_op jit(solution)/shard_map/ppermute | solution.py:326
  57.7 2.0 %collective-permute-done.19.refs_3_ = bf16[16,2048]{1,0:T(8,128)(2,1)S(1)} collective-permute-done((bf16[16,2048]{1,0:T(8,128)(2,1)S(1)}, bf16[16,2048]{1,0:T(8,128)(2,1)S(1)}, u32[]{:S(2)}, u32[]{:S(2)}) %collective-permute-start.19) | collective-permute-done | bytes 65568 | tf_op jit(solution)/shard_map/ppermute | solution.py:326
  59.7 1.5 %collective-permute-done.20.refs_4_ = bf16[16,2048]{1,0:T(8,128)(2,1)S(1)} collective-permute-done((bf16[16,2048]{1,0:T(8,128)(2,1)S(1)}, bf16[16,2048]{1,0:T(8,128)(2,1)S(1)}, u32[]{:S(2)}, u32[]{:S(2)}) %collective-permute-start.20) | collective-permute-done | bytes 65568 | tf_op jit(solution)/shard_map/ppermute | solution.py:326
  61.4 1.1 %collective-permute-done.22.refs_6_ = bf16[16,2048]{1,0:T(8,128)(2,1)S(1)} collective-permute-done((bf16[16,2048]{1,0:T(8,128)(2,1)S(1)}, bf16[16,2048]{1,0:T(8,128)(2,1)S(1)}, u32[]{:S(2)}, u32[]{:S(2)}) %collective-permute-start.22) | collective-permute-done | bytes 65568 | tf_op jit(solution)/shard_map/ppermute | solution.py:326
  62.5 0.9 %pick_rows.1 = bf16[4,16,2048]{2,1,0:T(8,128)(2,1)} custom-call(bf16[4,16,128]{2,1,0:T(8,128)(2,1)S(1)} %get-tuple-element.26.source_ref, bf16[16,2048]{1,0:T(8,128)(2,1)S(1)} %collective-permute-done.16.refs_0_, bf16[16,2048]{1,0:T(8,128)(2,1)S(1)} %collective-permute-done.17.refs_1_, bf16[16,2048]{1,0:T(8,128)(2,1)S(1)} %collective-permute-done.18.refs_2_, ...), custom_call_target="tpu_custom_call" | custom-call | tf_op jit(solution)/shard_map/pick_rows/pallas_call | solution.py:289
  (47 shorter events, 3.7 us)
Async XLA Ops:
  0.0 17.4 %collective-permute-start.4 = (bf16[256,1024]{1,0:T(8,128)(2,1)}, bf16[256,1024]{1,0:T(8,128)(2,1)S(1)}, u32[]{:S(2)}, u32[]{:S(2)}) collective-permute-start(bf16[256,1024]{1,0:T(8,128)(2,1)} %key_ref.1), channel_id=1, source_target_pairs={{0,1},{1,0},{2,3},{3,2},{4,5},{5,4},{6,7},{7,6},{8,9},{9,8},{10,11... | collective-permute-start | bytes 1572872 | tf_op jit(solution)/shard_map/ppermute | solution.py:326
  0.5 17.0 %collective-permute-start.5 = (bf16[256,1024]{1,0:T(8,128)(2,1)}, bf16[256,1024]{1,0:T(8,128)(2,1)S(1)}, u32[]{:S(2)}, u32[]{:S(2)}) collective-permute-start(bf16[256,1024]{1,0:T(8,128)(2,1)} %value_ref.1), channel_id=1, source_target_pairs={{0,1},{1,0},{2,3},{3,2},{4,5},{5,4},{6,7},{7,6},{8,9},{9,8},{10,11... | collective-permute-start | bytes 1572872 | tf_op jit(solution)/shard_map/ppermute | solution.py:326
  0.5 16.9 %copy-start.4 = (bf16[256,1024]{1,0:T(8,128)(2,1)S(1)}, bf16[256,1024]{1,0:T(8,128)(2,1)}, u32[]{:S(2)}) copy-start(bf16[256,1024]{1,0:T(8,128)(2,1)} %value_ref.1) | copy-start | bytes 1572868
  1.6 9.3 %collective-permute-start = (bf16[64,512]{1,0:T(8,128)(2,1)S(1)}, bf16[64,512]{1,0:T(8,128)(2,1)S(1)}, u32[]{:S(2)}, u32[]{:S(2)}) collective-permute-start(bf16[64,512]{1,0:T(8,128)(2,1)S(1)} %get-tuple-element.47), channel_id=1, source_target_pairs={{0,0},{1,8},{2,16},{3,24},{4,2},{5,10},{6,18},{7,26},{8,4},{9,12},... | collective-permute-start | bytes 196616 | tf_op jit(solution)/shard_map/ppermute | solution.py:326
  2.2 12.2 %collective-permute-start.3 = (bf16[64,512]{1,0:T(8,128)(2,1)S(1)}, bf16[64,512]{1,0:T(8,128)(2,1)S(1)}, u32[]{:S(2)}, u32[]{:S(2)}) collective-permute-start(bf16[64,512]{1,0:T(8,128)(2,1)S(1)} %get-tuple-element.48), channel_id=1, source_target_pairs={{0,6},{1,14},{2,22},{3,30},{4,4},{5,12},{6,20},{7,28},{8,2},{9,10}... | collective-permute-start | bytes 196616 | tf_op jit(solution)/shard_map/ppermute | solution.py:326
  10.7 6.6 %collective-permute-start.2 = (bf16[64,512]{1,0:T(8,128)(2,1)S(1)}, bf16[64,512]{1,0:T(8,128)(2,1)S(1)}, u32[]{:S(2)}, u32[]{:S(2)}) collective-permute-start(bf16[64,512]{1,0:T(8,128)(2,1)S(1)} %get-tuple-element.49), channel_id=1, source_target_pairs={{0,4},{1,12},{2,20},{3,28},{4,6},{5,14},{6,22},{7,30},{8,0},{9,8},... | collective-permute-start | bytes 196616 | tf_op jit(solution)/shard_map/ppermute | solution.py:326
  10.8 6.5 %collective-permute-start.1 = (bf16[64,512]{1,0:T(8,128)(2,1)S(1)}, bf16[64,512]{1,0:T(8,128)(2,1)S(1)}, u32[]{:S(2)}, u32[]{:S(2)}) collective-permute-start(bf16[64,512]{1,0:T(8,128)(2,1)S(1)} %get-tuple-element.50), channel_id=1, source_target_pairs={{0,2},{1,10},{2,18},{3,26},{4,0},{5,8},{6,16},{7,24},{8,6},{9,14},... | collective-permute-start | bytes 196616 | tf_op jit(solution)/shard_map/ppermute | solution.py:326
  19.0 9.1 %collective-permute-start.10 = (bf16[8,16,512]{2,1,0:T(8,128)(2,1)S(1)}, bf16[8,16,512]{2,1,0:T(8,128)(2,1)S(1)}, u32[]{:S(2)}, u32[]{:S(2)}) collective-permute-start(bf16[8,16,512]{2,1,0:T(8,128)(2,1)S(1)} %get-tuple-element.33), channel_id=1, source_target_pairs={{0,3},{1,19},{2,1},{3,17},{4,7},{5,23},{6,5},{7,21},{8,11},{9,27},... | collective-permute-start | bytes 393224 | tf_op jit(solution)/shard_map/ppermute | solution.py:326
  22.4 7.2 %collective-permute-start.11 = (bf16[8,16,512]{2,1,0:T(8,128)(2,1)S(1)}, bf16[8,16,512]{2,1,0:T(8,128)(2,1)S(1)}, u32[]{:S(2)}, u32[]{:S(2)}) collective-permute-start(bf16[8,16,512]{2,1,0:T(8,128)(2,1)S(1)} %get-tuple-element.34), channel_id=1, source_target_pairs={{0,2},{1,18},{2,0},{3,16},{4,6},{5,22},{6,4},{7,20},{8,10},{9,26},... | collective-permute-start | bytes 393224 | tf_op jit(solution)/shard_map/ppermute | solution.py:326
  23.0 6.6 %collective-permute-start.12 = (bf16[8,16,512]{2,1,0:T(8,128)(2,1)S(1)}, bf16[8,16,512]{2,1,0:T(8,128)(2,1)S(1)}, u32[]{:S(2)}, u32[]{:S(2)}) collective-permute-start(bf16[8,16,512]{2,1,0:T(8,128)(2,1)S(1)} %get-tuple-element.35), channel_id=1, source_target_pairs={{0,1},{1,17},{2,3},{3,19},{4,5},{5,21},{6,7},{7,23},{8,9},{9,25},{... | collective-permute-start | bytes 393224 | tf_op jit(solution)/shard_map/ppermute | solution.py:326
  23.0 7.4 %collective-permute-start.13 = (bf16[8,16,512]{2,1,0:T(8,128)(2,1)S(1)}, bf16[8,16,512]{2,1,0:T(8,128)(2,1)S(1)}, u32[]{:S(2)}, u32[]{:S(2)}) collective-permute-start(bf16[8,16,512]{2,1,0:T(8,128)(2,1)S(1)} %get-tuple-element.36), channel_id=1, source_target_pairs={{0,0},{1,16},{2,2},{3,18},{4,4},{5,20},{6,6},{7,22},{8,8},{9,24},{... | collective-permute-start | bytes 393224 | tf_op jit(solution)/shard_map/ppermute | solution.py:326
  23.6 13.0 %collective-permute-start.6 = (bf16[8,16,512]{2,1,0:T(8,128)(2,1)}, bf16[8,16,512]{2,1,0:T(8,128)(2,1)S(1)}, u32[]{:S(2)}, u32[]{:S(2)}) collective-permute-start(bf16[8,16,512]{2,1,0:T(8,128)(2,1)} %get-tuple-element.29), channel_id=1, source_target_pairs={{0,3},{1,19},{2,1},{3,17},{4,7},{5,23},{6,5},{7,21},{8,11},{9,27},... | collective-permute-start | bytes 393224 | tf_op jit(solution)/shard_map/ppermute | solution.py:326
  28.1 8.5 %collective-permute-start.7 = (bf16[8,16,512]{2,1,0:T(8,128)(2,1)S(1)}, bf16[8,16,512]{2,1,0:T(8,128)(2,1)S(1)}, u32[]{:S(2)}, u32[]{:S(2)}) collective-permute-start(bf16[8,16,512]{2,1,0:T(8,128)(2,1)S(1)} %get-tuple-element.30), channel_id=1, source_target_pairs={{0,2},{1,18},{2,0},{3,16},{4,6},{5,22},{6,4},{7,20},{8,10},{9,26},... | collective-permute-start | bytes 393224 | tf_op jit(solution)/shard_map/ppermute | solution.py:326
  29.5 7.1 %collective-permute-start.8 = (bf16[8,16,512]{2,1,0:T(8,128)(2,1)S(1)}, bf16[8,16,512]{2,1,0:T(8,128)(2,1)S(1)}, u32[]{:S(2)}, u32[]{:S(2)}) collective-permute-start(bf16[8,16,512]{2,1,0:T(8,128)(2,1)S(1)} %get-tuple-element.31), channel_id=1, source_target_pairs={{0,1},{1,17},{2,3},{3,19},{4,5},{5,21},{6,7},{7,23},{8,9},{9,25},{... | collective-permute-start | bytes 393224 | tf_op jit(solution)/shard_map/ppermute | solution.py:326
  29.5 7.1 %collective-permute-start.9 = (bf16[8,16,512]{2,1,0:T(8,128)(2,1)S(1)}, bf16[8,16,512]{2,1,0:T(8,128)(2,1)S(1)}, u32[]{:S(2)}, u32[]{:S(2)}) collective-permute-start(bf16[8,16,512]{2,1,0:T(8,128)(2,1)S(1)} %get-tuple-element.32), channel_id=1, source_target_pairs={{0,0},{1,16},{2,2},{3,18},{4,4},{5,20},{6,6},{7,22},{8,8},{9,24},{... | collective-permute-start | bytes 393224 | tf_op jit(solution)/shard_map/ppermute | solution.py:326
  30.4 9.1 %collective-permute-start.14 = (bf16[8,16,512]{2,1,0:T(8,128)(2,1)S(1)}, bf16[8,16,512]{2,1,0:T(8,128)(2,1)S(1)}, u32[]{:S(2)}, u32[]{:S(2)}) collective-permute-start(bf16[8,16,512]{2,1,0:T(8,128)(2,1)S(1)} %add.17), channel_id=1, source_target_pairs={{0,8},{1,9},{2,10},{3,11},{4,12},{5,13},{6,14},{7,15},{8,0},{9,1},... | collective-permute-start | bytes 393224 | tf_op jit(solution)/shard_map/ppermute | solution.py:326
  39.6 4.9 %collective-permute-start.15 = (bf16[4,16,512]{2,1,0:T(8,128)(2,1)S(1)}, bf16[4,16,512]{2,1,0:T(8,128)(2,1)S(1)}, u32[]{:S(2)}, u32[]{:S(2)}) collective-permute-start(bf16[4,16,512]{2,1,0:T(8,128)(2,1)S(1)} %get-tuple-element.38), channel_id=1, source_target_pairs={{0,4},{1,5},{2,6},{3,7},{4,0},{5,1},{6,2},{7,3},{8,12},{9,13},{10,... | collective-permute-start | bytes 196616 | tf_op jit(solution)/shard_map/ppermute | solution.py:326
  46.3 9.9 %collective-permute-start.16 = (bf16[16,2048]{1,0:T(8,128)(2,1)S(1)}, bf16[16,2048]{1,0:T(8,128)(2,1)S(1)}, u32[]{:S(2)}, u32[]{:S(2)}) collective-permute-start(bf16[16,2048]{1,0:T(8,128)(2,1)S(1)} %get-tuple-element.39), channel_id=1, source_target_pairs={{0,16},{1,17},{2,18},{3,19},{4,20},{5,21},{6,22},{7,23},{8,24},{9,... | collective-permute-start | bytes 196616 | tf_op jit(solution)/shard_map/ppermute | solution.py:326
  48.5 7.7 %collective-permute-start.17 = (bf16[16,2048]{1,0:T(8,128)(2,1)S(1)}, bf16[16,2048]{1,0:T(8,128)(2,1)S(1)}, u32[]{:S(2)}, u32[]{:S(2)}) collective-permute-start(bf16[16,2048]{1,0:T(8,128)(2,1)S(1)} %get-tuple-element.40), channel_id=1, source_target_pairs={{0,12},{1,13},{2,14},{3,15},{4,8},{5,9},{6,10},{7,11},{8,4},{9,5},... | collective-permute-start | bytes 196616 | tf_op jit(solution)/shard_map/ppermute | solution.py:326
  48.5 9.2 %collective-permute-start.18 = (bf16[16,2048]{1,0:T(8,128)(2,1)S(1)}, bf16[16,2048]{1,0:T(8,128)(2,1)S(1)}, u32[]{:S(2)}, u32[]{:S(2)}) collective-permute-start(bf16[16,2048]{1,0:T(8,128)(2,1)S(1)} %get-tuple-element.41), channel_id=1, source_target_pairs={{0,28},{1,29},{2,30},{3,31},{4,24},{5,25},{6,26},{7,27},{8,20},{9,... | collective-permute-start | bytes 196616 | tf_op jit(solution)/shard_map/ppermute | solution.py:326
  51.8 7.9 %collective-permute-start.19 = (bf16[16,2048]{1,0:T(8,128)(2,1)S(1)}, bf16[16,2048]{1,0:T(8,128)(2,1)S(1)}, u32[]{:S(2)}, u32[]{:S(2)}) collective-permute-start(bf16[16,2048]{1,0:T(8,128)(2,1)S(1)} %get-tuple-element.42), channel_id=1, source_target_pairs={{0,8},{1,9},{2,10},{3,11},{4,12},{5,13},{6,14},{7,15},{8,0},{9,1},... | collective-permute-start | bytes 196616 | tf_op jit(solution)/shard_map/ppermute | solution.py:326
  51.8 9.3 %collective-permute-start.20 = (bf16[16,2048]{1,0:T(8,128)(2,1)S(1)}, bf16[16,2048]{1,0:T(8,128)(2,1)S(1)}, u32[]{:S(2)}, u32[]{:S(2)}) collective-permute-start(bf16[16,2048]{1,0:T(8,128)(2,1)S(1)} %get-tuple-element.43), channel_id=1, source_target_pairs={{0,24},{1,25},{2,26},{3,27},{4,28},{5,29},{6,30},{7,31},{8,16},{9,... | collective-permute-start | bytes 196616 | tf_op jit(solution)/shard_map/ppermute | solution.py:326
  56.2 5.2 %collective-permute-start.21 = (bf16[16,2048]{1,0:T(8,128)(2,1)S(1)}, bf16[16,2048]{1,0:T(8,128)(2,1)S(1)}, u32[]{:S(2)}, u32[]{:S(2)}) collective-permute-start(bf16[16,2048]{1,0:T(8,128)(2,1)S(1)} %get-tuple-element.44), channel_id=1, source_target_pairs={{0,4},{1,5},{2,6},{3,7},{4,0},{5,1},{6,2},{7,3},{8,12},{9,13},{10,... | collective-permute-start | bytes 196616 | tf_op jit(solution)/shard_map/ppermute | solution.py:326
  56.2 6.3 %collective-permute-start.22 = (bf16[16,2048]{1,0:T(8,128)(2,1)S(1)}, bf16[16,2048]{1,0:T(8,128)(2,1)S(1)}, u32[]{:S(2)}, u32[]{:S(2)}) collective-permute-start(bf16[16,2048]{1,0:T(8,128)(2,1)S(1)} %get-tuple-element.45), channel_id=1, source_target_pairs={{0,20},{1,21},{2,22},{3,23},{4,16},{5,17},{6,18},{7,19},{8,28},{9,... | collective-permute-start | bytes 196616 | tf_op jit(solution)/shard_map/ppermute | solution.py:326
  (7 other events, 54.1 us)

commit v4 on v3

--- a/solution.py
+++ b/solution.py
@@ -348,10 +348,11 @@
     meta = jnp.concatenate([scalars, prompt_lengths, rollout_lengths, batch_slots])
 
     flat_hidden = hidden.reshape(tokens, feats)
-    near = [
-        send(lax.dynamic_slice_in_dim(flat_hidden, (z ^ m) * wide, wide, 1), to_features(m))
-        for m in range(dp)
-    ]
+    near = []
+    for m in range(dp):
+        piece = lax.dynamic_slice_in_dim(flat_hidden, (z ^ m) * wide, wide, 1)
+        flat_hidden, piece = lax.optimization_barrier((flat_hidden, piece))
+        near.append(send(piece, to_features(m)))
     weights = (w_key, w_value)
     mates = [send(w, to_mate) for w in weights]
     o_cache, stats, sources = cache_attention(meta, queries, key_cache, value_cache, groups)
@@ -361,7 +362,7 @@
     near = cut(stats, near + [send(add(far), to_depth(spans))], spans)
     parts = [a if m == 0 else send(a, to_depth(m)) for m, a in enumerate(near)]
     sends = merge(meta, queries, o_cache, stats, parts, groups)
-    order = [dp] + sorted((m for m in range(1, groups) if m != dp), key=lambda m: -(m & (dp - 1)))
+    order = sorted(range(1, groups), key=lambda m: -(m & (dp - 1)))
     blocks = [send(sends[m], to_group(m)) for m in order]
     return pick(sources, blocks + [sends[0]], order + [0])
 

time: 63.6 us -> 64.1 us (level)
  waiting for transfers between devices: 17.1 us -> 11 us
  starting transfers between devices: 36.5 us -> 42.3 us
  Pallas kernels: 7.71 us -> 9.08 us
    ppermute x23, waiting for transfers between devices: 17.1 us -> 11 us  [send(): return lax.ppermute(a, everyone, [(flat(*d), target(*d)) for d in devices])]
    ppermute x23, starting transfers between devices: 36.5 us -> 42.3 us  [send(): return lax.ppermute(a, everyone, [(flat(*d), target(*d)) for d in devices])]
    pallas_call x1, Pallas kernels: 1.51 us -> 2.88 us  [project(): pl.pallas_call(functools.partial(project_kernel, dp), in_specs=[vmem()] *...]
    dynamic_slice x1 -> x4, local copies, waits for them, and re-layouts: 1.04 us -> 0.04 us  [shards(): piece = lax.dynamic_slice_in_dim(flat_hidden, (z ^ m) * wide, wide, 1)]
  transfers between devices with their start and end apart: 23 -> 23, of which waited for: 9 -> 12; matrix products, arithmetic and copies ran while one was open for 2% -> 0% of each run, Pallas kernels for 5% -> 5%
where the time goes in v4:
time: 64.1 us; the launch traced here: 63.9 us
  starting transfers between devices  42.3 us (66%)
  waiting for transfers between devices  11 us (17%)
  Pallas kernels  9.08 us (14%)
  local copies, waits for them, and re-layouts  1.25 us (2%)
    ppermute x23, starting transfers between devices, send(): return lax.ppermute(a, everyone, [(flat(*d), target(*d)) for d in devices])  42.3 us
    ppermute x23, waiting for transfers between devices, send(): return lax.ppermute(a, everyone, [(flat(*d), target(*d)) for d in devices])  11 us
    pallas_call x1, Pallas kernels, cache_attention(): pl.pallas_call(functools.partial(cache_kernel, groups), grid_spec=pltpu.P...  3.38 us
    pallas_call x1, Pallas kernels, project(): pl.pallas_call(functools.partial(project_kernel, dp), in_specs=[vmem()] *...  2.88 us
    pallas_call x1, Pallas kernels, merge(): pl.pallas_call(functools.partial(merge_kernel, groups), in_specs=[pl.Bloc...  1.74 us
  transfers between devices with their start and end apart: 23, of which 12 were waited for; matrix products, arithmetic and copies ran while one was open for 0% of the time, Pallas kernels for 5%

profile of v4, /device:TPU:0, one launch (start us, length us, event | category | flops | bytes accessed | tf_op | source)
XLA Modules:
  0.0 63.9 jit_solution(16156650192907007399)
XLA Ops:
  1.0 6.0 %collective-permute-start.3 = (bf16[64,512]{1,0:T(8,128)(2,1)S(1)}, bf16[64,512]{1,0:T(8,128)(2,1)S(1)}, u32[]{:S(2)}, u32[]{:S(2)}) collective-permute-start(bf16[64,512]{1,0:T(8,128)(2,1)S(1)} %constant_dynamic-slice_fusion), channel_id=1, source_target_pairs={{0,6},{1,14},{2,22},{3,30},{4,4},{5,12},{6,20},{7,28},{8,2},{9,10}... | collective-permute-start | bytes 196616 | tf_op jit(solution)/shard_map/ppermute | solution.py:326
  7.1 1.5 %collective-permute-start.1 = (bf16[64,512]{1,0:T(8,128)(2,1)S(1)}, bf16[64,512]{1,0:T(8,128)(2,1)S(1)}, u32[]{:S(2)}, u32[]{:S(2)}) collective-permute-start(bf16[64,512]{1,0:T(8,128)(2,1)S(1)} %constant_dynamic-slice_fusion.2), channel_id=1, source_target_pairs={{0,2},{1,10},{2,18},{3,26},{4,0},{5,8},{6,16},{7,24},{8,6},{9,14},... | collective-permute-start | bytes 196616 | tf_op jit(solution)/shard_map/ppermute | solution.py:326
  8.7 2.4 %collective-permute-done.3 = bf16[64,512]{1,0:T(8,128)(2,1)S(1)} collective-permute-done((bf16[64,512]{1,0:T(8,128)(2,1)S(1)}, bf16[64,512]{1,0:T(8,128)(2,1)S(1)}, u32[]{:S(2)}, u32[]{:S(2)}) %collective-permute-start.3) | collective-permute-done | bytes 65568 | tf_op jit(solution)/shard_map/ppermute | solution.py:326
  11.1 0.7 %collective-permute-start = (bf16[64,512]{1,0:T(8,128)(2,1)S(1)}, bf16[64,512]{1,0:T(8,128)(2,1)S(1)}, u32[]{:S(2)}, u32[]{:S(2)}) collective-permute-start(bf16[64,512]{1,0:T(8,128)(2,1)S(1)} %constant_dynamic-slice_fusion.3), channel_id=1, source_target_pairs={{0,0},{1,8},{2,16},{3,24},{4,2},{5,10},{6,18},{7,26},{8,4},{9,12},... | collective-permute-start | bytes 196616 | tf_op jit(solution)/shard_map/ppermute | solution.py:326
  12.7 2.9 %project.1 = (bf16[8,16,512]{2,1,0:T(8,128)(2,1)S(1)}, bf16[8,16,512]{2,1,0:T(8,128)(2,1)S(1)}, bf16[8,16,512]{2,1,0:T(8,128)(2,1)S(1)}, bf16[8,16,512]{2,1,0:T(...) custom-call(bf16[256,512]{1,0:T(8,128)(2,1)S(1)} %pad_maximum_fusion, ...), custom_call_target="tpu_custom_call" | custom-call | tf_op jit(solution)/shard_map/project/pallas_call | solution.py:145
  15.6 8.1 %collective-permute-start.10 = (bf16[8,16,512]{2,1,0:T(8,128)(2,1)S(1)}, bf16[8,16,512]{2,1,0:T(8,128)(2,1)S(1)}, u32[]{:S(2)}, u32[]{:S(2)}) collective-permute-start(bf16[8,16,512]{2,1,0:T(8,128)(2,1)S(1)} %get-tuple-element.47), channel_id=1, source_target_pairs={{0,3},{1,19},{2,1},{3,17},{4,7},{5,23},{6,5},{7,21},{8,11},{9,27},... | collective-permute-start | bytes 393224 | tf_op jit(solution)/shard_map/ppermute | solution.py:326
  23.7 0.7 %collective-permute-start.13 = (bf16[8,16,512]{2,1,0:T(8,128)(2,1)S(1)}, bf16[8,16,512]{2,1,0:T(8,128)(2,1)S(1)}, u32[]{:S(2)}, u32[]{:S(2)}) collective-permute-start(bf16[8,16,512]{2,1,0:T(8,128)(2,1)S(1)} %get-tuple-element.50), channel_id=1, source_target_pairs={{0,0},{1,16},{2,2},{3,18},{4,4},{5,20},{6,6},{7,22},{8,8},{9,24},{... | collective-permute-start | bytes 393224 | tf_op jit(solution)/shard_map/ppermute | solution.py:326
  24.3 5.1 %collective-permute-start.6 = (bf16[8,16,512]{2,1,0:T(8,128)(2,1)}, bf16[8,16,512]{2,1,0:T(8,128)(2,1)S(1)}, u32[]{:S(2)}, u32[]{:S(2)}) collective-permute-start(bf16[8,16,512]{2,1,0:T(8,128)(2,1)} %get-tuple-element.43), channel_id=1, source_target_pairs={{0,3},{1,19},{2,1},{3,17},{4,7},{5,23},{6,5},{7,21},{8,11},{9,27},... | collective-permute-start | bytes 393224 | tf_op jit(solution)/shard_map/ppermute | solution.py:326
  30.5 0.8 %collective-permute-start.9 = (bf16[8,16,512]{2,1,0:T(8,128)(2,1)S(1)}, bf16[8,16,512]{2,1,0:T(8,128)(2,1)S(1)}, u32[]{:S(2)}, u32[]{:S(2)}) collective-permute-start(bf16[8,16,512]{2,1,0:T(8,128)(2,1)S(1)} %get-tuple-element.46), channel_id=1, source_target_pairs={{0,0},{1,16},{2,2},{3,18},{4,4},{5,20},{6,6},{7,22},{8,8},{9,24},{... | collective-permute-start | bytes 393224 | tf_op jit(solution)/shard_map/ppermute | solution.py:326
  31.4 1.2 %collective-permute-start.14 = (bf16[8,16,512]{2,1,0:T(8,128)(2,1)S(1)}, bf16[8,16,512]{2,1,0:T(8,128)(2,1)S(1)}, u32[]{:S(2)}, u32[]{:S(2)}) collective-permute-start(bf16[8,16,512]{2,1,0:T(8,128)(2,1)S(1)} %add.17), channel_id=1, source_target_pairs={{0,8},{1,9},{2,10},{3,11},{4,12},{5,13},{6,14},{7,15},{8,0},{9,1},... | collective-permute-start | bytes 393224 | tf_op jit(solution)/shard_map/ppermute | solution.py:326
  32.6 0.6 %copy-done.6 = s32[4]{0:T(128)S(1)} copy-done((s32[4]{0:T(128)S(1)}, s32[4]{0:T(128)}, u32[]{:S(2)}) %copy-start.6) | copy-done | bytes 40
  33.4 3.4 %cache_attention.1 = (f32[4,2,128,128]{3,2,1,0:T(8,128)S(1)}, f32[4,2,128,128]{3,2,1,0:T(8,128)S(1)}, bf16[4,16,128]{2,1,0:T(8,128)(2,1)S(1)}) custom-call(s32[42]{0:T(128)S(1)} %concatenate.6.meta_ref.meta_hbm, bf16[4,16,2048]{2,1,0:T(8,128)(2,1)S(1)} %copy-done.3, bf16[4,512,256]{2,1,0:T(8,128)(2,1)S(1)} %copy-done.1, bf16[4,512,256]{2,1,0:T(8,128)(2,1)S(1)} %copy-done.2), custom_call_target="tpu_custom_call" | custom-call | tf_op jit(solution)/shard_map/cache_attention/pallas_call | solution.py:90
  37.4 3.0 %collective-permute-start.15 = (bf16[4,16,512]{2,1,0:T(8,128)(2,1)S(1)}, bf16[4,16,512]{2,1,0:T(8,128)(2,1)S(1)}, u32[]{:S(2)}, u32[]{:S(2)}) collective-permute-start(bf16[4,16,512]{2,1,0:T(8,128)(2,1)S(1)} %get-tuple-element.52), channel_id=1, source_target_pairs={{0,4},{1,5},{2,6},{3,7},{4,0},{5,1},{6,2},{7,3},{8,12},{9,13},{10,... | collective-permute-start | bytes 196616 | tf_op jit(solution)/shard_map/ppermute | solution.py:326
  40.4 2.2 %collective-permute-done.15.refs_1_ = bf16[4,16,512]{2,1,0:T(8,128)(2,1)S(1)} collective-permute-done((bf16[4,16,512]{2,1,0:T(8,128)(2,1)S(1)}, bf16[4,16,512]{2,1,0:T(8,128)(2,1)S(1)}, u32[]{:S(2)}, u32[]{:S(2)}) %collective-permute-start.15) | collective-permute-done | bytes 65568 | tf_op jit(solution)/shard_map/ppermute | solution.py:326
  42.7 1.7 %merge_fresh.1 = (bf16[16,2048]{1,0:T(8,128)(2,1)S(1)}, bf16[16,2048]{1,0:T(8,128)(2,1)S(1)}, bf16[16,2048]{1,0:T(8,128)(2,1)S(1)}, bf16[16,2048]{1,0:T(8,128)(2...) custom-call(s32[42]{0:T(128)S(1)} %concatenate.6.meta_ref.meta_hbm, ...), custom_call_target="tpu_custom_call" | custom-call | tf_op jit(solution)/shard_map/merge_fresh/pallas_call | solution.py:254
  44.4 4.9 %collective-permute-start.16 = (bf16[16,2048]{1,0:T(8,128)(2,1)S(1)}, bf16[16,2048]{1,0:T(8,128)(2,1)S(1)}, u32[]{:S(2)}, u32[]{:S(2)}) collective-permute-start(bf16[16,2048]{1,0:T(8,128)(2,1)S(1)} %get-tuple-element.53), channel_id=1, source_target_pairs={{0,12},{1,13},{2,14},{3,15},{4,8},{5,9},{6,10},{7,11},{8,4},{9,5},... | collective-permute-start | bytes 196616 | tf_op jit(solution)/shard_map/ppermute | solution.py:326
  49.4 3.1 %collective-permute-start.17 = (bf16[16,2048]{1,0:T(8,128)(2,1)S(1)}, bf16[16,2048]{1,0:T(8,128)(2,1)S(1)}, u32[]{:S(2)}, u32[]{:S(2)}) collective-permute-start(bf16[16,2048]{1,0:T(8,128)(2,1)S(1)} %get-tuple-element.54), channel_id=1, source_target_pairs={{0,28},{1,29},{2,30},{3,31},{4,24},{5,25},{6,26},{7,27},{8,20},{9,... | collective-permute-start | bytes 196616 | tf_op jit(solution)/shard_map/ppermute | solution.py:326
  52.4 1.1 %collective-permute-start.19 = (bf16[16,2048]{1,0:T(8,128)(2,1)S(1)}, bf16[16,2048]{1,0:T(8,128)(2,1)S(1)}, u32[]{:S(2)}, u32[]{:S(2)}) collective-permute-start(bf16[16,2048]{1,0:T(8,128)(2,1)S(1)} %get-tuple-element.56), channel_id=1, source_target_pairs={{0,24},{1,25},{2,26},{3,27},{4,28},{5,29},{6,30},{7,31},{8,16},{9,... | collective-permute-start | bytes 196616 | tf_op jit(solution)/shard_map/ppermute | solution.py:326
  53.5 1.5 %collective-permute-start.20 = (bf16[16,2048]{1,0:T(8,128)(2,1)S(1)}, bf16[16,2048]{1,0:T(8,128)(2,1)S(1)}, u32[]{:S(2)}, u32[]{:S(2)}) collective-permute-start(bf16[16,2048]{1,0:T(8,128)(2,1)S(1)} %get-tuple-element.57), channel_id=1, source_target_pairs={{0,4},{1,5},{2,6},{3,7},{4,0},{5,1},{6,2},{7,3},{8,12},{9,13},{10,... | collective-permute-start | bytes 196616 | tf_op jit(solution)/shard_map/ppermute | solution.py:326
  55.0 3.3 %collective-permute-start.21 = (bf16[16,2048]{1,0:T(8,128)(2,1)S(1)}, bf16[16,2048]{1,0:T(8,128)(2,1)S(1)}, u32[]{:S(2)}, u32[]{:S(2)}) collective-permute-start(bf16[16,2048]{1,0:T(8,128)(2,1)S(1)} %get-tuple-element.58), channel_id=1, source_target_pairs={{0,20},{1,21},{2,22},{3,23},{4,16},{5,17},{6,18},{7,19},{8,28},{9,... | collective-permute-start | bytes 196616 | tf_op jit(solution)/shard_map/ppermute | solution.py:326
  59.2 2.5 %collective-permute-done.19.refs_3_ = bf16[16,2048]{1,0:T(8,128)(2,1)S(1)} collective-permute-done((bf16[16,2048]{1,0:T(8,128)(2,1)S(1)}, bf16[16,2048]{1,0:T(8,128)(2,1)S(1)}, u32[]{:S(2)}, u32[]{:S(2)}) %collective-permute-start.19) | collective-permute-done | bytes 65568 | tf_op jit(solution)/shard_map/ppermute | solution.py:326
  61.7 0.7 %collective-permute-done.21.refs_5_ = bf16[16,2048]{1,0:T(8,128)(2,1)S(1)} collective-permute-done((bf16[16,2048]{1,0:T(8,128)(2,1)S(1)}, bf16[16,2048]{1,0:T(8,128)(2,1)S(1)}, u32[]{:S(2)}, u32[]{:S(2)}) %collective-permute-start.21) | collective-permute-done | bytes 65568 | tf_op jit(solution)/shard_map/ppermute | solution.py:326
  62.3 0.7 %collective-permute-done.22.refs_6_ = bf16[16,2048]{1,0:T(8,128)(2,1)S(1)} collective-permute-done((bf16[16,2048]{1,0:T(8,128)(2,1)S(1)}, bf16[16,2048]{1,0:T(8,128)(2,1)S(1)}, u32[]{:S(2)}, u32[]{:S(2)}) %collective-permute-start.22) | collective-permute-done | bytes 65568 | tf_op jit(solution)/shard_map/ppermute | solution.py:326
  63.0 0.9 %pick_rows.1 = bf16[4,16,2048]{2,1,0:T(8,128)(2,1)} custom-call(bf16[4,16,128]{2,1,0:T(8,128)(2,1)S(1)} %get-tuple-element.33.source_ref, bf16[16,2048]{1,0:T(8,128)(2,1)S(1)} %collective-permute-done.16.refs_0_, bf16[16,2048]{1,0:T(8,128)(2,1)S(1)} %collective-permute-done.17.refs_1_, bf16[16,2048]{1,0:T(8,128)(2,1)S(1)} %collective-permute-done.18.refs_2_, ...), custom_call_target="tpu_custom_call" | custom-call | tf_op jit(solution)/shard_map/pick_rows/pallas_call | solution.py:289
  (52 shorter events, 4.8 us)
Async XLA Ops:
  0.0 12.7 %collective-permute-start.4 = (bf16[256,1024]{1,0:T(8,128)(2,1)}, bf16[256,1024]{1,0:T(8,128)(2,1)}, u32[]{:S(2)}, u32[]{:S(2)}) collective-permute-start(bf16[256,1024]{1,0:T(8,128)(2,1)} %key_ref.1), channel_id=1, source_target_pairs={{0,1},{1,0},{2,3},{3,2},{4,5},{5,4},{6,7},{7,6},{8,9},{9,8},{10,11... | collective-permute-start | bytes 1572872 | tf_op jit(solution)/shard_map/ppermute | solution.py:326
  0.5 12.2 %collective-permute-start.5 = (bf16[256,1024]{1,0:T(8,128)(2,1)}, bf16[256,1024]{1,0:T(8,128)(2,1)}, u32[]{:S(2)}, u32[]{:S(2)}) collective-permute-start(bf16[256,1024]{1,0:T(8,128)(2,1)} %value_ref.1), channel_id=1, source_target_pairs={{0,1},{1,0},{2,3},{3,2},{4,5},{5,4},{6,7},{7,6},{8,9},{9,8},{10,11... | collective-permute-start | bytes 1572872 | tf_op jit(solution)/shard_map/ppermute | solution.py:326
  1.0 10.0 %collective-permute-start.3 = (bf16[64,512]{1,0:T(8,128)(2,1)S(1)}, bf16[64,512]{1,0:T(8,128)(2,1)S(1)}, u32[]{:S(2)}, u32[]{:S(2)}) collective-permute-start(bf16[64,512]{1,0:T(8,128)(2,1)S(1)} %constant_dynamic-slice_fusion), channel_id=1, source_target_pairs={{0,6},{1,14},{2,22},{3,30},{4,4},{5,12},{6,20},{7,28},{8,2},{9,10}... | collective-permute-start | bytes 196616 | tf_op jit(solution)/shard_map/ppermute | solution.py:326
  7.1 5.3 %collective-permute-start.2 = (bf16[64,512]{1,0:T(8,128)(2,1)S(1)}, bf16[64,512]{1,0:T(8,128)(2,1)S(1)}, u32[]{:S(2)}, u32[]{:S(2)}) collective-permute-start(bf16[64,512]{1,0:T(8,128)(2,1)S(1)} %constant_dynamic-slice_fusion.1), channel_id=1, source_target_pairs={{0,4},{1,12},{2,20},{3,28},{4,6},{5,14},{6,22},{7,30},{8,0},{9,8},... | collective-permute-start | bytes 196616 | tf_op jit(solution)/shard_map/ppermute | solution.py:326
  7.1 5.5 %collective-permute-start.1 = (bf16[64,512]{1,0:T(8,128)(2,1)S(1)}, bf16[64,512]{1,0:T(8,128)(2,1)S(1)}, u32[]{:S(2)}, u32[]{:S(2)}) collective-permute-start(bf16[64,512]{1,0:T(8,128)(2,1)S(1)} %constant_dynamic-slice_fusion.2), channel_id=1, source_target_pairs={{0,2},{1,10},{2,18},{3,26},{4,0},{5,8},{6,16},{7,24},{8,6},{9,14},... | collective-permute-start | bytes 196616 | tf_op jit(solution)/shard_map/ppermute | solution.py:326
  11.1 1.5 %collective-permute-start = (bf16[64,512]{1,0:T(8,128)(2,1)S(1)}, bf16[64,512]{1,0:T(8,128)(2,1)S(1)}, u32[]{:S(2)}, u32[]{:S(2)}) collective-permute-start(bf16[64,512]{1,0:T(8,128)(2,1)S(1)} %constant_dynamic-slice_fusion.3), channel_id=1, source_target_pairs={{0,0},{1,8},{2,16},{3,24},{4,2},{5,10},{6,18},{7,26},{8,4},{9,12},... | collective-permute-start | bytes 196616 | tf_op jit(solution)/shard_map/ppermute | solution.py:326
  12.6 20.7 %copy-start.1 = (bf16[4,512,256]{2,1,0:T(8,128)(2,1)S(1)}, bf16[4,512,256]{2,1,0:T(8,128)(2,1)}, u32[]{:S(2)}) copy-start(bf16[4,512,256]{2,1,0:T(8,128)(2,1)} %k_ref.1) | copy-start | bytes 3145732
  15.6 13.8 %collective-permute-start.10 = (bf16[8,16,512]{2,1,0:T(8,128)(2,1)S(1)}, bf16[8,16,512]{2,1,0:T(8,128)(2,1)S(1)}, u32[]{:S(2)}, u32[]{:S(2)}) collective-permute-start(bf16[8,16,512]{2,1,0:T(8,128)(2,1)S(1)} %get-tuple-element.47), channel_id=1, source_target_pairs={{0,3},{1,19},{2,1},{3,17},{4,7},{5,23},{6,5},{7,21},{8,11},{9,27},... | collective-permute-start | bytes 393224 | tf_op jit(solution)/shard_map/ppermute | solution.py:326
  23.7 6.7 %collective-permute-start.11 = (bf16[8,16,512]{2,1,0:T(8,128)(2,1)S(1)}, bf16[8,16,512]{2,1,0:T(8,128)(2,1)S(1)}, u32[]{:S(2)}, u32[]{:S(2)}) collective-permute-start(bf16[8,16,512]{2,1,0:T(8,128)(2,1)S(1)} %get-tuple-element.48), channel_id=1, source_target_pairs={{0,2},{1,18},{2,0},{3,16},{4,6},{5,22},{6,4},{7,20},{8,10},{9,26},... | collective-permute-start | bytes 393224 | tf_op jit(solution)/shard_map/ppermute | solution.py:326
  23.7 6.8 %collective-permute-start.12 = (bf16[8,16,512]{2,1,0:T(8,128)(2,1)S(1)}, bf16[8,16,512]{2,1,0:T(8,128)(2,1)S(1)}, u32[]{:S(2)}, u32[]{:S(2)}) collective-permute-start(bf16[8,16,512]{2,1,0:T(8,128)(2,1)S(1)} %get-tuple-element.49), channel_id=1, source_target_pairs={{0,1},{1,17},{2,3},{3,19},{4,5},{5,21},{6,7},{7,23},{8,9},{9,25},{... | collective-permute-start | bytes 393224 | tf_op jit(solution)/shard_map/ppermute | solution.py:326
  23.7 7.6 %collective-permute-start.13 = (bf16[8,16,512]{2,1,0:T(8,128)(2,1)S(1)}, bf16[8,16,512]{2,1,0:T(8,128)(2,1)S(1)}, u32[]{:S(2)}, u32[]{:S(2)}) collective-permute-start(bf16[8,16,512]{2,1,0:T(8,128)(2,1)S(1)} %get-tuple-element.50), channel_id=1, source_target_pairs={{0,0},{1,16},{2,2},{3,18},{4,4},{5,20},{6,6},{7,22},{8,8},{9,24},{... | collective-permute-start | bytes 393224 | tf_op jit(solution)/shard_map/ppermute | solution.py:326
  24.3 12.4 %collective-permute-start.6 = (bf16[8,16,512]{2,1,0:T(8,128)(2,1)}, bf16[8,16,512]{2,1,0:T(8,128)(2,1)S(1)}, u32[]{:S(2)}, u32[]{:S(2)}) collective-permute-start(bf16[8,16,512]{2,1,0:T(8,128)(2,1)} %get-tuple-element.43), channel_id=1, source_target_pairs={{0,3},{1,19},{2,1},{3,17},{4,7},{5,23},{6,5},{7,21},{8,11},{9,27},... | collective-permute-start | bytes 393224 | tf_op jit(solution)/shard_map/ppermute | solution.py:326
  29.4 7.9 %collective-permute-start.7 = (bf16[8,16,512]{2,1,0:T(8,128)(2,1)}, bf16[8,16,512]{2,1,0:T(8,128)(2,1)S(1)}, u32[]{:S(2)}, u32[]{:S(2)}) collective-permute-start(bf16[8,16,512]{2,1,0:T(8,128)(2,1)} %get-tuple-element.44), channel_id=1, source_target_pairs={{0,2},{1,18},{2,0},{3,16},{4,6},{5,22},{6,4},{7,20},{8,10},{9,26},... | collective-permute-start | bytes 393224 | tf_op jit(solution)/shard_map/ppermute | solution.py:326
  30.4 6.9 %collective-permute-start.8 = (bf16[8,16,512]{2,1,0:T(8,128)(2,1)}, bf16[8,16,512]{2,1,0:T(8,128)(2,1)S(1)}, u32[]{:S(2)}, u32[]{:S(2)}) collective-permute-start(bf16[8,16,512]{2,1,0:T(8,128)(2,1)} %get-tuple-element.45), channel_id=1, source_target_pairs={{0,1},{1,17},{2,3},{3,19},{4,5},{5,21},{6,7},{7,23},{8,9},{9,25},{... | collective-permute-start | bytes 393224 | tf_op jit(solution)/shard_map/ppermute | solution.py:326
  30.5 6.8 %collective-permute-start.9 = (bf16[8,16,512]{2,1,0:T(8,128)(2,1)S(1)}, bf16[8,16,512]{2,1,0:T(8,128)(2,1)S(1)}, u32[]{:S(2)}, u32[]{:S(2)}) collective-permute-start(bf16[8,16,512]{2,1,0:T(8,128)(2,1)S(1)} %get-tuple-element.46), channel_id=1, source_target_pairs={{0,0},{1,16},{2,2},{3,18},{4,4},{5,20},{6,6},{7,22},{8,8},{9,24},{... | collective-permute-start | bytes 393224 | tf_op jit(solution)/shard_map/ppermute | solution.py:326
  31.4 5.9 %collective-permute-start.14 = (bf16[8,16,512]{2,1,0:T(8,128)(2,1)S(1)}, bf16[8,16,512]{2,1,0:T(8,128)(2,1)S(1)}, u32[]{:S(2)}, u32[]{:S(2)}) collective-permute-start(bf16[8,16,512]{2,1,0:T(8,128)(2,1)S(1)} %add.17), channel_id=1, source_target_pairs={{0,8},{1,9},{2,10},{3,11},{4,12},{5,13},{6,14},{7,15},{8,0},{9,1},... | collective-permute-start | bytes 393224 | tf_op jit(solution)/shard_map/ppermute | solution.py:326
  37.4 5.2 %collective-permute-start.15 = (bf16[4,16,512]{2,1,0:T(8,128)(2,1)S(1)}, bf16[4,16,512]{2,1,0:T(8,128)(2,1)S(1)}, u32[]{:S(2)}, u32[]{:S(2)}) collective-permute-start(bf16[4,16,512]{2,1,0:T(8,128)(2,1)S(1)} %get-tuple-element.52), channel_id=1, source_target_pairs={{0,4},{1,5},{2,6},{3,7},{4,0},{5,1},{6,2},{7,3},{8,12},{9,13},{10,... | collective-permute-start | bytes 196616 | tf_op jit(solution)/shard_map/ppermute | solution.py:326
  44.4 10.6 %collective-permute-start.16 = (bf16[16,2048]{1,0:T(8,128)(2,1)S(1)}, bf16[16,2048]{1,0:T(8,128)(2,1)S(1)}, u32[]{:S(2)}, u32[]{:S(2)}) collective-permute-start(bf16[16,2048]{1,0:T(8,128)(2,1)S(1)} %get-tuple-element.53), channel_id=1, source_target_pairs={{0,12},{1,13},{2,14},{3,15},{4,8},{5,9},{6,10},{7,11},{8,4},{9,5},... | collective-permute-start | bytes 196616 | tf_op jit(solution)/shard_map/ppermute | solution.py:326
  49.4 8.9 %collective-permute-start.17 = (bf16[16,2048]{1,0:T(8,128)(2,1)S(1)}, bf16[16,2048]{1,0:T(8,128)(2,1)S(1)}, u32[]{:S(2)}, u32[]{:S(2)}) collective-permute-start(bf16[16,2048]{1,0:T(8,128)(2,1)S(1)} %get-tuple-element.54), channel_id=1, source_target_pairs={{0,28},{1,29},{2,30},{3,31},{4,24},{5,25},{6,26},{7,27},{8,20},{9,... | collective-permute-start | bytes 196616 | tf_op jit(solution)/shard_map/ppermute | solution.py:326
  52.4 6.7 %collective-permute-start.18 = (bf16[16,2048]{1,0:T(8,128)(2,1)S(1)}, bf16[16,2048]{1,0:T(8,128)(2,1)S(1)}, u32[]{:S(2)}, u32[]{:S(2)}) collective-permute-start(bf16[16,2048]{1,0:T(8,128)(2,1)S(1)} %get-tuple-element.55), channel_id=1, source_target_pairs={{0,8},{1,9},{2,10},{3,11},{4,12},{5,13},{6,14},{7,15},{8,0},{9,1},... | collective-permute-start | bytes 196616 | tf_op jit(solution)/shard_map/ppermute | solution.py:326
  52.4 9.2 %collective-permute-start.19 = (bf16[16,2048]{1,0:T(8,128)(2,1)S(1)}, bf16[16,2048]{1,0:T(8,128)(2,1)S(1)}, u32[]{:S(2)}, u32[]{:S(2)}) collective-permute-start(bf16[16,2048]{1,0:T(8,128)(2,1)S(1)} %get-tuple-element.56), channel_id=1, source_target_pairs={{0,24},{1,25},{2,26},{3,27},{4,28},{5,29},{6,30},{7,31},{8,16},{9,... | collective-permute-start | bytes 196616 | tf_op jit(solution)/shard_map/ppermute | solution.py:326
  53.5 8.2 %collective-permute-start.20 = (bf16[16,2048]{1,0:T(8,128)(2,1)S(1)}, bf16[16,2048]{1,0:T(8,128)(2,1)S(1)}, u32[]{:S(2)}, u32[]{:S(2)}) collective-permute-start(bf16[16,2048]{1,0:T(8,128)(2,1)S(1)} %get-tuple-element.57), channel_id=1, source_target_pairs={{0,4},{1,5},{2,6},{3,7},{4,0},{5,1},{6,2},{7,3},{8,12},{9,13},{10,... | collective-permute-start | bytes 196616 | tf_op jit(solution)/shard_map/ppermute | solution.py:326
  55.0 7.4 %collective-permute-start.21 = (bf16[16,2048]{1,0:T(8,128)(2,1)S(1)}, bf16[16,2048]{1,0:T(8,128)(2,1)S(1)}, u32[]{:S(2)}, u32[]{:S(2)}) collective-permute-start(bf16[16,2048]{1,0:T(8,128)(2,1)S(1)} %get-tuple-element.58), channel_id=1, source_target_pairs={{0,20},{1,21},{2,22},{3,23},{4,16},{5,17},{6,18},{7,19},{8,28},{9,... | collective-permute-start | bytes 196616 | tf_op jit(solution)/shard_map/ppermute | solution.py:326
  58.3 4.7 %collective-permute-start.22 = (bf16[16,2048]{1,0:T(8,128)(2,1)S(1)}, bf16[16,2048]{1,0:T(8,128)(2,1)S(1)}, u32[]{:S(2)}, u32[]{:S(2)}) collective-permute-start(bf16[16,2048]{1,0:T(8,128)(2,1)S(1)} %get-tuple-element.59), channel_id=1, source_target_pairs={{0,16},{1,17},{2,18},{3,19},{4,20},{5,21},{6,22},{7,23},{8,24},{9,... | collective-permute-start | bytes 196616 | tf_op jit(solution)/shard_map/ppermute | solution.py:326
  (8 other events, 50.0 us)

commit v5 on v3

--- a/solution.py
+++ b/solution.py
@@ -361,7 +361,7 @@
     near = cut(stats, near + [send(add(far), to_depth(spans))], spans)
     parts = [a if m == 0 else send(a, to_depth(m)) for m, a in enumerate(near)]
     sends = merge(meta, queries, o_cache, stats, parts, groups)
-    order = [dp] + sorted((m for m in range(1, groups) if m != dp), key=lambda m: -(m & (dp - 1)))
+    order = sorted(range(1, groups), key=lambda m: (-(m & (dp - 1)), -m))
     blocks = [send(sends[m], to_group(m)) for m in order]
     return pick(sources, blocks + [sends[0]], order + [0])
 

time: 63.6 us -> 63.1 us (level)
  transfers between devices with their start and end apart: 23 -> 23, of which waited for: 9 -> 11; matrix products, arithmetic and copies ran while one was open for 2% -> 2% of each run, Pallas kernels for 5% -> 5%
where the time goes in v5:
time: 63.1 us; the launch traced here: 62.9 us
  starting transfers between devices  36.4 us (58%)
  waiting for transfers between devices  16.8 us (27%)
  Pallas kernels  7.71 us (12%)
  local copies, waits for them, and re-layouts  1.82 us (3%)
    ppermute x23, starting transfers between devices, send(): return lax.ppermute(a, everyone, [(flat(*d), target(*d)) for d in devices])  36.4 us
    ppermute x23, waiting for transfers between devices, send(): return lax.ppermute(a, everyone, [(flat(*d), target(*d)) for d in devices])  16.8 us
    pallas_call x1, Pallas kernels, cache_attention(): pl.pallas_call(functools.partial(cache_kernel, groups), grid_spec=pltpu.P...  3.38 us
    pallas_call x1, Pallas kernels, merge(): pl.pallas_call(functools.partial(merge_kernel, groups), in_specs=[pl.Bloc...  1.74 us
    pallas_call x1, Pallas kernels, project(): pl.pallas_call(functools.partial(project_kernel, dp), in_specs=[vmem()] *...  1.51 us
  transfers between devices with their start and end apart: 23, of which 11 were waited for; matrix products, arithmetic and copies ran while one was open for 2% of the time, Pallas kernels for 5%

profile of v5, /device:TPU:0, one launch (start us, length us, event | category | flops | bytes accessed | tf_op | source)
XLA Modules:
  0.0 62.9 jit_solution(4496093532984092583)
XLA Ops:
  0.5 1.0 %constant_dynamic-slice_fusion.3 = (bf16[64,512]{1,0:T(8,128)(2,1)S(1)}, bf16[64,512]{1,0:T(8,128)(2,1)S(1)}, bf16[64,512]{1,0:T(8,128)(2,1)S(1)}, bf16[64,512]{1,0:T(8,128)(2,1)S(1)}) fusion(bf16[64,2048]{1,0:T(8,128)(2,1)} %bitcast.3, s32[]{:T(128)S(6)} %select_n.12, s32[]{:T(128)S(6)} %select_n.15, s32[]{:T(128)S(6)} %select_n.14, s32[]{:T(128)S(6)} %select_n.13), kind=kLoop, calls=%fused_computation.4 | loop fusion | bytes 524304 | tf_op jit(solution)/shard_map/dynamic_slice | solution.py:352
  1.6 0.7 %collective-permute-start = (bf16[64,512]{1,0:T(8,128)(2,1)S(1)}, bf16[64,512]{1,0:T(8,128)(2,1)S(1)}, u32[]{:S(2)}, u32[]{:S(2)}) collective-permute-start(bf16[64,512]{1,0:T(8,128)(2,1)S(1)} %get-tuple-element.47), channel_id=1, source_target_pairs={{0,0},{1,8},{2,16},{3,24},{4,2},{5,10},{6,18},{7,26},{8,4},{9,12},... | collective-permute-start | bytes 196616 | tf_op jit(solution)/shard_map/ppermute | solution.py:326
  2.2 8.5 %collective-permute-start.3 = (bf16[64,512]{1,0:T(8,128)(2,1)S(1)}, bf16[64,512]{1,0:T(8,128)(2,1)S(1)}, u32[]{:S(2)}, u32[]{:S(2)}) collective-permute-start(bf16[64,512]{1,0:T(8,128)(2,1)S(1)} %get-tuple-element.48), channel_id=1, source_target_pairs={{0,6},{1,14},{2,22},{3,30},{4,4},{5,12},{6,20},{7,28},{8,2},{9,10}... | collective-permute-start | bytes 196616 | tf_op jit(solution)/shard_map/ppermute | solution.py:326
  10.8 2.8 %collective-permute-start.1 = (bf16[64,512]{1,0:T(8,128)(2,1)S(1)}, bf16[64,512]{1,0:T(8,128)(2,1)S(1)}, u32[]{:S(2)}, u32[]{:S(2)}) collective-permute-start(bf16[64,512]{1,0:T(8,128)(2,1)S(1)} %get-tuple-element.50), channel_id=1, source_target_pairs={{0,2},{1,10},{2,18},{3,26},{4,0},{5,8},{6,16},{7,24},{8,6},{9,14},... | collective-permute-start | bytes 196616 | tf_op jit(solution)/shard_map/ppermute | solution.py:326
  13.7 0.8 %collective-permute-done.3 = bf16[64,512]{1,0:T(8,128)(2,1)S(1)} collective-permute-done((bf16[64,512]{1,0:T(8,128)(2,1)S(1)}, bf16[64,512]{1,0:T(8,128)(2,1)S(1)}, u32[]{:S(2)}, u32[]{:S(2)}) %collective-permute-start.3) | collective-permute-done | bytes 65568 | tf_op jit(solution)/shard_map/ppermute | solution.py:326
  14.4 3.0 %collective-permute-done.2 = bf16[64,512]{1,0:T(8,128)(2,1)S(1)} collective-permute-done((bf16[64,512]{1,0:T(8,128)(2,1)S(1)}, bf16[64,512]{1,0:T(8,128)(2,1)S(1)}, u32[]{:S(2)}, u32[]{:S(2)}) %collective-permute-start.2) | collective-permute-done | bytes 65568 | tf_op jit(solution)/shard_map/ppermute | solution.py:326
  17.5 1.5 %project.1 = (bf16[8,16,512]{2,1,0:T(8,128)(2,1)S(1)}, bf16[8,16,512]{2,1,0:T(8,128)(2,1)S(1)}, bf16[8,16,512]{2,1,0:T(8,128)(2,1)S(1)}, bf16[8,16,512]{2,1,0:T(...) custom-call(bf16[256,512]{1,0:T(8,128)(2,1)S(1)} %pad_maximum_fusion, ...), custom_call_target="tpu_custom_call" | custom-call | tf_op jit(solution)/shard_map/project/pallas_call | solution.py:145
  19.0 3.4 %collective-permute-start.10 = (bf16[8,16,512]{2,1,0:T(8,128)(2,1)S(1)}, bf16[8,16,512]{2,1,0:T(8,128)(2,1)S(1)}, u32[]{:S(2)}, u32[]{:S(2)}) collective-permute-start(bf16[8,16,512]{2,1,0:T(8,128)(2,1)S(1)} %get-tuple-element.33), channel_id=1, source_target_pairs={{0,3},{1,19},{2,1},{3,17},{4,7},{5,23},{6,5},{7,21},{8,11},{9,27},... | collective-permute-start | bytes 393224 | tf_op jit(solution)/shard_map/ppermute | solution.py:326
  23.0 0.7 %collective-permute-start.13 = (bf16[8,16,512]{2,1,0:T(8,128)(2,1)S(1)}, bf16[8,16,512]{2,1,0:T(8,128)(2,1)S(1)}, u32[]{:S(2)}, u32[]{:S(2)}) collective-permute-start(bf16[8,16,512]{2,1,0:T(8,128)(2,1)S(1)} %get-tuple-element.36), channel_id=1, source_target_pairs={{0,0},{1,16},{2,2},{3,18},{4,4},{5,20},{6,6},{7,22},{8,8},{9,24},{... | collective-permute-start | bytes 393224 | tf_op jit(solution)/shard_map/ppermute | solution.py:326
  23.6 4.5 %collective-permute-start.6 = (bf16[8,16,512]{2,1,0:T(8,128)(2,1)}, bf16[8,16,512]{2,1,0:T(8,128)(2,1)S(1)}, u32[]{:S(2)}, u32[]{:S(2)}) collective-permute-start(bf16[8,16,512]{2,1,0:T(8,128)(2,1)} %get-tuple-element.29), channel_id=1, source_target_pairs={{0,3},{1,19},{2,1},{3,17},{4,7},{5,23},{6,5},{7,21},{8,11},{9,27},... | collective-permute-start | bytes 393224 | tf_op jit(solution)/shard_map/ppermute | solution.py:326
  28.7 0.8 %collective-permute-done.11.refs_1_ = bf16[8,16,512]{2,1,0:T(8,128)(2,1)S(1)} collective-permute-done((bf16[8,16,512]{2,1,0:T(8,128)(2,1)S(1)}, bf16[8,16,512]{2,1,0:T(8,128)(2,1)S(1)}, u32[]{:S(2)}, u32[]{:S(2)}) %collective-permute-start.11) | collective-permute-done | bytes 131104 | tf_op jit(solution)/shard_map/ppermute | solution.py:326
  29.5 0.8 %collective-permute-start.9 = (bf16[8,16,512]{2,1,0:T(8,128)(2,1)S(1)}, bf16[8,16,512]{2,1,0:T(8,128)(2,1)S(1)}, u32[]{:S(2)}, u32[]{:S(2)}) collective-permute-start(bf16[8,16,512]{2,1,0:T(8,128)(2,1)S(1)} %get-tuple-element.32), channel_id=1, source_target_pairs={{0,0},{1,16},{2,2},{3,18},{4,4},{5,20},{6,6},{7,22},{8,8},{9,24},{... | collective-permute-start | bytes 393224 | tf_op jit(solution)/shard_map/ppermute | solution.py:326
  30.4 2.0 %collective-permute-start.14 = (bf16[8,16,512]{2,1,0:T(8,128)(2,1)S(1)}, bf16[8,16,512]{2,1,0:T(8,128)(2,1)S(1)}, u32[]{:S(2)}, u32[]{:S(2)}) collective-permute-start(bf16[8,16,512]{2,1,0:T(8,128)(2,1)S(1)} %add.17), channel_id=1, source_target_pairs={{0,8},{1,9},{2,10},{3,11},{4,12},{5,13},{6,14},{7,15},{8,0},{9,1},... | collective-permute-start | bytes 393224 | tf_op jit(solution)/shard_map/ppermute | solution.py:326
  33.2 3.4 %cache_attention.1 = (f32[4,2,128,128]{3,2,1,0:T(8,128)S(1)}, f32[4,2,128,128]{3,2,1,0:T(8,128)S(1)}, bf16[4,16,128]{2,1,0:T(8,128)(2,1)S(1)}) custom-call(s32[42]{0:T(128)S(1)} %concatenate.6.meta_ref.meta_hbm, bf16[4,16,2048]{2,1,0:T(8,128)(2,1)S(1)} %copy-done.2, bf16[4,512,256]{2,1,0:T(8,128)(2,1)S(1)} %copy-done, bf16[4,512,256]{2,1,0:T(8,128)(2,1)S(1)} %copy-done.1), custom_call_target="tpu_custom_call" | custom-call | tf_op jit(solution)/shard_map/cache_attention/pallas_call | solution.py:90
  36.6 2.9 %collective-permute-done.14.refs_4_ = bf16[8,16,512]{2,1,0:T(8,128)(2,1)S(1)} collective-permute-done((bf16[8,16,512]{2,1,0:T(8,128)(2,1)S(1)}, bf16[8,16,512]{2,1,0:T(8,128)(2,1)S(1)}, u32[]{:S(2)}, u32[]{:S(2)}) %collective-permute-start.14) | collective-permute-done | bytes 131104 | tf_op jit(solution)/shard_map/ppermute | solution.py:326
  39.7 4.9 %collective-permute-done.15.refs_1_ = bf16[4,16,512]{2,1,0:T(8,128)(2,1)S(1)} collective-permute-done((bf16[4,16,512]{2,1,0:T(8,128)(2,1)S(1)}, bf16[4,16,512]{2,1,0:T(8,128)(2,1)S(1)}, u32[]{:S(2)}, u32[]{:S(2)}) %collective-permute-start.15) | collective-permute-done | bytes 65568 | tf_op jit(solution)/shard_map/ppermute | solution.py:326
  44.5 1.7 %merge_fresh.1 = (bf16[16,2048]{1,0:T(8,128)(2,1)S(1)}, bf16[16,2048]{1,0:T(8,128)(2,1)S(1)}, bf16[16,2048]{1,0:T(8,128)(2,1)S(1)}, bf16[16,2048]{1,0:T(8,128)(2...) custom-call(s32[42]{0:T(128)S(1)} %concatenate.6.meta_ref.meta_hbm, ...), custom_call_target="tpu_custom_call" | custom-call | tf_op jit(solution)/shard_map/merge_fresh/pallas_call | solution.py:254
  46.3 1.6 %collective-permute-start.16 = (bf16[16,2048]{1,0:T(8,128)(2,1)S(1)}, bf16[16,2048]{1,0:T(8,128)(2,1)S(1)}, u32[]{:S(2)}, u32[]{:S(2)}) collective-permute-start(bf16[16,2048]{1,0:T(8,128)(2,1)S(1)} %get-tuple-element.39), channel_id=1, source_target_pairs={{0,28},{1,29},{2,30},{3,31},{4,24},{5,25},{6,26},{7,27},{8,20},{9,... | collective-permute-start | bytes 196616 | tf_op jit(solution)/shard_map/ppermute | solution.py:326
  47.9 3.9 %collective-permute-start.17 = (bf16[16,2048]{1,0:T(8,128)(2,1)S(1)}, bf16[16,2048]{1,0:T(8,128)(2,1)S(1)}, u32[]{:S(2)}, u32[]{:S(2)}) collective-permute-start(bf16[16,2048]{1,0:T(8,128)(2,1)S(1)} %get-tuple-element.40), channel_id=1, source_target_pairs={{0,12},{1,13},{2,14},{3,15},{4,8},{5,9},{6,10},{7,11},{8,4},{9,5},... | collective-permute-start | bytes 196616 | tf_op jit(solution)/shard_map/ppermute | solution.py:326
  51.8 2.2 %collective-permute-start.19 = (bf16[16,2048]{1,0:T(8,128)(2,1)S(1)}, bf16[16,2048]{1,0:T(8,128)(2,1)S(1)}, u32[]{:S(2)}, u32[]{:S(2)}) collective-permute-start(bf16[16,2048]{1,0:T(8,128)(2,1)S(1)} %get-tuple-element.42), channel_id=1, source_target_pairs={{0,8},{1,9},{2,10},{3,11},{4,12},{5,13},{6,14},{7,15},{8,0},{9,1},... | collective-permute-start | bytes 196616 | tf_op jit(solution)/shard_map/ppermute | solution.py:326
  54.1 3.5 %collective-permute-start.21 = (bf16[16,2048]{1,0:T(8,128)(2,1)S(1)}, bf16[16,2048]{1,0:T(8,128)(2,1)S(1)}, u32[]{:S(2)}, u32[]{:S(2)}) collective-permute-start(bf16[16,2048]{1,0:T(8,128)(2,1)S(1)} %get-tuple-element.44), channel_id=1, source_target_pairs={{0,4},{1,5},{2,6},{3,7},{4,0},{5,1},{6,2},{7,3},{8,12},{9,13},{10,... | collective-permute-start | bytes 196616 | tf_op jit(solution)/shard_map/ppermute | solution.py:326
  57.6 2.1 %collective-permute-done.18.refs_2_ = bf16[16,2048]{1,0:T(8,128)(2,1)S(1)} collective-permute-done((bf16[16,2048]{1,0:T(8,128)(2,1)S(1)}, bf16[16,2048]{1,0:T(8,128)(2,1)S(1)}, u32[]{:S(2)}, u32[]{:S(2)}) %collective-permute-start.18) | collective-permute-done | bytes 65568 | tf_op jit(solution)/shard_map/ppermute | solution.py:326
  60.1 1.2 %collective-permute-done.20.refs_4_ = bf16[16,2048]{1,0:T(8,128)(2,1)S(1)} collective-permute-done((bf16[16,2048]{1,0:T(8,128)(2,1)S(1)}, bf16[16,2048]{1,0:T(8,128)(2,1)S(1)}, u32[]{:S(2)}, u32[]{:S(2)}) %collective-permute-start.20) | collective-permute-done | bytes 65568 | tf_op jit(solution)/shard_map/ppermute | solution.py:326
  62.0 0.9 %pick_rows.1 = bf16[4,16,2048]{2,1,0:T(8,128)(2,1)} custom-call(bf16[4,16,128]{2,1,0:T(8,128)(2,1)S(1)} %get-tuple-element.26.source_ref, bf16[16,2048]{1,0:T(8,128)(2,1)S(1)} %collective-permute-done.16.refs_0_, bf16[16,2048]{1,0:T(8,128)(2,1)S(1)} %collective-permute-done.17.refs_1_, bf16[16,2048]{1,0:T(8,128)(2,1)S(1)} %collective-permute-done.18.refs_2_, ...), custom_call_target="tpu_custom_call" | custom-call | tf_op jit(solution)/shard_map/pick_rows/pallas_call | solution.py:289
  (47 shorter events, 4.0 us)
Async XLA Ops:
  0.0 17.4 %collective-permute-start.4 = (bf16[256,1024]{1,0:T(8,128)(2,1)}, bf16[256,1024]{1,0:T(8,128)(2,1)S(1)}, u32[]{:S(2)}, u32[]{:S(2)}) collective-permute-start(bf16[256,1024]{1,0:T(8,128)(2,1)} %key_ref.1), channel_id=1, source_target_pairs={{0,1},{1,0},{2,3},{3,2},{4,5},{5,4},{6,7},{7,6},{8,9},{9,8},{10,11... | collective-permute-start | bytes 1572872 | tf_op jit(solution)/shard_map/ppermute | solution.py:326
  0.5 17.0 %collective-permute-start.5 = (bf16[256,1024]{1,0:T(8,128)(2,1)}, bf16[256,1024]{1,0:T(8,128)(2,1)S(1)}, u32[]{:S(2)}, u32[]{:S(2)}) collective-permute-start(bf16[256,1024]{1,0:T(8,128)(2,1)} %value_ref.1), channel_id=1, source_target_pairs={{0,1},{1,0},{2,3},{3,2},{4,5},{5,4},{6,7},{7,6},{8,9},{9,8},{10,11... | collective-permute-start | bytes 1572872 | tf_op jit(solution)/shard_map/ppermute | solution.py:326
  0.5 16.9 %copy-start.4 = (bf16[256,1024]{1,0:T(8,128)(2,1)S(1)}, bf16[256,1024]{1,0:T(8,128)(2,1)}, u32[]{:S(2)}) copy-start(bf16[256,1024]{1,0:T(8,128)(2,1)} %value_ref.1) | copy-start | bytes 1572868
  1.6 9.3 %collective-permute-start = (bf16[64,512]{1,0:T(8,128)(2,1)S(1)}, bf16[64,512]{1,0:T(8,128)(2,1)S(1)}, u32[]{:S(2)}, u32[]{:S(2)}) collective-permute-start(bf16[64,512]{1,0:T(8,128)(2,1)S(1)} %get-tuple-element.47), channel_id=1, source_target_pairs={{0,0},{1,8},{2,16},{3,24},{4,2},{5,10},{6,18},{7,26},{8,4},{9,12},... | collective-permute-start | bytes 196616 | tf_op jit(solution)/shard_map/ppermute | solution.py:326
  2.2 12.2 %collective-permute-start.3 = (bf16[64,512]{1,0:T(8,128)(2,1)S(1)}, bf16[64,512]{1,0:T(8,128)(2,1)S(1)}, u32[]{:S(2)}, u32[]{:S(2)}) collective-permute-start(bf16[64,512]{1,0:T(8,128)(2,1)S(1)} %get-tuple-element.48), channel_id=1, source_target_pairs={{0,6},{1,14},{2,22},{3,30},{4,4},{5,12},{6,20},{7,28},{8,2},{9,10}... | collective-permute-start | bytes 196616 | tf_op jit(solution)/shard_map/ppermute | solution.py:326
  10.7 6.6 %collective-permute-start.2 = (bf16[64,512]{1,0:T(8,128)(2,1)S(1)}, bf16[64,512]{1,0:T(8,128)(2,1)S(1)}, u32[]{:S(2)}, u32[]{:S(2)}) collective-permute-start(bf16[64,512]{1,0:T(8,128)(2,1)S(1)} %get-tuple-element.49), channel_id=1, source_target_pairs={{0,4},{1,12},{2,20},{3,28},{4,6},{5,14},{6,22},{7,30},{8,0},{9,8},... | collective-permute-start | bytes 196616 | tf_op jit(solution)/shard_map/ppermute | solution.py:326
  10.8 6.5 %collective-permute-start.1 = (bf16[64,512]{1,0:T(8,128)(2,1)S(1)}, bf16[64,512]{1,0:T(8,128)(2,1)S(1)}, u32[]{:S(2)}, u32[]{:S(2)}) collective-permute-start(bf16[64,512]{1,0:T(8,128)(2,1)S(1)} %get-tuple-element.50), channel_id=1, source_target_pairs={{0,2},{1,10},{2,18},{3,26},{4,0},{5,8},{6,16},{7,24},{8,6},{9,14},... | collective-permute-start | bytes 196616 | tf_op jit(solution)/shard_map/ppermute | solution.py:326
  19.0 9.1 %collective-permute-start.10 = (bf16[8,16,512]{2,1,0:T(8,128)(2,1)S(1)}, bf16[8,16,512]{2,1,0:T(8,128)(2,1)S(1)}, u32[]{:S(2)}, u32[]{:S(2)}) collective-permute-start(bf16[8,16,512]{2,1,0:T(8,128)(2,1)S(1)} %get-tuple-element.33), channel_id=1, source_target_pairs={{0,3},{1,19},{2,1},{3,17},{4,7},{5,23},{6,5},{7,21},{8,11},{9,27},... | collective-permute-start | bytes 393224 | tf_op jit(solution)/shard_map/ppermute | solution.py:326
  22.4 7.2 %collective-permute-start.11 = (bf16[8,16,512]{2,1,0:T(8,128)(2,1)S(1)}, bf16[8,16,512]{2,1,0:T(8,128)(2,1)S(1)}, u32[]{:S(2)}, u32[]{:S(2)}) collective-permute-start(bf16[8,16,512]{2,1,0:T(8,128)(2,1)S(1)} %get-tuple-element.34), channel_id=1, source_target_pairs={{0,2},{1,18},{2,0},{3,16},{4,6},{5,22},{6,4},{7,20},{8,10},{9,26},... | collective-permute-start | bytes 393224 | tf_op jit(solution)/shard_map/ppermute | solution.py:326
  23.0 6.6 %collective-permute-start.12 = (bf16[8,16,512]{2,1,0:T(8,128)(2,1)S(1)}, bf16[8,16,512]{2,1,0:T(8,128)(2,1)S(1)}, u32[]{:S(2)}, u32[]{:S(2)}) collective-permute-start(bf16[8,16,512]{2,1,0:T(8,128)(2,1)S(1)} %get-tuple-element.35), channel_id=1, source_target_pairs={{0,1},{1,17},{2,3},{3,19},{4,5},{5,21},{6,7},{7,23},{8,9},{9,25},{... | collective-permute-start | bytes 393224 | tf_op jit(solution)/shard_map/ppermute | solution.py:326
  23.0 7.4 %collective-permute-start.13 = (bf16[8,16,512]{2,1,0:T(8,128)(2,1)S(1)}, bf16[8,16,512]{2,1,0:T(8,128)(2,1)S(1)}, u32[]{:S(2)}, u32[]{:S(2)}) collective-permute-start(bf16[8,16,512]{2,1,0:T(8,128)(2,1)S(1)} %get-tuple-element.36), channel_id=1, source_target_pairs={{0,0},{1,16},{2,2},{3,18},{4,4},{5,20},{6,6},{7,22},{8,8},{9,24},{... | collective-permute-start | bytes 393224 | tf_op jit(solution)/shard_map/ppermute | solution.py:326
  23.6 13.0 %collective-permute-start.6 = (bf16[8,16,512]{2,1,0:T(8,128)(2,1)}, bf16[8,16,512]{2,1,0:T(8,128)(2,1)S(1)}, u32[]{:S(2)}, u32[]{:S(2)}) collective-permute-start(bf16[8,16,512]{2,1,0:T(8,128)(2,1)} %get-tuple-element.29), channel_id=1, source_target_pairs={{0,3},{1,19},{2,1},{3,17},{4,7},{5,23},{6,5},{7,21},{8,11},{9,27},... | collective-permute-start | bytes 393224 | tf_op jit(solution)/shard_map/ppermute | solution.py:326
  28.1 8.5 %collective-permute-start.7 = (bf16[8,16,512]{2,1,0:T(8,128)(2,1)S(1)}, bf16[8,16,512]{2,1,0:T(8,128)(2,1)S(1)}, u32[]{:S(2)}, u32[]{:S(2)}) collective-permute-start(bf16[8,16,512]{2,1,0:T(8,128)(2,1)S(1)} %get-tuple-element.30), channel_id=1, source_target_pairs={{0,2},{1,18},{2,0},{3,16},{4,6},{5,22},{6,4},{7,20},{8,10},{9,26},... | collective-permute-start | bytes 393224 | tf_op jit(solution)/shard_map/ppermute | solution.py:326
  29.5 7.1 %collective-permute-start.8 = (bf16[8,16,512]{2,1,0:T(8,128)(2,1)S(1)}, bf16[8,16,512]{2,1,0:T(8,128)(2,1)S(1)}, u32[]{:S(2)}, u32[]{:S(2)}) collective-permute-start(bf16[8,16,512]{2,1,0:T(8,128)(2,1)S(1)} %get-tuple-element.31), channel_id=1, source_target_pairs={{0,1},{1,17},{2,3},{3,19},{4,5},{5,21},{6,7},{7,23},{8,9},{9,25},{... | collective-permute-start | bytes 393224 | tf_op jit(solution)/shard_map/ppermute | solution.py:326
  29.5 7.1 %collective-permute-start.9 = (bf16[8,16,512]{2,1,0:T(8,128)(2,1)S(1)}, bf16[8,16,512]{2,1,0:T(8,128)(2,1)S(1)}, u32[]{:S(2)}, u32[]{:S(2)}) collective-permute-start(bf16[8,16,512]{2,1,0:T(8,128)(2,1)S(1)} %get-tuple-element.32), channel_id=1, source_target_pairs={{0,0},{1,16},{2,2},{3,18},{4,4},{5,20},{6,6},{7,22},{8,8},{9,24},{... | collective-permute-start | bytes 393224 | tf_op jit(solution)/shard_map/ppermute | solution.py:326
  30.4 9.1 %collective-permute-start.14 = (bf16[8,16,512]{2,1,0:T(8,128)(2,1)S(1)}, bf16[8,16,512]{2,1,0:T(8,128)(2,1)S(1)}, u32[]{:S(2)}, u32[]{:S(2)}) collective-permute-start(bf16[8,16,512]{2,1,0:T(8,128)(2,1)S(1)} %add.17), channel_id=1, source_target_pairs={{0,8},{1,9},{2,10},{3,11},{4,12},{5,13},{6,14},{7,15},{8,0},{9,1},... | collective-permute-start | bytes 393224 | tf_op jit(solution)/shard_map/ppermute | solution.py:326
  39.6 4.9 %collective-permute-start.15 = (bf16[4,16,512]{2,1,0:T(8,128)(2,1)S(1)}, bf16[4,16,512]{2,1,0:T(8,128)(2,1)S(1)}, u32[]{:S(2)}, u32[]{:S(2)}) collective-permute-start(bf16[4,16,512]{2,1,0:T(8,128)(2,1)S(1)} %get-tuple-element.38), channel_id=1, source_target_pairs={{0,4},{1,5},{2,6},{3,7},{4,0},{5,1},{6,2},{7,3},{8,12},{9,13},{10,... | collective-permute-start | bytes 196616 | tf_op jit(solution)/shard_map/ppermute | solution.py:326
  46.3 7.8 %collective-permute-start.16 = (bf16[16,2048]{1,0:T(8,128)(2,1)S(1)}, bf16[16,2048]{1,0:T(8,128)(2,1)S(1)}, u32[]{:S(2)}, u32[]{:S(2)}) collective-permute-start(bf16[16,2048]{1,0:T(8,128)(2,1)S(1)} %get-tuple-element.39), channel_id=1, source_target_pairs={{0,28},{1,29},{2,30},{3,31},{4,24},{5,25},{6,26},{7,27},{8,20},{9,... | collective-permute-start | bytes 196616 | tf_op jit(solution)/shard_map/ppermute | solution.py:326
  47.9 9.7 %collective-permute-start.17 = (bf16[16,2048]{1,0:T(8,128)(2,1)S(1)}, bf16[16,2048]{1,0:T(8,128)(2,1)S(1)}, u32[]{:S(2)}, u32[]{:S(2)}) collective-permute-start(bf16[16,2048]{1,0:T(8,128)(2,1)S(1)} %get-tuple-element.40), channel_id=1, source_target_pairs={{0,12},{1,13},{2,14},{3,15},{4,8},{5,9},{6,10},{7,11},{8,4},{9,5},... | collective-permute-start | bytes 196616 | tf_op jit(solution)/shard_map/ppermute | solution.py:326
  51.8 7.9 %collective-permute-start.18 = (bf16[16,2048]{1,0:T(8,128)(2,1)S(1)}, bf16[16,2048]{1,0:T(8,128)(2,1)S(1)}, u32[]{:S(2)}, u32[]{:S(2)}) collective-permute-start(bf16[16,2048]{1,0:T(8,128)(2,1)S(1)} %get-tuple-element.41), channel_id=1, source_target_pairs={{0,24},{1,25},{2,26},{3,27},{4,28},{5,29},{6,30},{7,31},{8,16},{9,... | collective-permute-start | bytes 196616 | tf_op jit(solution)/shard_map/ppermute | solution.py:326
  51.8 8.3 %collective-permute-start.19 = (bf16[16,2048]{1,0:T(8,128)(2,1)S(1)}, bf16[16,2048]{1,0:T(8,128)(2,1)S(1)}, u32[]{:S(2)}, u32[]{:S(2)}) collective-permute-start(bf16[16,2048]{1,0:T(8,128)(2,1)S(1)} %get-tuple-element.42), channel_id=1, source_target_pairs={{0,8},{1,9},{2,10},{3,11},{4,12},{5,13},{6,14},{7,15},{8,0},{9,1},... | collective-permute-start | bytes 196616 | tf_op jit(solution)/shard_map/ppermute | solution.py:326
  54.0 7.3 %collective-permute-start.20 = (bf16[16,2048]{1,0:T(8,128)(2,1)S(1)}, bf16[16,2048]{1,0:T(8,128)(2,1)S(1)}, u32[]{:S(2)}, u32[]{:S(2)}) collective-permute-start(bf16[16,2048]{1,0:T(8,128)(2,1)S(1)} %get-tuple-element.43), channel_id=1, source_target_pairs={{0,20},{1,21},{2,22},{3,23},{4,16},{5,17},{6,18},{7,19},{8,28},{9,... | collective-permute-start | bytes 196616 | tf_op jit(solution)/shard_map/ppermute | solution.py:326
  54.1 7.3 %collective-permute-start.21 = (bf16[16,2048]{1,0:T(8,128)(2,1)S(1)}, bf16[16,2048]{1,0:T(8,128)(2,1)S(1)}, u32[]{:S(2)}, u32[]{:S(2)}) collective-permute-start(bf16[16,2048]{1,0:T(8,128)(2,1)S(1)} %get-tuple-element.44), channel_id=1, source_target_pairs={{0,4},{1,5},{2,6},{3,7},{4,0},{5,1},{6,2},{7,3},{8,12},{9,13},{10,... | collective-permute-start | bytes 196616 | tf_op jit(solution)/shard_map/ppermute | solution.py:326
  57.6 4.3 %collective-permute-start.22 = (bf16[16,2048]{1,0:T(8,128)(2,1)S(1)}, bf16[16,2048]{1,0:T(8,128)(2,1)S(1)}, u32[]{:S(2)}, u32[]{:S(2)}) collective-permute-start(bf16[16,2048]{1,0:T(8,128)(2,1)S(1)} %get-tuple-element.45), channel_id=1, source_target_pairs={{0,16},{1,17},{2,18},{3,19},{4,20},{5,21},{6,22},{7,23},{8,24},{9,... | collective-permute-start | bytes 196616 | tf_op jit(solution)/shard_map/ppermute | solution.py:326
  (7 other events, 54.1 us)
